TPU v7x, 256 devices: a whole 4x4x8 slice. The times are simulated.
256 devices in a mesh: dp: 32 (over y, x, core), expert: 8 (over z).
Axes of the slice: x: 4, y: 4, z: 8, core: 2. Of those that a mesh axis runs over, the one named last changes fastest.
Arguments:
- tokens: bfloat16 [32768, 1024], P(('dp', 'expert')), may hold values from -24 to 24
- out_grad: bfloat16 [32768, 1024], P(('dp', 'expert')), may hold values from -6 to 6
- expert_ids: int32 [32768, 8], P(('dp', 'expert')), may hold values from 0 to 63, all different within a row; in each aligned block of 128 rows (0 to 127, 128 to 255, ...) at most 20 rows name the same one
- gate_values: bfloat16 [32768, 8], P(('dp', 'expert')), may hold values from 0.049804688 to 1
- gate_weight: bfloat16 [1024, 64, 384], P('dp', 'expert'), may hold values from -0.1875 to 0.1875
- down_weight: bfloat16 [1024, 64, 384], P('dp', 'expert'), may hold values from -0.3125 to 0.3125
Outputs:
- input_grad: bfloat16 [32768, 1024], P(('dp', 'expert'))
- gate_grad: float32 [1024, 64, 384], P('dp', 'expert')
- down_grad: float32 [1024, 64, 384], P('dp', 'expert')
Inputs may be any that keep to these rules, and one draw needn't show every extreme that they name: `expert_ids`: each row names 8 different experts. Within the rows of one device (aligned blocks of 128 rows) no expert is named more than 20 times, a bound that some block reaches.
All inputs are finite; a program needn't handle non-finite values.
Results may differ from a plain program's by a relative error of at most 0.018.
Values may be sent and summed in bfloat16 or wider, within the bound.
No kernel may reach another device: no remote copies, remote signals or barrier semaphores. Data moves between devices by JAX's collectives and lax.ppermute only.
A program may use at most 128 MiB of HBM per device.

v0:
```python
import math

import jax
import jax.numpy as jnp
from jax import lax
from jax.experimental import pallas as pl
from jax.experimental.pallas import tpu as pltpu
from jax.sharding import Mesh
from jax.sharding import PartitionSpec as P

BF, F32 = jnp.bfloat16, jnp.float32
NY, NX, NC, NZ = 4, 4, 2, 8
ROWS, WIDTH, HID = 128, 1024, 384
EXPERTS_CORE = 4
META = 16
CAP = 20
QROWS = 4 * ROWS
QSLOTS = 4 * CAP
QUADS = NC * NZ * ROWS // QROWS
SLOTS = QUADS * QSLOTS
PIECE = WIDTH // (NY * NX)
SIZES = {"y": NY, "x": NX}
ANYWHERE = pl.BlockSpec(memory_space=pl.ANY)
PARAMS = pltpu.CompilerParams(vmem_limit_bytes=60 * 2**20)


def swap(value):
    return lax.ppermute(value, "c", [(0, 1), (1, 0)])


def step(value, axis, by=1):
    n = SIZES[axis]
    pairs = [(2 * i + c, 2 * ((i + by * (1 - 2 * c)) % n) + c) for i in range(n) for c in range(NC)]
    return lax.ppermute(value, (axis, "c"), pairs)


def shift(value, axis, by):
    n = SIZES[axis]
    return lax.ppermute(value, axis, [(i, (i + by) % n) for i in range(n)])


def dot(a, b, contract):
    return lax.dot_general(a, b, ((contract[:1], contract[1:]), ((), ())), preferred_element_type=F32)


def cost(flops, moved, other=0):
    return pl.CostEstimate(flops=flops, bytes_accessed=moved, transcendentals=other)


def row_of(pos, ky, kx):
    y, x = (pos[0] + ky) & (NY - 1), (pos[1] + kx) & (NX - 1)
    return pl.multiple_of((y * NX + x) * PIECE, PIECE)


def pick_rows(srow):
    iota = lax.broadcasted_iota(jnp.int32, (QSLOTS, QROWS), 0).astype(F32)
    picks = [(srow[e : e + 1, :] == iota).astype(F32).astype(BF) for e in range(EXPERTS_CORE)]
    return jnp.concatenate(picks, axis=0)


def layer_kernel(scale, pos, rows, *refs):
    a_in, b_in = refs[0:4], refs[4:8]
    sums, a_out, b_out = refs[8:10], refs[10:15], refs[15:20]
    wg, wd, term, xg, gg, weighting, slot_grad, srow, before = refs[20:]
    step_id = pl.program_id(0)

    @pl.when(step_id == 0)
    def _():
        token = lambda dim: lax.broadcasted_iota(jnp.int32, (QROWS, QROWS), dim)
        before[...] = (token(0) < token(1)).astype(F32).astype(BF)

    @pl.when(step_id < QUADS)
    def _():
        expert = (pos[3] + lax.broadcasted_iota(jnp.int32, (8, 1), 0)).astype(F32)
        meta = [rows[i * ROWS : i * ROWS + META, 2 * WIDTH :].astype(F32) for i in range(QROWS // ROWS)]
        meta = jnp.concatenate(meta, axis=1)
        member = jnp.zeros((8, QROWS), F32)
        gates = jnp.zeros((8, QROWS), F32)
        for k in range(8):
            hit = meta[k : k + 1, :] == expert
            member = jnp.where(hit, 1.0, member)
            gates = jnp.where(hit, meta[8 + k : 9 + k, :], gates)
        slot = jnp.where(member > 0.0, dot(member.astype(BF), before[...], (1, 0)), -1.0)
        srow[step_id] = slot
        picks = pick_rows(slot)
        at = pl.ds(pl.multiple_of(step_id * QSLOTS, QSLOTS), QSLOTS)
        for half, to in enumerate((xg, gg)):
            to[:, at, :] = (
                dot(picks, rows[:, half * WIDTH : (half + 1) * WIDTH], (1, 0))
                .astype(BF)
                .reshape(EXPERTS_CORE, QSLOTS, WIDTH)
            )
        slot_gates = dot(picks, gates.astype(BF), (1, 1))
        for e in range(EXPERTS_CORE):
            weighting[e, at, :] = jnp.broadcast_to(
                slot_gates[e * QSLOTS : (e + 1) * QSLOTS, e : e + 1], (QSLOTS, 128)
            )

    @pl.when(step_id >= QUADS)
    def _():
        expert_step(scale, pos, step_id - QUADS, a_in, b_in, a_out, b_out, wg, wd, term, xg, gg, weighting, slot_grad)

    @pl.when(step_id == QUADS + EXPERTS_CORE - 1)
    def _():
        half = QUADS // 2
        for other, out in enumerate(sums):
            for i in range(half):
                q = (pos[2] ^ other) * half + i
                total = dot(pick_rows(srow[q]), slot_grad[q], (0, 0))
                out[i * QROWS : (i + 1) * QROWS, :] = total.astype(BF)


def expert_step(scale, pos, e, a_in, b_in, a_out, b_out, wg, wd, term, xg, gg, weighting, slot_grad):
    way = pos[4]
    for ky in range(NY):
        for kx in range(NX):
            at = pl.ds(row_of(pos, -way * ky, -way * kx), PIECE)
            wg[at, :] = a_in[ky][kx, 0]
            wd[at, :] = b_in[kx][ky, 0]
    gate = weighting[e][:, :1]
    pre = dot(xg[e], wg[...], (1, 0))
    hidden = dot(gg[e], wd[...], (1, 0))
    sigmoid = jax.nn.sigmoid(pre)
    scaled = (gate * (pre * sigmoid)).astype(BF)
    grad = (gate * hidden * (sigmoid * (1.0 + pre * (1.0 - sigmoid)))).astype(BF)
    back = dot(grad, wg[...], (1, 1)).astype(BF)
    for q in range(QUADS):
        slot_grad[q, pl.ds(pl.multiple_of(e * QSLOTS, QSLOTS), QSLOTS), :] = back[q * QSLOTS : (q + 1) * QSLOTS]
    for rows, value, out, y_first in ((xg, grad, a_out, True), (gg, scaled, b_out, False)):
        term[...] = (dot(rows[e], value, (0, 0)) * scale).astype(BF)
        for k in range(4):
            for j in range(4):
                piece = term[pl.ds(row_of(pos, *((k, j) if y_first else (j, k))), PIECE), :]
                if k == 2:
                    out[2 + j // 2][j % 2, 0] = piece
                else:
                    out[4 if k == 3 else k][j, 0] = piece


def layer(scale, pos, rows, a_in, b_in):
    expert = lambda i: jnp.maximum(i - QUADS, 0)
    piece = lambda n: pl.BlockSpec((n, 1, PIECE, HID), lambda i, p: (0, expert(i), 0, 0))
    grads = lambda n: jax.ShapeDtypeStruct((n, EXPERTS_CORE, PIECE, HID), BF)
    half = (QUADS * QROWS // 2, WIDTH)
    sizes = (4, 4, 2, 2, 4) * 2
    slots = lambda n, dtype: pltpu.VMEM((EXPERTS_CORE, SLOTS, n), dtype)
    out = pl.pallas_call(
        lambda *refs: layer_kernel(scale, *refs),
        grid_spec=pltpu.PrefetchScalarGridSpec(
            num_scalar_prefetch=1,
            grid=(QUADS + EXPERTS_CORE,),
            in_specs=[pl.BlockSpec((QROWS, rows.shape[1]), lambda i, p: (jnp.minimum(i, QUADS - 1), 0))]
            + [piece(4)] * 8,
            out_specs=[pl.BlockSpec(half, lambda i, p: (0, 0))] * 2 + [piece(n) for n in sizes],
            scratch_shapes=[pltpu.VMEM((WIDTH, HID), BF)] * 3
            + [slots(WIDTH, BF), slots(WIDTH, BF), slots(128, F32)]
            + [pltpu.VMEM((QUADS, EXPERTS_CORE * QSLOTS, WIDTH), BF), pltpu.VMEM((QUADS, 8, QROWS), F32)]
            + [pltpu.VMEM((QROWS, QROWS), BF)],
        ),
        out_shape=[jax.ShapeDtypeStruct(half, BF)] * 2 + [grads(n) for n in sizes],
        compiler_params=PARAMS,
        cost_estimate=cost(13_000_000_000, 26_000_000, 600_000),
    )(pos, rows, *a_in, *b_in)
    return out[0], out[1], out[2:7], out[7:12]


def add_kernel(own, got, *refs):
    refs[-1][...] = (own[...].astype(F32) + got[...].astype(F32)).astype(BF)


def add(own, got, after):
    rows = pl.BlockSpec((QROWS // 2, WIDTH), lambda i: (i, 0))
    return pl.pallas_call(
        add_kernel,
        grid=(own.shape[0] * 2 // QROWS,),
        in_specs=[rows, rows] + [ANYWHERE] * len(after),
        out_specs=rows,
        out_shape=jax.ShapeDtypeStruct(own.shape, BF),
        compiler_params=PARAMS,
        cost_estimate=cost(1_000_000, 6_000_000),
    )(own, got, *after)


def gather_plane(own, first, second):
    plane = [jnp.stack([own] + [step(own, first, k) for k in range(1, SIZES[first])])]
    for _ in range(SIZES[second] - 1):
        plane.append(step(plane[-1], second))
    return plane


def passed_on(after, before, up, down):
    f32 = lambda a: a.astype(F32)
    n = up.shape[0]
    return (
        after.at[:n].set((f32(after[:n]) + f32(up)).astype(BF)),
        before.at[n:].set((f32(before[n:]) + f32(down)).astype(BF)),
    )


def scatter_line(own, after, before, axis):
    f32 = lambda a: a.astype(F32)
    return (f32(own) + f32(shift(after, axis, 1)) + f32(shift(before, axis, -1))).astype(BF)


def scatter_last(line, axis):
    return sum([line[0].astype(F32)] + [shift(line[k], axis, k).astype(F32) for k in range(1, SIZES[axis])])


def shards(tokens, out_grad, expert_ids, gate_values, gate_weight, down_weight):
    scale = 1.0 / math.sqrt(NY * NX * NC * NZ * ROWS * 8 / 64)
    y, x, c, z = (lax.axis_index(a) for a in ("y", "x", "c", "z"))
    pos = jnp.stack([y, x, c, (z * NC + c) * EXPERTS_CORE, 1 - 2 * c]).astype(jnp.int32)
    meta = jnp.concatenate([expert_ids.T.astype(BF), gate_values.T], axis=0)
    meta = jnp.pad(meta, ((0, ROWS - META), (0, 0)))
    rows = lax.all_gather(jnp.concatenate([tokens, out_grad, meta], axis=1), ("c", "z"), axis=0, tiled=True)

    def by_core(own, sister):
        return jnp.where(c == 0, own, sister), jnp.where(c == 0, sister, own)

    def halves(weight):
        rows = weight.transpose(1, 0, 2).reshape(NC, EXPERTS_CORE, weight.shape[0], HID)
        return by_core(rows[0], rows[1])

    (keep_a, send_a), (keep_b, send_b) = halves(gate_weight), halves(down_weight)
    got = swap(jnp.stack([send_a, send_b]))
    own_a = jnp.concatenate(by_core(keep_a, got[0]), axis=1)
    own_b = jnp.concatenate(by_core(keep_b, got[1]), axis=1)
    a_in = gather_plane(own_a, "x", "y")
    b_in = gather_plane(own_b, "y", "x")
    own, sister, a_out, b_out = layer(scale, pos, rows, a_in, b_in)
    a_up, a_down = shift(a_out[2], "y", 1), shift(a_out[3], "y", -1)
    b_up, b_down = shift(b_out[2], "x", 1), shift(b_out[3], "x", -1)
    a_ends = passed_on(a_out[1], a_out[4], a_up, a_down)
    b_ends = passed_on(b_out[1], b_out[4], b_up, b_down)
    partial = add(own, swap(sister), (*a_ends, *b_ends))
    input_grad = lax.psum_scatter(partial, "z", scatter_dimension=0, tiled=True)
    a_line = scatter_line(a_out[0], *a_ends, "y")
    b_line = scatter_line(b_out[0], *b_ends, "x")

    sums = jnp.stack([scatter_last(a_line, "x"), scatter_last(b_line, "y")]).astype(BF)
    n = gate_weight.shape[0]
    keep, send = by_core(sums[:, :, :n], sums[:, :, n:])
    back = swap(send)

    def placed(k):
        return jnp.concatenate(by_core(keep[k], back[k])).transpose(1, 0, 2).astype(F32)

    return input_grad, placed(0), placed(1)


def solution(mesh):
    fine = Mesh(mesh.devices.reshape(NY, NX, NC, NZ), ("y", "x", "c", "z"))
    rows = P(("y", "x", "c", "z"), None)
    weights = P(("y", "x", "c"), "z", None)
    return jax.shard_map(
        shards,
        mesh=fine,
        in_specs=(rows, rows, rows, rows, weights, weights),
        out_specs=(rows, weights, weights),
        check_vma=False,
    )
```

profile of v0, /device:TPU:1, one launch (start us, length us, event | category | flops | bytes accessed | tf_op | source)
XLA Modules:
  0.0 174.4 jit_solution(12361280009384003581)
XLA Ops:
  8.7 1.9 %pad_maximum_fusion.2 = bf16[128,2176]{1,0:T(8,128)(2,1)} fusion(bf16[128,128]{1,0:T(8,128)(2,1)S(1)} %fusion.15, bf16[128,1024]{1,0:T(8,128)(2,1)} %param.15, bf16[128,1024]{1,0:T(8,128)(2,1)} %param.14), kind=kLoop, calls=%fused_computation.8 | loop fusion | flops 1671168 | bytes 1114112 | tf_op jit(solution)/shard_map/concatenate | solution.py:215
  10.8 3.3 %collective-permute-start = (bf16[2,4,32,384]{3,2,1,0:T(8,128)(2,1)S(1)}, bf16[2,4,32,384]{3,2,1,0:T(8,128)(2,1)S(1)}, u32[]{:S(2)}, u32[]{:S(2)}) collective-permute-start(bf16[2,4,32,384]{3,2,1,0:T(8,128)(2,1)S(1)} %pad_maximum_fusion.4), channel_id=1, source_target_pairs={{0,8},{8,0},{1,9},{9,1},{2,10},{10,2},{3,11},{11,3},{4,12},{12,4},... | collective-permute-start | bytes 589832 | tf_op jit(solution)/shard_map/ppermute | solution.py:28
  17.9 3.0 %collective-permute-start.8 = (bf16[4,64,384]{2,1,0:T(8,128)(2,1)S(1)}, bf16[4,64,384]{2,1,0:T(8,128)(2,1)S(1)}, u32[]{:S(2)}, u32[]{:S(2)}) collective-permute-start(bf16[4,64,384]{2,1,0:T(8,128)(2,1)S(1)} %get-tuple-element.95), channel_id=1, source_target_pairs={{0,128},{8,136},{64,192},{72,200},{128,0},{136,8},{192,64},{200,72... | collective-permute-start | bytes 589832 | tf_op jit(solution)/shard_map/ppermute | solution.py:34
  23.1 2.6 %collective-permute-done.1 = bf16[4,64,384]{2,1,0:T(8,128)(2,1)S(1)} collective-permute-done((bf16[4,64,384]{2,1,0:T(8,128)(2,1)S(1)}, bf16[4,64,384]{2,1,0:T(8,128)(2,1)S(1)}, u32[]{:S(2)}, u32[]{:S(2)}) %collective-permute-start.1) | collective-permute-done | bytes 196640 | tf_op jit(solution)/shard_map/ppermute | solution.py:34
  25.6 2.4 %collective-permute-done.3 = bf16[4,64,384]{2,1,0:T(8,128)(2,1)S(1)} collective-permute-done((bf16[4,64,384]{2,1,0:T(8,128)(2,1)S(1)}, bf16[4,64,384]{2,1,0:T(8,128)(2,1)S(1)}, u32[]{:S(2)}, u32[]{:S(2)}) %collective-permute-start.3) | collective-permute-done | bytes 196640 | tf_op jit(solution)/shard_map/ppermute | solution.py:34
  29.2 2.0 %collective-permute-done.9 = bf16[4,64,384]{2,1,0:T(8,128)(2,1)S(1)} collective-permute-done((bf16[4,64,384]{2,1,0:T(8,128)(2,1)S(1)}, bf16[4,64,384]{2,1,0:T(8,128)(2,1)S(1)}, u32[]{:S(2)}, u32[]{:S(2)}) %collective-permute-start.9) | collective-permute-done | bytes 196640 | tf_op jit(solution)/shard_map/ppermute | solution.py:34
  31.3 1.7 collective-permute-start.10
  33.0 6.5 %collective-permute-done.4.refs_3_ = bf16[4,4,64,384]{3,2,1,0:T(8,128)(2,1)S(1)} collective-permute-done((bf16[4,4,64,384]{3,2,1,0:T(8,128)(2,1)S(1)}, bf16[4,4,64,384]{3,2,1,0:T(8,128)(2,1)S(1)}, u32[]{:S(2)}, u32[]{:S(2)}) %collective-permute-start.4) | collective-permute-done | bytes 786464 | tf_op jit(solution)/shard_map/ppermute | solution.py:34
  39.5 2.4 %collective-permute-start.5 = (bf16[4,4,64,384]{3,2,1,0:T(8,128)(2,1)S(1)}, bf16[4,4,64,384]{3,2,1,0:T(8,128)(2,1)}, u32[]{:S(2)}, u32[]{:S(2)}) collective-permute-start(bf16[4,4,64,384]{3,2,1,0:T(8,128)(2,1)S(1)} %collective-permute-done.4.refs_3_), channel_id=1, source_target_pairs={{0,64},{8,200},{64,128},{72,8},{128,192},{136,72},{192,0},{200,136... | collective-permute-start | bytes 2359304 | tf_op jit(solution)/shard_map/ppermute | solution.py:34
  42.7 2.8 %collective-permute-start.11 = (bf16[4,4,64,384]{3,2,1,0:T(8,128)(2,1)S(1)}, bf16[4,4,64,384]{3,2,1,0:T(8,128)(2,1)}, u32[]{:S(2)}, u32[]{:S(2)}) collective-permute-start(bf16[4,4,64,384]{3,2,1,0:T(8,128)(2,1)S(1)} %collective-permute-done.10.refs_7_), channel_id=1, source_target_pairs={{0,16},{8,56},{16,32},{24,8},{32,48},{40,24},{48,0},{56,40},{1,17}... | collective-permute-start | bytes 2359304 | tf_op jit(solution)/shard_map/ppermute | solution.py:34
  45.5 5.4 %collective-permute-done.5.refs_4_ = bf16[4,4,64,384]{3,2,1,0:T(8,128)(2,1)} collective-permute-done((bf16[4,4,64,384]{3,2,1,0:T(8,128)(2,1)S(1)}, bf16[4,4,64,384]{3,2,1,0:T(8,128)(2,1)}, u32[]{:S(2)}, u32[]{:S(2)}) %collective-permute-start.5) | collective-permute-done | bytes 786464 | tf_op jit(solution)/shard_map/ppermute | solution.py:34
  50.8 3.5 %collective-permute-start.6 = (bf16[4,4,64,384]{3,2,1,0:T(8,128)(2,1)}, bf16[4,4,64,384]{3,2,1,0:T(8,128)(2,1)}, u32[]{:S(2)}, u32[]{:S(2)}) collective-permute-start(bf16[4,4,64,384]{3,2,1,0:T(8,128)(2,1)} %collective-permute-done.5.refs_4_), channel_id=1, source_target_pairs={{0,64},{8,200},{64,128},{72,8},{128,192},{136,72},{192,0},{200,136... | collective-permute-start | bytes 2359304 | tf_op jit(solution)/shard_map/ppermute | solution.py:34
  54.4 3.5 %collective-permute-start.12 = (bf16[4,4,64,384]{3,2,1,0:T(8,128)(2,1)}, bf16[4,4,64,384]{3,2,1,0:T(8,128)(2,1)}, u32[]{:S(2)}, u32[]{:S(2)}) collective-permute-start(bf16[4,4,64,384]{3,2,1,0:T(8,128)(2,1)} %collective-permute-done.11.refs_8_), channel_id=1, source_target_pairs={{0,16},{8,56},{16,32},{24,8},{32,48},{40,24},{48,0},{56,40},{1,17}... | collective-permute-start | bytes 2359304 | tf_op jit(solution)/shard_map/ppermute | solution.py:34
  58.5 5.1 %collective-permute-done.6.refs_5_ = bf16[4,4,64,384]{3,2,1,0:T(8,128)(2,1)} collective-permute-done((bf16[4,4,64,384]{3,2,1,0:T(8,128)(2,1)}, bf16[4,4,64,384]{3,2,1,0:T(8,128)(2,1)}, u32[]{:S(2)}, u32[]{:S(2)}) %collective-permute-start.6) | collective-permute-done | bytes 786464 | tf_op jit(solution)/shard_map/ppermute | solution.py:34
  63.6 3.6 %collective-permute-done.12.refs_9_ = bf16[4,4,64,384]{3,2,1,0:T(8,128)(2,1)} collective-permute-done((bf16[4,4,64,384]{3,2,1,0:T(8,128)(2,1)}, bf16[4,4,64,384]{3,2,1,0:T(8,128)(2,1)}, u32[]{:S(2)}, u32[]{:S(2)}) %collective-permute-start.12) | collective-permute-done | bytes 786464 | tf_op jit(solution)/shard_map/ppermute | solution.py:34
  67.2 6.2 %all-gather.2.cloned.1.call-done.refs_1_ = bf16[2048,2176]{1,0:T(8,128)(2,1)} async-done(((bf16[128,2176]{1,0:T(8,128)(2,1)}), bf16[2048,2176]{1,0:T(8,128)(2,1)}) %all-gather.2.cloned.1.call-update) | async-done | bytes 8912912 | tf_op jit(solution)/shard_map/all_gather | solution.py:215
  73.4 23.5 %shard_map.85 = (bf16[1024,1024]{1,0:T(8,128)(2,1)}, bf16[1024,1024]{1,0:T(8,128)(2,1)}, bf16[4,4,64,384]{3,2,1,0:T(8,128)(2,1)}, bf16[4,4,64,384]{3,2,1,0:T(8,1...) custom-call(s32[5]{0:T(128)} %stack.74.refs_0_, ...), custom_call_target="tpu_custom_call" | custom-call | flops 12999999488 | bytes 26000000 | tf_op jit(solution)/shard_map/pallas_call | solution.py:147
  101.1 1.5 collective-permute-start.17
  102.6 6.5 %collective-permute-done.14 = bf16[2,4,64,384]{3,2,1,0:T(8,128)(2,1)S(1)} collective-permute-done((bf16[2,4,64,384]{3,2,1,0:T(8,128)(2,1)}, bf16[2,4,64,384]{3,2,1,0:T(8,128)(2,1)S(1)}, u32[]{:S(2)}, u32[]{:S(2)}) %collective-permute-start.14) | collective-permute-done | bytes 393248 | tf_op jit(solution)/shard_map/ppermute | solution.py:39
  109.1 1.9 %fusion.refs_0_ = bf16[4,4,64,384]{3,2,1,0:T(8,128)(2,1)} fusion(bf16[4,4,64,384]{3,2,1,0:T(8,128)(2,1)} %get-tuple-element.65, bf16[2,4,64,384]{3,2,1,0:T(8,128)(2,1)S(1)} %collective-permute-done.14), kind=kLoop, calls=%fused_computation.9 | loop fusion | flops 786432 | bytes 1179648 | tf_op jit(solution)/shard_map/scatter | solution.py:195
  111.0 1.9 %fusion.1.refs_1_ = bf16[4,4,64,384]{3,2,1,0:T(8,128)(2,1)} fusion(bf16[4,4,64,384]{3,2,1,0:T(8,128)(2,1)} %get-tuple-element.67, bf16[2,4,64,384]{3,2,1,0:T(8,128)(2,1)S(1)} %collective-permute-done.15), kind=kLoop, calls=%fused_computation.10 | loop fusion | flops 786432 | bytes 1179648 | tf_op jit(solution)/shard_map/scatter | solution.py:196
  115.2 4.3 %shard_map.86 = bf16[1024,1024]{1,0:T(8,128)(2,1)} custom-call(bf16[1024,1024]{1,0:T(8,128)(2,1)} %get-tuple-element.63.own, bf16[1024,1024]{1,0:T(8,128)(2,1)} %copy-done, bf16[4,4,64,384]{3,2,1,0:T(8,128)(2,1)} %fusion.refs_0_, bf16[4,4,64,384]{3,2,1,0:T(8,128)(2,1)} %fusion.1.refs_1_, bf16[4,4,64,384]{3,2,1,0:T(8,128)(2,1)} %copy-done.5, ...), custom_call_target="tpu_custom_call" | custom-call | flops 1000000 | bytes 6000000 | tf_op jit(solution)/shard_map/pallas_call | solution.py:173
  120.6 2.4 %collective-permute-start.24 = (bf16[4,4,64,384]{3,2,1,0:T(8,128)(2,1)S(1)}, bf16[4,4,64,384]{3,2,1,0:T(8,128)(2,1)S(1)}, u32[]{:S(2)}, u32[]{:S(2)}) collective-permute-start(bf16[4,4,64,384]{3,2,1,0:T(8,128)(2,1)S(1)} %copy-done.3), channel_id=1, source_target_pairs={{0,48},{16,0},{32,16},{48,32},{1,49},{17,1},{33,17},{49,33},{2,50}... | collective-permute-start | bytes 2359304 | tf_op jit(solution)/shard_map/ppermute | solution.py:39
  124.5 14.3 %collective-permute-done.24 = bf16[4,4,64,384]{3,2,1,0:T(8,128)(2,1)S(1)} collective-permute-done((bf16[4,4,64,384]{3,2,1,0:T(8,128)(2,1)S(1)}, bf16[4,4,64,384]{3,2,1,0:T(8,128)(2,1)S(1)}, u32[]{:S(2)}, u32[]{:S(2)}) %collective-permute-start.24) | collective-permute-done | bytes 786464 | tf_op jit(solution)/shard_map/ppermute | solution.py:39
  138.8 3.2 %collective-permute-done.23 = bf16[4,4,64,384]{3,2,1,0:T(8,128)(2,1)S(1)} collective-permute-done((bf16[4,4,64,384]{3,2,1,0:T(8,128)(2,1)S(1)}, bf16[4,4,64,384]{3,2,1,0:T(8,128)(2,1)S(1)}, u32[]{:S(2)}, u32[]{:S(2)}) %collective-permute-start.23) | collective-permute-done | bytes 786464 | tf_op jit(solution)/shard_map/ppermute | solution.py:39
  142.0 1.6 add_convert_fusion
  143.8 2.7 %collective-permute-start.27 = (bf16[4,64,384]{2,1,0:T(8,128)(2,1)S(1)}, bf16[4,64,384]{2,1,0:T(8,128)(2,1)S(1)}, u32[]{:S(2)}, u32[]{:S(2)}) collective-permute-start(bf16[4,64,384]{2,1,0:T(8,128)(2,1)S(1)} %get-tuple-element.82), channel_id=1, source_target_pairs={{0,192},{64,0},{128,64},{192,128},{1,193},{65,1},{129,65},{193,129... | collective-permute-start | bytes 589832 | tf_op jit(solution)/shard_map/ppermute | solution.py:39
  147.2 2.7 %collective-permute-start.22 = (bf16[4,64,384]{2,1,0:T(8,128)(2,1)S(1)}, bf16[4,64,384]{2,1,0:T(8,128)(2,1)S(1)}, u32[]{:S(2)}, u32[]{:S(2)}) collective-permute-start(bf16[4,64,384]{2,1,0:T(8,128)(2,1)S(1)} %get-tuple-element.79), channel_id=1, source_target_pairs={{0,48},{16,0},{32,16},{48,32},{1,49},{17,1},{33,17},{49,33},{2,50}... | collective-permute-start | bytes 589832 | tf_op jit(solution)/shard_map/ppermute | solution.py:39
  149.9 1.7 collective-permute-done.27
  151.6 3.0 %collective-permute-done.26 = bf16[4,64,384]{2,1,0:T(8,128)(2,1)S(1)} collective-permute-done((bf16[4,64,384]{2,1,0:T(8,128)(2,1)S(1)}, bf16[4,64,384]{2,1,0:T(8,128)(2,1)S(1)}, u32[]{:S(2)}, u32[]{:S(2)}) %collective-permute-start.26) | collective-permute-done | bytes 196640 | tf_op jit(solution)/shard_map/ppermute | solution.py:39
  154.8 2.4 %collective-permute-done.21 = bf16[4,64,384]{2,1,0:T(8,128)(2,1)S(1)} collective-permute-done((bf16[4,64,384]{2,1,0:T(8,128)(2,1)S(1)}, bf16[4,64,384]{2,1,0:T(8,128)(2,1)S(1)}, u32[]{:S(2)}, u32[]{:S(2)}) %collective-permute-start.21) | collective-permute-done | bytes 196640 | tf_op jit(solution)/shard_map/ppermute | solution.py:39
  157.4 7.1 %collective-permute-start.28 = (bf16[2,4,32,384]{3,2,1,0:T(8,128)(2,1)S(1)}, bf16[2,4,32,384]{3,2,1,0:T(8,128)(2,1)S(1)}, u32[]{:S(2)}, u32[]{:S(2)}) collective-permute-start(bf16[2,4,32,384]{3,2,1,0:T(8,128)(2,1)S(1)} %get-tuple-element.89), channel_id=1, source_target_pairs={{0,8},{8,0},{1,9},{9,1},{2,10},{10,2},{3,11},{11,3},{4,12},{12,4},... | collective-permute-start | bytes 589832 | tf_op jit(solution)/shard_map/ppermute | solution.py:28
  (91 shorter events, 23.6 us)
Async XLA Ops:
  7.2 66.2 %all-gather.2.cloned.1.call-start = ((), (), s32[]{:S(2)}) async-start(), calls=%async_computation.1 | async-start | bytes 9469952 | tf_op jit(solution)/shard_map/all_gather | solution.py:215
  10.6 157.0 %reduce-scatter.2.cloned.1.call-start = ((), (), s32[]{:S(2)}) async-start(), calls=%async_computation.2 | async-start | bytes 2359296 | tf_op jit(solution)/shard_map/reduce_scatter | solution.py:236
  10.8 4.4 %collective-permute-start = (bf16[2,4,32,384]{3,2,1,0:T(8,128)(2,1)S(1)}, bf16[2,4,32,384]{3,2,1,0:T(8,128)(2,1)S(1)}, u32[]{:S(2)}, u32[]{:S(2)}) collective-permute-start(bf16[2,4,32,384]{3,2,1,0:T(8,128)(2,1)S(1)} %pad_maximum_fusion.4), channel_id=1, source_target_pairs={{0,8},{8,0},{1,9},{9,1},{2,10},{10,2},{3,11},{11,3},{4,12},{12,4},... | collective-permute-start | bytes 589832 | tf_op jit(solution)/shard_map/ppermute | solution.py:28
  15.3 7.7 %collective-permute-start.2 = (bf16[4,64,384]{2,1,0:T(8,128)(2,1)S(1)}, bf16[4,64,384]{2,1,0:T(8,128)(2,1)S(1)}, u32[]{:S(2)}, u32[]{:S(2)}) collective-permute-start(bf16[4,64,384]{2,1,0:T(8,128)(2,1)S(1)} %get-tuple-element.99), channel_id=1, source_target_pairs={{0,32},{8,40},{16,48},{24,56},{32,0},{40,8},{48,16},{56,24},{1,33}... | collective-permute-start | bytes 589832 | tf_op jit(solution)/shard_map/ppermute | solution.py:34
  16.4 9.2 %collective-permute-start.1 = (bf16[4,64,384]{2,1,0:T(8,128)(2,1)S(1)}, bf16[4,64,384]{2,1,0:T(8,128)(2,1)S(1)}, u32[]{:S(2)}, u32[]{:S(2)}) collective-permute-start(bf16[4,64,384]{2,1,0:T(8,128)(2,1)S(1)} %get-tuple-element.99), channel_id=1, source_target_pairs={{0,16},{8,56},{16,32},{24,8},{32,48},{40,24},{48,0},{56,40},{1,17}... | collective-permute-start | bytes 589832 | tf_op jit(solution)/shard_map/ppermute | solution.py:34
  17.3 10.7 %collective-permute-start.3 = (bf16[4,64,384]{2,1,0:T(8,128)(2,1)S(1)}, bf16[4,64,384]{2,1,0:T(8,128)(2,1)S(1)}, u32[]{:S(2)}, u32[]{:S(2)}) collective-permute-start(bf16[4,64,384]{2,1,0:T(8,128)(2,1)S(1)} %get-tuple-element.99), channel_id=1, source_target_pairs={{0,48},{8,24},{16,0},{24,40},{32,16},{40,56},{48,32},{56,8},{1,49}... | collective-permute-start | bytes 589832 | tf_op jit(solution)/shard_map/ppermute | solution.py:34
  17.9 11.3 %collective-permute-start.8 = (bf16[4,64,384]{2,1,0:T(8,128)(2,1)S(1)}, bf16[4,64,384]{2,1,0:T(8,128)(2,1)S(1)}, u32[]{:S(2)}, u32[]{:S(2)}) collective-permute-start(bf16[4,64,384]{2,1,0:T(8,128)(2,1)S(1)} %get-tuple-element.95), channel_id=1, source_target_pairs={{0,128},{8,136},{64,192},{72,200},{128,0},{136,8},{192,64},{200,72... | collective-permute-start | bytes 589832 | tf_op jit(solution)/shard_map/ppermute | solution.py:34
  20.9 8.3 %collective-permute-start.7 = (bf16[4,64,384]{2,1,0:T(8,128)(2,1)S(1)}, bf16[4,64,384]{2,1,0:T(8,128)(2,1)S(1)}, u32[]{:S(2)}, u32[]{:S(2)}) collective-permute-start(bf16[4,64,384]{2,1,0:T(8,128)(2,1)S(1)} %get-tuple-element.95), channel_id=1, source_target_pairs={{0,64},{8,200},{64,128},{72,8},{128,192},{136,72},{192,0},{200,136... | collective-permute-start | bytes 589832 | tf_op jit(solution)/shard_map/ppermute | solution.py:34
  23.1 8.2 %collective-permute-start.9 = (bf16[4,64,384]{2,1,0:T(8,128)(2,1)S(1)}, bf16[4,64,384]{2,1,0:T(8,128)(2,1)S(1)}, u32[]{:S(2)}, u32[]{:S(2)}) collective-permute-start(bf16[4,64,384]{2,1,0:T(8,128)(2,1)S(1)} %get-tuple-element.95), channel_id=1, source_target_pairs={{0,192},{8,72},{64,0},{72,136},{128,64},{136,200},{192,128},{200,8... | collective-permute-start | bytes 589832 | tf_op jit(solution)/shard_map/ppermute | solution.py:34
  28.1 45.2 %copy-start.7 = (bf16[4,4,64,384]{3,2,1,0:T(8,128)(2,1)}, bf16[4,4,64,384]{3,2,1,0:T(8,128)(2,1)S(1)}, u32[]{:S(2)}) copy-start(bf16[4,4,64,384]{3,2,1,0:T(8,128)(2,1)S(1)} %pad_maximum_fusion.refs_2_) | copy-start | bytes 2359300
  28.2 11.4 %collective-permute-start.4 = (bf16[4,4,64,384]{3,2,1,0:T(8,128)(2,1)S(1)}, bf16[4,4,64,384]{3,2,1,0:T(8,128)(2,1)S(1)}, u32[]{:S(2)}, u32[]{:S(2)}) collective-permute-start(bf16[4,4,64,384]{3,2,1,0:T(8,128)(2,1)S(1)} %pad_maximum_fusion.refs_2_), channel_id=1, source_target_pairs={{0,64},{8,200},{64,128},{72,8},{128,192},{136,72},{192,0},{200,136... | collective-permute-start | bytes 2359304 | tf_op jit(solution)/shard_map/ppermute | solution.py:34
  31.3 11.3 %collective-permute-start.10 = (bf16[4,4,64,384]{3,2,1,0:T(8,128)(2,1)S(1)}, bf16[4,4,64,384]{3,2,1,0:T(8,128)(2,1)S(1)}, u32[]{:S(2)}, u32[]{:S(2)}) collective-permute-start(bf16[4,4,64,384]{3,2,1,0:T(8,128)(2,1)S(1)} %pad_maximum_fusion.1.refs_6_), channel_id=1, source_target_pairs={{0,16},{8,56},{16,32},{24,8},{32,48},{40,24},{48,0},{56,40},{1,17}... | collective-permute-start | bytes 2359304 | tf_op jit(solution)/shard_map/ppermute | solution.py:34
  39.5 11.3 %collective-permute-start.5 = (bf16[4,4,64,384]{3,2,1,0:T(8,128)(2,1)S(1)}, bf16[4,4,64,384]{3,2,1,0:T(8,128)(2,1)}, u32[]{:S(2)}, u32[]{:S(2)}) collective-permute-start(bf16[4,4,64,384]{3,2,1,0:T(8,128)(2,1)S(1)} %collective-permute-done.4.refs_3_), channel_id=1, source_target_pairs={{0,64},{8,200},{64,128},{72,8},{128,192},{136,72},{192,0},{200,136... | collective-permute-start | bytes 2359304 | tf_op jit(solution)/shard_map/ppermute | solution.py:34
  42.7 11.8 %collective-permute-start.11 = (bf16[4,4,64,384]{3,2,1,0:T(8,128)(2,1)S(1)}, bf16[4,4,64,384]{3,2,1,0:T(8,128)(2,1)}, u32[]{:S(2)}, u32[]{:S(2)}) collective-permute-start(bf16[4,4,64,384]{3,2,1,0:T(8,128)(2,1)S(1)} %collective-permute-done.10.refs_7_), channel_id=1, source_target_pairs={{0,16},{8,56},{16,32},{24,8},{32,48},{40,24},{48,0},{56,40},{1,17}... | collective-permute-start | bytes 2359304 | tf_op jit(solution)/shard_map/ppermute | solution.py:34
  50.8 12.8 %collective-permute-start.6 = (bf16[4,4,64,384]{3,2,1,0:T(8,128)(2,1)}, bf16[4,4,64,384]{3,2,1,0:T(8,128)(2,1)}, u32[]{:S(2)}, u32[]{:S(2)}) collective-permute-start(bf16[4,4,64,384]{3,2,1,0:T(8,128)(2,1)} %collective-permute-done.5.refs_4_), channel_id=1, source_target_pairs={{0,64},{8,200},{64,128},{72,8},{128,192},{136,72},{192,0},{200,136... | collective-permute-start | bytes 2359304 | tf_op jit(solution)/shard_map/ppermute | solution.py:34
  54.4 12.8 %collective-permute-start.12 = (bf16[4,4,64,384]{3,2,1,0:T(8,128)(2,1)}, bf16[4,4,64,384]{3,2,1,0:T(8,128)(2,1)}, u32[]{:S(2)}, u32[]{:S(2)}) collective-permute-start(bf16[4,4,64,384]{3,2,1,0:T(8,128)(2,1)} %collective-permute-done.11.refs_8_), channel_id=1, source_target_pairs={{0,16},{8,56},{16,32},{24,8},{32,48},{40,24},{48,0},{56,40},{1,17}... | collective-permute-start | bytes 2359304 | tf_op jit(solution)/shard_map/ppermute | solution.py:34
  96.9 16.7 %collective-permute-start.13 = (bf16[1024,1024]{1,0:T(8,128)(2,1)}, bf16[1024,1024]{1,0:T(8,128)(2,1)S(1)}, u32[]{:S(2)}, u32[]{:S(2)}) collective-permute-start(bf16[1024,1024]{1,0:T(8,128)(2,1)} %get-tuple-element.64), channel_id=1, source_target_pairs={{0,8},{8,0},{1,9},{9,1},{2,10},{10,2},{3,11},{11,3},{4,12},{12,4},... | collective-permute-start | bytes 6291464 | tf_op jit(solution)/shard_map/ppermute | solution.py:28
  97.2 11.9 %collective-permute-start.14 = (bf16[2,4,64,384]{3,2,1,0:T(8,128)(2,1)}, bf16[2,4,64,384]{3,2,1,0:T(8,128)(2,1)S(1)}, u32[]{:S(2)}, u32[]{:S(2)}) collective-permute-start(bf16[2,4,64,384]{3,2,1,0:T(8,128)(2,1)} %get-tuple-element.66), channel_id=1, source_target_pairs={{0,64},{64,128},{128,192},{192,0},{1,65},{65,129},{129,193},{193,1... | collective-permute-start | bytes 1179656 | tf_op jit(solution)/shard_map/ppermute | solution.py:39
  98.4 12.6 %collective-permute-start.15 = (bf16[2,4,64,384]{3,2,1,0:T(8,128)(2,1)}, bf16[2,4,64,384]{3,2,1,0:T(8,128)(2,1)S(1)}, u32[]{:S(2)}, u32[]{:S(2)}) collective-permute-start(bf16[2,4,64,384]{3,2,1,0:T(8,128)(2,1)} %get-tuple-element.68), channel_id=1, source_target_pairs={{0,192},{64,0},{128,64},{192,128},{1,193},{65,1},{129,65},{193,129... | collective-permute-start | bytes 1179656 | tf_op jit(solution)/shard_map/ppermute | solution.py:39
  99.9 13.0 %collective-permute-start.16 = (bf16[2,4,64,384]{3,2,1,0:T(8,128)(2,1)}, bf16[2,4,64,384]{3,2,1,0:T(8,128)(2,1)S(1)}, u32[]{:S(2)}, u32[]{:S(2)}) collective-permute-start(bf16[2,4,64,384]{3,2,1,0:T(8,128)(2,1)} %get-tuple-element.70), channel_id=1, source_target_pairs={{0,16},{16,32},{32,48},{48,0},{1,17},{17,33},{33,49},{49,1},{2,18}... | collective-permute-start | bytes 1179656 | tf_op jit(solution)/shard_map/ppermute | solution.py:39
  101.1 12.2 %collective-permute-start.17 = (bf16[2,4,64,384]{3,2,1,0:T(8,128)(2,1)}, bf16[2,4,64,384]{3,2,1,0:T(8,128)(2,1)S(1)}, u32[]{:S(2)}, u32[]{:S(2)}) collective-permute-start(bf16[2,4,64,384]{3,2,1,0:T(8,128)(2,1)} %get-tuple-element.72), channel_id=1, source_target_pairs={{0,48},{16,0},{32,16},{48,32},{1,49},{17,1},{33,17},{49,33},{2,50}... | collective-permute-start | bytes 1179656 | tf_op jit(solution)/shard_map/ppermute | solution.py:39
  120.6 18.2 %collective-permute-start.24 = (bf16[4,4,64,384]{3,2,1,0:T(8,128)(2,1)S(1)}, bf16[4,4,64,384]{3,2,1,0:T(8,128)(2,1)S(1)}, u32[]{:S(2)}, u32[]{:S(2)}) collective-permute-start(bf16[4,4,64,384]{3,2,1,0:T(8,128)(2,1)S(1)} %copy-done.3), channel_id=1, source_target_pairs={{0,48},{16,0},{32,16},{48,32},{1,49},{17,1},{33,17},{49,33},{2,50}... | collective-permute-start | bytes 2359304 | tf_op jit(solution)/shard_map/ppermute | solution.py:39
  123.0 19.0 %collective-permute-start.23 = (bf16[4,4,64,384]{3,2,1,0:T(8,128)(2,1)S(1)}, bf16[4,4,64,384]{3,2,1,0:T(8,128)(2,1)S(1)}, u32[]{:S(2)}, u32[]{:S(2)}) collective-permute-start(bf16[4,4,64,384]{3,2,1,0:T(8,128)(2,1)S(1)} %copy-done.6), channel_id=1, source_target_pairs={{0,16},{16,32},{32,48},{48,0},{1,17},{17,33},{33,49},{49,1},{2,18}... | collective-permute-start | bytes 2359304 | tf_op jit(solution)/shard_map/ppermute | solution.py:39
  123.0 23.6 %collective-permute-start.19 = (bf16[4,4,64,384]{3,2,1,0:T(8,128)(2,1)}, bf16[4,4,64,384]{3,2,1,0:T(8,128)(2,1)S(1)}, u32[]{:S(2)}, u32[]{:S(2)}) collective-permute-start(bf16[4,4,64,384]{3,2,1,0:T(8,128)(2,1)} %fusion.1.refs_1_), channel_id=1, source_target_pairs={{0,192},{64,0},{128,64},{192,128},{1,193},{65,1},{129,65},{193,129... | collective-permute-start | bytes 2359304 | tf_op jit(solution)/shard_map/ppermute | solution.py:39
  124.3 22.4 %collective-permute-start.18 = (bf16[4,4,64,384]{3,2,1,0:T(8,128)(2,1)}, bf16[4,4,64,384]{3,2,1,0:T(8,128)(2,1)S(1)}, u32[]{:S(2)}, u32[]{:S(2)}) collective-permute-start(bf16[4,4,64,384]{3,2,1,0:T(8,128)(2,1)} %fusion.refs_0_), channel_id=1, source_target_pairs={{0,64},{64,128},{128,192},{192,0},{1,65},{65,129},{129,193},{193,1... | collective-permute-start | bytes 2359304 | tf_op jit(solution)/shard_map/ppermute | solution.py:39
  143.7 6.2 %collective-permute-start.25 = (bf16[4,64,384]{2,1,0:T(8,128)(2,1)S(1)}, bf16[4,64,384]{2,1,0:T(8,128)(2,1)S(1)}, u32[]{:S(2)}, u32[]{:S(2)}) collective-permute-start(bf16[4,64,384]{2,1,0:T(8,128)(2,1)S(1)} %get-tuple-element.81), channel_id=1, source_target_pairs={{0,64},{64,128},{128,192},{192,0},{1,65},{65,129},{129,193},{193,1... | collective-permute-start | bytes 589832 | tf_op jit(solution)/shard_map/ppermute | solution.py:39
  143.8 7.9 %collective-permute-start.27 = (bf16[4,64,384]{2,1,0:T(8,128)(2,1)S(1)}, bf16[4,64,384]{2,1,0:T(8,128)(2,1)S(1)}, u32[]{:S(2)}, u32[]{:S(2)}) collective-permute-start(bf16[4,64,384]{2,1,0:T(8,128)(2,1)S(1)} %get-tuple-element.82), channel_id=1, source_target_pairs={{0,192},{64,0},{128,64},{192,128},{1,193},{65,1},{129,65},{193,129... | collective-permute-start | bytes 589832 | tf_op jit(solution)/shard_map/ppermute | solution.py:39
  146.4 8.2 %collective-permute-start.26 = (bf16[4,64,384]{2,1,0:T(8,128)(2,1)S(1)}, bf16[4,64,384]{2,1,0:T(8,128)(2,1)S(1)}, u32[]{:S(2)}, u32[]{:S(2)}) collective-permute-start(bf16[4,64,384]{2,1,0:T(8,128)(2,1)S(1)} %get-tuple-element.83), channel_id=1, source_target_pairs={{0,128},{64,192},{128,0},{192,64},{1,129},{65,193},{129,1},{193,65... | collective-permute-start | bytes 589832 | tf_op jit(solution)/shard_map/ppermute | solution.py:39
  147.1 7.7 %collective-permute-start.20 = (bf16[4,64,384]{2,1,0:T(8,128)(2,1)S(1)}, bf16[4,64,384]{2,1,0:T(8,128)(2,1)S(1)}, u32[]{:S(2)}, u32[]{:S(2)}) collective-permute-start(bf16[4,64,384]{2,1,0:T(8,128)(2,1)S(1)} %get-tuple-element.78), channel_id=1, source_target_pairs={{0,16},{16,32},{32,48},{48,0},{1,17},{17,33},{33,49},{49,1},{2,18}... | collective-permute-start | bytes 589832 | tf_op jit(solution)/shard_map/ppermute | solution.py:39
  147.2 7.6 %collective-permute-start.22 = (bf16[4,64,384]{2,1,0:T(8,128)(2,1)S(1)}, bf16[4,64,384]{2,1,0:T(8,128)(2,1)S(1)}, u32[]{:S(2)}, u32[]{:S(2)}) collective-permute-start(bf16[4,64,384]{2,1,0:T(8,128)(2,1)S(1)} %get-tuple-element.79), channel_id=1, source_target_pairs={{0,48},{16,0},{32,16},{48,32},{1,49},{17,1},{33,17},{49,33},{2,50}... | collective-permute-start | bytes 589832 | tf_op jit(solution)/shard_map/ppermute | solution.py:39
  149.9 7.3 %collective-permute-start.21 = (bf16[4,64,384]{2,1,0:T(8,128)(2,1)S(1)}, bf16[4,64,384]{2,1,0:T(8,128)(2,1)S(1)}, u32[]{:S(2)}, u32[]{:S(2)}) collective-permute-start(bf16[4,64,384]{2,1,0:T(8,128)(2,1)S(1)} %get-tuple-element.80), channel_id=1, source_target_pairs={{0,32},{16,48},{32,0},{48,16},{1,33},{17,49},{33,1},{49,17},{2,34}... | collective-permute-start | bytes 589832 | tf_op jit(solution)/shard_map/ppermute | solution.py:39
  157.4 8.1 %collective-permute-start.28 = (bf16[2,4,32,384]{3,2,1,0:T(8,128)(2,1)S(1)}, bf16[2,4,32,384]{3,2,1,0:T(8,128)(2,1)S(1)}, u32[]{:S(2)}, u32[]{:S(2)}) collective-permute-start(bf16[2,4,32,384]{3,2,1,0:T(8,128)(2,1)S(1)} %get-tuple-element.89), channel_id=1, source_target_pairs={{0,8},{8,0},{1,9},{9,1},{2,10},{10,2},{3,11},{11,3},{4,12},{12,4},... | collective-permute-start | bytes 589832 | tf_op jit(solution)/shard_map/ppermute | solution.py:28
  (13 other events, 146.4 us)
Sparse Core Ops, SparseCore 0:
  10.7 62.5 all-gather.1
  119.6 36.7 reduce-scatter.1
where the time goes:
time: 175 us; the launch traced here: 174 us
  waiting for transfers between devices  69.3 us (40%)
  starting transfers between devices  47 us (27%)
  Pallas kernels  27.8 us (16%)
  between operations  14.4 us (8%)
  other arithmetic  10.5 us (6%)
  local copies, waits for them, and re-layouts  5.44 us (3%)
    ppermute x14, waiting for transfers between devices, shift(): return lax.ppermute(value, axis, [(i, (i + by) % n) for i in range(n)])  31.3 us
    ppermute x12, waiting for transfers between devices, step(): return lax.ppermute(value, (axis, 'c'), pairs)  29.7 us
    pallas_call x1, Pallas kernels, layer(): pl.pallas_call(lambda *refs: layer_kernel(scale, *refs), grid_spec=pltpu....  23.5 us
    ppermute x12, starting transfers between devices, step(): return lax.ppermute(value, (axis, 'c'), pairs)  21.3 us
    ppermute x14, starting transfers between devices, shift(): return lax.ppermute(value, axis, [(i, (i + by) % n) for i in range(n)])  14.9 us
    ppermute x3, starting transfers between devices, swap(): return lax.ppermute(value, 'c', [(0, 1), (1, 0)])  10.7 us
    all_gather x1, waiting for transfers between devices, shards(): lax.all_gather(jnp.concatenate([tokens, out_grad, meta], axis=1), ('c', '...  6.16 us
    unnamed x32, local copies, waits for them, and re-layouts  4.72 us
  transfers between devices with their start and end apart: 31, of which 19 were waited for; matrix products, arithmetic and copies ran while one was open for 6% of the time, Pallas kernels for 0%

commit v1 on v0

--- a/solution.py
+++ b/solution.py
@@ -19,6 +19,7 @@
 QUADS = NC * NZ * ROWS // QROWS
 SLOTS = QUADS * QSLOTS
 PIECE = WIDTH // (NY * NX)
+PARTS = (4, 4, 4, 2, 2)
 SIZES = {"y": NY, "x": NX}
 ANYWHERE = pl.BlockSpec(memory_space=pl.ANY)
 PARAMS = pltpu.CompilerParams(vmem_limit_bytes=60 * 2**20)
@@ -60,8 +61,8 @@
 
 def layer_kernel(scale, pos, rows, *refs):
     a_in, b_in = refs[0:4], refs[4:8]
-    sums, a_out, b_out = refs[8:10], refs[10:15], refs[15:20]
-    wg, wd, term, xg, gg, weighting, slot_grad, srow, before = refs[20:]
+    sums, a_out, b_out = refs[8], refs[9:14], refs[14:19]
+    wg, wd, term, xg, gg, weighting, slot_grad, srow, before = refs[19:]
     step_id = pl.program_id(0)
 
     @pl.when(step_id == 0)
@@ -102,12 +103,21 @@
 
     @pl.when(step_id == QUADS + EXPERTS_CORE - 1)
     def _():
-        half = QUADS // 2
-        for other, out in enumerate(sums):
-            for i in range(half):
-                q = (pos[2] ^ other) * half + i
-                total = dot(pick_rows(srow[q]), slot_grad[q], (0, 0))
-                out[i * QROWS : (i + 1) * QROWS, :] = total.astype(BF)
+        n = QROWS // ROWS
+        for q in range(QUADS):
+            total = dot(pick_rows(srow[q]), slot_grad[q], (0, 0)).astype(BF)
+            z = q * n % NZ
+            sums[z : z + n, q * n // NZ] = total.reshape(n, ROWS, WIDTH)
+
+
+def place(k, j):
+    if k == 0:
+        return 0, j
+    if k == 1:
+        return (3, j) if j < 2 else (1, j - 2)
+    if k == 2:
+        return (1, j + 2) if j < 2 else (2, j)
+    return (2, j) if j < 2 else (4, j - 2)
 
 
 def expert_step(scale, pos, e, a_in, b_in, a_out, b_out, wg, wd, term, xg, gg, weighting, slot_grad):
@@ -131,18 +141,15 @@
         for k in range(4):
             for j in range(4):
                 piece = term[pl.ds(row_of(pos, *((k, j) if y_first else (j, k))), PIECE), :]
-                if k == 2:
-                    out[2 + j // 2][j % 2, 0] = piece
-                else:
-                    out[4 if k == 3 else k][j, 0] = piece
+                to, at = place(k, j)
+                out[to][at, 0] = piece
 
 
 def layer(scale, pos, rows, a_in, b_in):
     expert = lambda i: jnp.maximum(i - QUADS, 0)
     piece = lambda n: pl.BlockSpec((n, 1, PIECE, HID), lambda i, p: (0, expert(i), 0, 0))
     grads = lambda n: jax.ShapeDtypeStruct((n, EXPERTS_CORE, PIECE, HID), BF)
-    half = (QUADS * QROWS // 2, WIDTH)
-    sizes = (4, 4, 2, 2, 4) * 2
+    by_z = (NZ, NC, ROWS, WIDTH)
     slots = lambda n, dtype: pltpu.VMEM((EXPERTS_CORE, SLOTS, n), dtype)
     out = pl.pallas_call(
         lambda *refs: layer_kernel(scale, *refs),
@@ -151,34 +158,17 @@
             grid=(QUADS + EXPERTS_CORE,),
             in_specs=[pl.BlockSpec((QROWS, rows.shape[1]), lambda i, p: (jnp.minimum(i, QUADS - 1), 0))]
             + [piece(4)] * 8,
-            out_specs=[pl.BlockSpec(half, lambda i, p: (0, 0))] * 2 + [piece(n) for n in sizes],
+            out_specs=[pl.BlockSpec(by_z, lambda i, p: (0, 0, 0, 0))] + [piece(n) for n in PARTS * 2],
             scratch_shapes=[pltpu.VMEM((WIDTH, HID), BF)] * 3
             + [slots(WIDTH, BF), slots(WIDTH, BF), slots(128, F32)]
             + [pltpu.VMEM((QUADS, EXPERTS_CORE * QSLOTS, WIDTH), BF), pltpu.VMEM((QUADS, 8, QROWS), F32)]
             + [pltpu.VMEM((QROWS, QROWS), BF)],
         ),
-        out_shape=[jax.ShapeDtypeStruct(half, BF)] * 2 + [grads(n) for n in sizes],
+        out_shape=[jax.ShapeDtypeStruct(by_z, BF)] + [grads(n) for n in PARTS * 2],
         compiler_params=PARAMS,
         cost_estimate=cost(13_000_000_000, 26_000_000, 600_000),
     )(pos, rows, *a_in, *b_in)
-    return out[0], out[1], out[2:7], out[7:12]
-
-
-def add_kernel(own, got, *refs):
-    refs[-1][...] = (own[...].astype(F32) + got[...].astype(F32)).astype(BF)
-
-
-def add(own, got, after):
-    rows = pl.BlockSpec((QROWS // 2, WIDTH), lambda i: (i, 0))
-    return pl.pallas_call(
-        add_kernel,
-        grid=(own.shape[0] * 2 // QROWS,),
-        in_specs=[rows, rows] + [ANYWHERE] * len(after),
-        out_specs=rows,
-        out_shape=jax.ShapeDtypeStruct(own.shape, BF),
-        compiler_params=PARAMS,
-        cost_estimate=cost(1_000_000, 6_000_000),
-    )(own, got, *after)
+    return out[0], out[1:6], out[6:11]
 
 
 def gather_plane(own, first, second):
@@ -188,22 +178,17 @@
     return plane
 
 
-def passed_on(after, before, up, down):
+def scatter_plane(parts, first, second):
     f32 = lambda a: a.astype(F32)
-    n = up.shape[0]
-    return (
-        after.at[:n].set((f32(after[:n]) + f32(up)).astype(BF)),
-        before.at[n:].set((f32(before[n:]) + f32(down)).astype(BF)),
-    )
-
-
-def scatter_line(own, after, before, axis):
-    f32 = lambda a: a.astype(F32)
-    return (f32(own) + f32(shift(after, axis, 1)) + f32(shift(before, axis, -1))).astype(BF)
-
-
-def scatter_last(line, axis):
-    return sum([line[0].astype(F32)] + [shift(line[k], axis, k).astype(F32) for k in range(1, SIZES[axis])])
+    own, up, down, next_up, next_down = parts
+    up, down = shift(up, second, 1), shift(down, second, -1)
+    n = own.shape[0] // 2
+    next_up = shift((f32(next_up) + f32(up[n:])).astype(BF), second, 1)
+    next_down = shift((f32(next_down) + f32(down[n:])).astype(BF), second, -1)
+    low = f32(own[:n]) + f32(next_up) + f32(down[:n])
+    high = f32(own[n:]) + f32(up[:n]) + f32(next_down)
+    line = [half[i] for half in (low, high) for i in range(n)]
+    return sum([line[0]] + [f32(shift(line[k].astype(BF), first, k)) for k in range(1, SIZES[first])])
 
 
 def shards(tokens, out_grad, expert_ids, gate_values, gate_weight, down_weight):
@@ -227,25 +212,17 @@
     own_b = jnp.concatenate(by_core(keep_b, got[1]), axis=1)
     a_in = gather_plane(own_a, "x", "y")
     b_in = gather_plane(own_b, "y", "x")
-    own, sister, a_out, b_out = layer(scale, pos, rows, a_in, b_in)
-    a_up, a_down = shift(a_out[2], "y", 1), shift(a_out[3], "y", -1)
-    b_up, b_down = shift(b_out[2], "x", 1), shift(b_out[3], "x", -1)
-    a_ends = passed_on(a_out[1], a_out[4], a_up, a_down)
-    b_ends = passed_on(b_out[1], b_out[4], b_up, b_down)
-    partial = add(own, swap(sister), (*a_ends, *b_ends))
-    input_grad = lax.psum_scatter(partial, "z", scatter_dimension=0, tiled=True)
-    a_line = scatter_line(a_out[0], *a_ends, "y")
-    b_line = scatter_line(b_out[0], *b_ends, "x")
-
-    sums = jnp.stack([scatter_last(a_line, "x"), scatter_last(b_line, "y")]).astype(BF)
-    n = gate_weight.shape[0]
-    keep, send = by_core(sums[:, :, :n], sums[:, :, n:])
-    back = swap(send)
-
-    def placed(k):
-        return jnp.concatenate(by_core(keep[k], back[k])).transpose(1, 0, 2).astype(F32)
-
-    return input_grad, placed(0), placed(1)
+    sums, a_out, b_out = layer(scale, pos, rows, a_in, b_in)
+    keep, send = by_core(*lax.psum_scatter(sums, "z", scatter_dimension=0))
+    input_grad = (keep.astype(F32) + swap(send).astype(F32)).astype(BF)
+
+    def placed(total):
+        n = gate_weight.shape[0]
+        keep, send = by_core(total[:, :n], total[:, n:])
+        both = by_core(keep, swap(send.astype(BF)).astype(F32))
+        return jnp.concatenate(both).transpose(1, 0, 2)
+
+    return input_grad, placed(scatter_plane(a_out, "x", "y")), placed(scatter_plane(b_out, "y", "x"))
 
 
 def solution(mesh):

time: 175 us -> 161 us (0.920)
  waiting for transfers between devices: 69.3 us -> 59.4 us
  starting transfers between devices: 47 us -> 52.9 us
  Pallas kernels: 27.8 us -> 23.5 us
  other arithmetic: 10.5 us -> 7.08 us
    ppermute x14, waiting for transfers between devices: 31.3 us -> 22.4 us  [shift(): return lax.ppermute(value, axis, [(i, (i + by) % n) for i in range(n)])]
    ppermute x14, starting transfers between devices: 14.9 us -> 20.1 us  [shift(): return lax.ppermute(value, axis, [(i, (i + by) % n) for i in range(n)])]
    scatter x4 -> x0, other arithmetic: 4.41 us -> none  [the longest x2 2.23 us: passed_on(): after.at[:n].set((f32(after[:n]) + f32(up)).astype(BF))]
    pallas_call x1 -> x0, Pallas kernels: 4.29 us -> none  [add(): pl.pallas_call(add_kernel, grid=(own.shape[0] * 2 // QROWS,), in_specs=[r...]
    unnamed x32 -> x38, local copies, waits for them, and re-layouts: 4.72 us -> 3.12 us
    ppermute x3 -> x4, starting transfers between devices: 10.7 us -> 11.5 us  [swap(): return lax.ppermute(value, 'c', [(0, 1), (1, 0)])]
  transfers between devices with their start and end apart: 31 -> 32, of which waited for: 19 -> 17; matrix products, arithmetic and copies ran while one was open for 6% -> 4% of each run, Pallas kernels for 0% -> 0%
where the time goes in v1:
time: 161 us
  waiting for transfers between devices  59.4 us (37%)
  starting transfers between devices  52.9 us (33%)
  Pallas kernels  23.5 us (15%)
  between operations  14.4 us (9%)
  other arithmetic  7.08 us (4%)
  local copies, waits for them, and re-layouts  3.87 us (2%)
    ppermute x12, waiting for transfers between devices, step(): return lax.ppermute(value, (axis, 'c'), pairs)  29.7 us
    pallas_call x1, Pallas kernels, layer(): pl.pallas_call(lambda *refs: layer_kernel(scale, *refs), grid_spec=pltpu....  23.5 us
    ppermute x14, waiting for transfers between devices, shift(): return lax.ppermute(value, axis, [(i, (i + by) % n) for i in range(n)])  22.4 us
    ppermute x12, starting transfers between devices, step(): return lax.ppermute(value, (axis, 'c'), pairs)  21.3 us
    ppermute x14, starting transfers between devices, shift(): return lax.ppermute(value, axis, [(i, (i + by) % n) for i in range(n)])  20.1 us
    ppermute x4, starting transfers between devices, swap(): return lax.ppermute(value, 'c', [(0, 1), (1, 0)])  11.5 us
    all_gather x1, waiting for transfers between devices, shards(): lax.all_gather(jnp.concatenate([tokens, out_grad, meta], axis=1), ('c', '...  6.16 us
  transfers between devices with their start and end apart: 32, of which 17 were waited for; matrix products, arithmetic and copies ran while one was open for 4% of the time, Pallas kernels for 0%

profile of v1, /device:TPU:1, one launch (start us, length us, event | category | flops | bytes accessed | tf_op | source)
XLA Modules:
  0.0 161.2 jit_solution(4777107957455545863)
XLA Ops:
  8.7 1.9 %pad_maximum_fusion.2 = bf16[128,2176]{1,0:T(8,128)(2,1)} fusion(bf16[128,128]{1,0:T(8,128)(2,1)S(1)} %fusion.11, bf16[128,1024]{1,0:T(8,128)(2,1)} %param.7, bf16[128,1024]{1,0:T(8,128)(2,1)} %param.6), kind=kLoop, calls=%fused_computation.10 | loop fusion | flops 1671168 | bytes 1114112 | tf_op jit(solution)/shard_map/concatenate | solution.py:200
  10.8 3.3 %collective-permute-start = (bf16[2,4,32,384]{3,2,1,0:T(8,128)(2,1)S(1)}, bf16[2,4,32,384]{3,2,1,0:T(8,128)(2,1)S(1)}, u32[]{:S(2)}, u32[]{:S(2)}) collective-permute-start(bf16[2,4,32,384]{3,2,1,0:T(8,128)(2,1)S(1)} %pad_maximum_fusion.3), channel_id=1, source_target_pairs={{0,8},{8,0},{1,9},{9,1},{2,10},{10,2},{3,11},{11,3},{4,12},{12,4},... | collective-permute-start | bytes 589832 | tf_op jit(solution)/shard_map/ppermute | solution.py:29
  17.9 3.0 %collective-permute-start.8 = (bf16[4,64,384]{2,1,0:T(8,128)(2,1)S(1)}, bf16[4,64,384]{2,1,0:T(8,128)(2,1)S(1)}, u32[]{:S(2)}, u32[]{:S(2)}) collective-permute-start(bf16[4,64,384]{2,1,0:T(8,128)(2,1)S(1)} %get-tuple-element.45), channel_id=1, source_target_pairs={{0,128},{8,136},{64,192},{72,200},{128,0},{136,8},{192,64},{200,72... | collective-permute-start | bytes 589832 | tf_op jit(solution)/shard_map/ppermute | solution.py:35
  21.7 1.4 collective-permute-done.2
  23.1 2.6 %collective-permute-done.1 = bf16[4,64,384]{2,1,0:T(8,128)(2,1)S(1)} collective-permute-done((bf16[4,64,384]{2,1,0:T(8,128)(2,1)S(1)}, bf16[4,64,384]{2,1,0:T(8,128)(2,1)S(1)}, u32[]{:S(2)}, u32[]{:S(2)}) %collective-permute-start.1) | collective-permute-done | bytes 196640 | tf_op jit(solution)/shard_map/ppermute | solution.py:35
  25.6 2.4 %collective-permute-done.3 = bf16[4,64,384]{2,1,0:T(8,128)(2,1)S(1)} collective-permute-done((bf16[4,64,384]{2,1,0:T(8,128)(2,1)S(1)}, bf16[4,64,384]{2,1,0:T(8,128)(2,1)S(1)}, u32[]{:S(2)}, u32[]{:S(2)}) %collective-permute-start.3) | collective-permute-done | bytes 196640 | tf_op jit(solution)/shard_map/ppermute | solution.py:35
  29.2 2.0 %collective-permute-done.9 = bf16[4,64,384]{2,1,0:T(8,128)(2,1)S(1)} collective-permute-done((bf16[4,64,384]{2,1,0:T(8,128)(2,1)S(1)}, bf16[4,64,384]{2,1,0:T(8,128)(2,1)S(1)}, u32[]{:S(2)}, u32[]{:S(2)}) %collective-permute-start.9) | collective-permute-done | bytes 196640 | tf_op jit(solution)/shard_map/ppermute | solution.py:35
  31.3 1.7 %collective-permute-start.10 = (bf16[4,4,64,384]{3,2,1,0:T(8,128)(2,1)S(1)}, bf16[4,4,64,384]{3,2,1,0:T(8,128)(2,1)S(1)}, u32[]{:S(2)}, u32[]{:S(2)}) collective-permute-start(bf16[4,4,64,384]{3,2,1,0:T(8,128)(2,1)S(1)} %pad_maximum_fusion.1.refs_6_), channel_id=1, source_target_pairs={{0,16},{8,56},{16,32},{24,8},{32,48},{40,24},{48,0},{56,40},{1,17}... | collective-permute-start | bytes 2359304 | tf_op jit(solution)/shard_map/ppermute | solution.py:35
  33.0 6.5 %collective-permute-done.4.refs_3_ = bf16[4,4,64,384]{3,2,1,0:T(8,128)(2,1)S(1)} collective-permute-done((bf16[4,4,64,384]{3,2,1,0:T(8,128)(2,1)S(1)}, bf16[4,4,64,384]{3,2,1,0:T(8,128)(2,1)S(1)}, u32[]{:S(2)}, u32[]{:S(2)}) %collective-permute-start.4) | collective-permute-done | bytes 786464 | tf_op jit(solution)/shard_map/ppermute | solution.py:35
  39.5 2.4 %collective-permute-start.5 = (bf16[4,4,64,384]{3,2,1,0:T(8,128)(2,1)S(1)}, bf16[4,4,64,384]{3,2,1,0:T(8,128)(2,1)}, u32[]{:S(2)}, u32[]{:S(2)}) collective-permute-start(bf16[4,4,64,384]{3,2,1,0:T(8,128)(2,1)S(1)} %collective-permute-done.4.refs_3_), channel_id=1, source_target_pairs={{0,64},{8,200},{64,128},{72,8},{128,192},{136,72},{192,0},{200,136... | collective-permute-start | bytes 2359304 | tf_op jit(solution)/shard_map/ppermute | solution.py:35
  42.7 2.8 %collective-permute-start.11 = (bf16[4,4,64,384]{3,2,1,0:T(8,128)(2,1)S(1)}, bf16[4,4,64,384]{3,2,1,0:T(8,128)(2,1)}, u32[]{:S(2)}, u32[]{:S(2)}) collective-permute-start(bf16[4,4,64,384]{3,2,1,0:T(8,128)(2,1)S(1)} %collective-permute-done.10.refs_7_), channel_id=1, source_target_pairs={{0,16},{8,56},{16,32},{24,8},{32,48},{40,24},{48,0},{56,40},{1,17}... | collective-permute-start | bytes 2359304 | tf_op jit(solution)/shard_map/ppermute | solution.py:35
  45.5 5.4 %collective-permute-done.5.refs_4_ = bf16[4,4,64,384]{3,2,1,0:T(8,128)(2,1)} collective-permute-done((bf16[4,4,64,384]{3,2,1,0:T(8,128)(2,1)S(1)}, bf16[4,4,64,384]{3,2,1,0:T(8,128)(2,1)}, u32[]{:S(2)}, u32[]{:S(2)}) %collective-permute-start.5) | collective-permute-done | bytes 786464 | tf_op jit(solution)/shard_map/ppermute | solution.py:35
  50.8 3.5 %collective-permute-start.6 = (bf16[4,4,64,384]{3,2,1,0:T(8,128)(2,1)}, bf16[4,4,64,384]{3,2,1,0:T(8,128)(2,1)}, u32[]{:S(2)}, u32[]{:S(2)}) collective-permute-start(bf16[4,4,64,384]{3,2,1,0:T(8,128)(2,1)} %collective-permute-done.5.refs_4_), channel_id=1, source_target_pairs={{0,64},{8,200},{64,128},{72,8},{128,192},{136,72},{192,0},{200,136... | collective-permute-start | bytes 2359304 | tf_op jit(solution)/shard_map/ppermute | solution.py:35
  54.4 3.5 %collective-permute-start.12 = (bf16[4,4,64,384]{3,2,1,0:T(8,128)(2,1)}, bf16[4,4,64,384]{3,2,1,0:T(8,128)(2,1)}, u32[]{:S(2)}, u32[]{:S(2)}) collective-permute-start(bf16[4,4,64,384]{3,2,1,0:T(8,128)(2,1)} %collective-permute-done.11.refs_8_), channel_id=1, source_target_pairs={{0,16},{8,56},{16,32},{24,8},{32,48},{40,24},{48,0},{56,40},{1,17}... | collective-permute-start | bytes 2359304 | tf_op jit(solution)/shard_map/ppermute | solution.py:35
  58.5 5.1 %collective-permute-done.6.refs_5_ = bf16[4,4,64,384]{3,2,1,0:T(8,128)(2,1)} collective-permute-done((bf16[4,4,64,384]{3,2,1,0:T(8,128)(2,1)}, bf16[4,4,64,384]{3,2,1,0:T(8,128)(2,1)}, u32[]{:S(2)}, u32[]{:S(2)}) %collective-permute-start.6) | collective-permute-done | bytes 786464 | tf_op jit(solution)/shard_map/ppermute | solution.py:35
  63.6 3.6 %collective-permute-done.12.refs_9_ = bf16[4,4,64,384]{3,2,1,0:T(8,128)(2,1)} collective-permute-done((bf16[4,4,64,384]{3,2,1,0:T(8,128)(2,1)}, bf16[4,4,64,384]{3,2,1,0:T(8,128)(2,1)}, u32[]{:S(2)}, u32[]{:S(2)}) %collective-permute-start.12) | collective-permute-done | bytes 786464 | tf_op jit(solution)/shard_map/ppermute | solution.py:35
  67.2 6.2 %all-gather.2.cloned.1.call-done.refs_1_ = bf16[2048,2176]{1,0:T(8,128)(2,1)} async-done(((bf16[128,2176]{1,0:T(8,128)(2,1)}), bf16[2048,2176]{1,0:T(8,128)(2,1)}) %all-gather.2.cloned.1.call-update) | async-done | bytes 8912912 | tf_op jit(solution)/shard_map/all_gather | solution.py:200
  73.4 23.5 %shard_map.85 = (bf16[8,2,128,1024]{3,2,1,0:T(8,128)(2,1)}, bf16[4,4,64,384]{3,2,1,0:T(8,128)(2,1)}, bf16[4,4,64,384]{3,2,1,0:T(8,128)(2,1)}, bf16[4,4,64,384]{3...) custom-call(s32[5]{0:T(128)} %stack.62.refs_0_, ...), custom_call_target="tpu_custom_call" | custom-call | flops 12999999488 | bytes 26000000 | tf_op jit(solution)/shard_map/pallas_call | solution.py:154
  98.0 1.2 collective-permute-start.14
  99.2 1.5 collective-permute-start.16
  101.9 1.5 collective-permute-start.24
  103.3 14.8 %collective-permute-done.14 = bf16[4,4,64,384]{3,2,1,0:T(8,128)(2,1)S(1)} collective-permute-done((bf16[4,4,64,384]{3,2,1,0:T(8,128)(2,1)S(1)}, bf16[4,4,64,384]{3,2,1,0:T(8,128)(2,1)S(1)}, u32[]{:S(2)}, u32[]{:S(2)}) %collective-permute-start.14) | collective-permute-done | bytes 786464 | tf_op jit(solution)/shard_map/ppermute | solution.py:40
  118.5 2.7 %collective-permute-start.18 = (bf16[2,4,64,384]{3,2,1,0:T(8,128)(2,1)S(1)}, bf16[2,4,64,384]{3,2,1,0:T(8,128)(2,1)S(1)}, u32[]{:S(2)}, u32[]{:S(2)}) collective-permute-start(bf16[2,4,64,384]{3,2,1,0:T(8,128)(2,1)S(1)} %add_convert_fusion.4), channel_id=1, source_target_pairs={{0,192},{64,0},{128,64},{192,128},{1,193},{65,1},{129,65},{193,129... | collective-permute-start | bytes 1179656 | tf_op jit(solution)/shard_map/ppermute | solution.py:40
  121.3 1.3 collective-permute-start.23
  122.7 1.6 collective-permute-start.26
  124.3 5.0 %collective-permute-done.15 = bf16[2,4,64,384]{3,2,1,0:T(8,128)(2,1)S(1)} collective-permute-done((bf16[2,4,64,384]{3,2,1,0:T(8,128)(2,1)S(1)}, bf16[2,4,64,384]{3,2,1,0:T(8,128)(2,1)S(1)}, u32[]{:S(2)}, u32[]{:S(2)}) %collective-permute-start.15) | collective-permute-done | bytes 393248 | tf_op jit(solution)/shard_map/ppermute | solution.py:40
  129.7 1.5 collective-permute-start.17
  131.2 2.5 %collective-permute-start.19 = (bf16[4,64,384]{2,1,0:T(8,128)(2,1)S(1)}, bf16[4,64,384]{2,1,0:T(8,128)(2,1)S(1)}, u32[]{:S(2)}, u32[]{:S(2)}) collective-permute-start(bf16[4,64,384]{2,1,0:T(8,128)(2,1)S(1)} %get-tuple-element.38), channel_id=1, source_target_pairs={{0,32},{16,48},{32,0},{48,16},{1,33},{17,49},{33,1},{49,17},{2,34}... | collective-permute-start | bytes 589832 | tf_op jit(solution)/shard_map/ppermute | solution.py:40
  135.5 3.8 %collective-permute-start.27 = (bf16[4,64,384]{2,1,0:T(8,128)(2,1)S(1)}, bf16[4,64,384]{2,1,0:T(8,128)(2,1)S(1)}, u32[]{:S(2)}, u32[]{:S(2)}) collective-permute-start(bf16[4,64,384]{2,1,0:T(8,128)(2,1)S(1)} %get-tuple-element.36), channel_id=1, source_target_pairs={{0,128},{64,192},{128,0},{192,64},{1,129},{65,193},{129,1},{193,65... | collective-permute-start | bytes 589832 | tf_op jit(solution)/shard_map/ppermute | solution.py:40
  139.3 1.4 collective-permute-done.19
  140.8 3.3 %collective-permute-start.21 = (bf16[4,32,384]{2,1,0:T(8,128)(2,1)S(1)}, bf16[4,32,384]{2,1,0:T(8,128)(2,1)S(1)}, u32[]{:S(2)}, u32[]{:S(2)}) collective-permute-start(bf16[4,32,384]{2,1,0:T(8,128)(2,1)S(1)} %select_convert_fusion.1), channel_id=1, source_target_pairs={{0,8},{8,0},{1,9},{9,1},{2,10},{10,2},{3,11},{11,3},{4,12},{12,4},... | collective-permute-start | bytes 294920 | tf_op jit(solution)/shard_map/ppermute | solution.py:29
  145.3 4.2 %collective-permute-start.29 = (bf16[4,32,384]{2,1,0:T(8,128)(2,1)S(1)}, bf16[4,32,384]{2,1,0:T(8,128)(2,1)S(1)}, u32[]{:S(2)}, u32[]{:S(2)}) collective-permute-start(bf16[4,32,384]{2,1,0:T(8,128)(2,1)S(1)} %select_convert_fusion), channel_id=1, source_target_pairs={{0,8},{8,0},{1,9},{9,1},{2,10},{10,2},{3,11},{11,3},{4,12},{12,4},... | collective-permute-start | bytes 294920 | tf_op jit(solution)/shard_map/ppermute | solution.py:29
  (104 shorter events, 19.9 us)
Async XLA Ops:
  7.2 66.2 %all-gather.2.cloned.1.call-start = ((), (), s32[]{:S(2)}) async-start(), calls=%async_computation.1 | async-start | bytes 9469952 | tf_op jit(solution)/shard_map/all_gather | solution.py:200
  10.6 139.9 %reduce-scatter.2.cloned.1.call-start = ((), (), s32[]{:S(2)}) async-start(), calls=%async_computation.2 | async-start | bytes 4718592 | tf_op jit(solution)/shard_map/reduce_scatter | solution.py:216
  10.8 4.4 %collective-permute-start = (bf16[2,4,32,384]{3,2,1,0:T(8,128)(2,1)S(1)}, bf16[2,4,32,384]{3,2,1,0:T(8,128)(2,1)S(1)}, u32[]{:S(2)}, u32[]{:S(2)}) collective-permute-start(bf16[2,4,32,384]{3,2,1,0:T(8,128)(2,1)S(1)} %pad_maximum_fusion.3), channel_id=1, source_target_pairs={{0,8},{8,0},{1,9},{9,1},{2,10},{10,2},{3,11},{11,3},{4,12},{12,4},... | collective-permute-start | bytes 589832 | tf_op jit(solution)/shard_map/ppermute | solution.py:29
  15.3 7.7 %collective-permute-start.2 = (bf16[4,64,384]{2,1,0:T(8,128)(2,1)S(1)}, bf16[4,64,384]{2,1,0:T(8,128)(2,1)S(1)}, u32[]{:S(2)}, u32[]{:S(2)}) collective-permute-start(bf16[4,64,384]{2,1,0:T(8,128)(2,1)S(1)} %get-tuple-element.49), channel_id=1, source_target_pairs={{0,32},{8,40},{16,48},{24,56},{32,0},{40,8},{48,16},{56,24},{1,33}... | collective-permute-start | bytes 589832 | tf_op jit(solution)/shard_map/ppermute | solution.py:35
  16.4 9.2 %collective-permute-start.1 = (bf16[4,64,384]{2,1,0:T(8,128)(2,1)S(1)}, bf16[4,64,384]{2,1,0:T(8,128)(2,1)S(1)}, u32[]{:S(2)}, u32[]{:S(2)}) collective-permute-start(bf16[4,64,384]{2,1,0:T(8,128)(2,1)S(1)} %get-tuple-element.49), channel_id=1, source_target_pairs={{0,16},{8,56},{16,32},{24,8},{32,48},{40,24},{48,0},{56,40},{1,17}... | collective-permute-start | bytes 589832 | tf_op jit(solution)/shard_map/ppermute | solution.py:35
  17.3 10.7 %collective-permute-start.3 = (bf16[4,64,384]{2,1,0:T(8,128)(2,1)S(1)}, bf16[4,64,384]{2,1,0:T(8,128)(2,1)S(1)}, u32[]{:S(2)}, u32[]{:S(2)}) collective-permute-start(bf16[4,64,384]{2,1,0:T(8,128)(2,1)S(1)} %get-tuple-element.49), channel_id=1, source_target_pairs={{0,48},{8,24},{16,0},{24,40},{32,16},{40,56},{48,32},{56,8},{1,49}... | collective-permute-start | bytes 589832 | tf_op jit(solution)/shard_map/ppermute | solution.py:35
  17.9 11.3 %collective-permute-start.8 = (bf16[4,64,384]{2,1,0:T(8,128)(2,1)S(1)}, bf16[4,64,384]{2,1,0:T(8,128)(2,1)S(1)}, u32[]{:S(2)}, u32[]{:S(2)}) collective-permute-start(bf16[4,64,384]{2,1,0:T(8,128)(2,1)S(1)} %get-tuple-element.45), channel_id=1, source_target_pairs={{0,128},{8,136},{64,192},{72,200},{128,0},{136,8},{192,64},{200,72... | collective-permute-start | bytes 589832 | tf_op jit(solution)/shard_map/ppermute | solution.py:35
  20.9 8.3 %collective-permute-start.7 = (bf16[4,64,384]{2,1,0:T(8,128)(2,1)S(1)}, bf16[4,64,384]{2,1,0:T(8,128)(2,1)S(1)}, u32[]{:S(2)}, u32[]{:S(2)}) collective-permute-start(bf16[4,64,384]{2,1,0:T(8,128)(2,1)S(1)} %get-tuple-element.45), channel_id=1, source_target_pairs={{0,64},{8,200},{64,128},{72,8},{128,192},{136,72},{192,0},{200,136... | collective-permute-start | bytes 589832 | tf_op jit(solution)/shard_map/ppermute | solution.py:35
  23.1 8.2 %collective-permute-start.9 = (bf16[4,64,384]{2,1,0:T(8,128)(2,1)S(1)}, bf16[4,64,384]{2,1,0:T(8,128)(2,1)S(1)}, u32[]{:S(2)}, u32[]{:S(2)}) collective-permute-start(bf16[4,64,384]{2,1,0:T(8,128)(2,1)S(1)} %get-tuple-element.45), channel_id=1, source_target_pairs={{0,192},{8,72},{64,0},{72,136},{128,64},{136,200},{192,128},{200,8... | collective-permute-start | bytes 589832 | tf_op jit(solution)/shard_map/ppermute | solution.py:35
  28.2 11.4 %collective-permute-start.4 = (bf16[4,4,64,384]{3,2,1,0:T(8,128)(2,1)S(1)}, bf16[4,4,64,384]{3,2,1,0:T(8,128)(2,1)S(1)}, u32[]{:S(2)}, u32[]{:S(2)}) collective-permute-start(bf16[4,4,64,384]{3,2,1,0:T(8,128)(2,1)S(1)} %pad_maximum_fusion.refs_2_), channel_id=1, source_target_pairs={{0,64},{8,200},{64,128},{72,8},{128,192},{136,72},{192,0},{200,136... | collective-permute-start | bytes 2359304 | tf_op jit(solution)/shard_map/ppermute | solution.py:35
  31.3 11.3 %collective-permute-start.10 = (bf16[4,4,64,384]{3,2,1,0:T(8,128)(2,1)S(1)}, bf16[4,4,64,384]{3,2,1,0:T(8,128)(2,1)S(1)}, u32[]{:S(2)}, u32[]{:S(2)}) collective-permute-start(bf16[4,4,64,384]{3,2,1,0:T(8,128)(2,1)S(1)} %pad_maximum_fusion.1.refs_6_), channel_id=1, source_target_pairs={{0,16},{8,56},{16,32},{24,8},{32,48},{40,24},{48,0},{56,40},{1,17}... | collective-permute-start | bytes 2359304 | tf_op jit(solution)/shard_map/ppermute | solution.py:35
  39.5 11.3 %collective-permute-start.5 = (bf16[4,4,64,384]{3,2,1,0:T(8,128)(2,1)S(1)}, bf16[4,4,64,384]{3,2,1,0:T(8,128)(2,1)}, u32[]{:S(2)}, u32[]{:S(2)}) collective-permute-start(bf16[4,4,64,384]{3,2,1,0:T(8,128)(2,1)S(1)} %collective-permute-done.4.refs_3_), channel_id=1, source_target_pairs={{0,64},{8,200},{64,128},{72,8},{128,192},{136,72},{192,0},{200,136... | collective-permute-start | bytes 2359304 | tf_op jit(solution)/shard_map/ppermute | solution.py:35
  42.7 11.8 %collective-permute-start.11 = (bf16[4,4,64,384]{3,2,1,0:T(8,128)(2,1)S(1)}, bf16[4,4,64,384]{3,2,1,0:T(8,128)(2,1)}, u32[]{:S(2)}, u32[]{:S(2)}) collective-permute-start(bf16[4,4,64,384]{3,2,1,0:T(8,128)(2,1)S(1)} %collective-permute-done.10.refs_7_), channel_id=1, source_target_pairs={{0,16},{8,56},{16,32},{24,8},{32,48},{40,24},{48,0},{56,40},{1,17}... | collective-permute-start | bytes 2359304 | tf_op jit(solution)/shard_map/ppermute | solution.py:35
  50.8 12.8 %collective-permute-start.6 = (bf16[4,4,64,384]{3,2,1,0:T(8,128)(2,1)}, bf16[4,4,64,384]{3,2,1,0:T(8,128)(2,1)}, u32[]{:S(2)}, u32[]{:S(2)}) collective-permute-start(bf16[4,4,64,384]{3,2,1,0:T(8,128)(2,1)} %collective-permute-done.5.refs_4_), channel_id=1, source_target_pairs={{0,64},{8,200},{64,128},{72,8},{128,192},{136,72},{192,0},{200,136... | collective-permute-start | bytes 2359304 | tf_op jit(solution)/shard_map/ppermute | solution.py:35
  54.4 12.8 %collective-permute-start.12 = (bf16[4,4,64,384]{3,2,1,0:T(8,128)(2,1)}, bf16[4,4,64,384]{3,2,1,0:T(8,128)(2,1)}, u32[]{:S(2)}, u32[]{:S(2)}) collective-permute-start(bf16[4,4,64,384]{3,2,1,0:T(8,128)(2,1)} %collective-permute-done.11.refs_8_), channel_id=1, source_target_pairs={{0,16},{8,56},{16,32},{24,8},{32,48},{40,24},{48,0},{56,40},{1,17}... | collective-permute-start | bytes 2359304 | tf_op jit(solution)/shard_map/ppermute | solution.py:35
  98.0 20.2 %collective-permute-start.14 = (bf16[4,4,64,384]{3,2,1,0:T(8,128)(2,1)S(1)}, bf16[4,4,64,384]{3,2,1,0:T(8,128)(2,1)S(1)}, u32[]{:S(2)}, u32[]{:S(2)}) collective-permute-start(bf16[4,4,64,384]{3,2,1,0:T(8,128)(2,1)S(1)} %copy-done.16), channel_id=1, source_target_pairs={{0,64},{64,128},{128,192},{192,0},{1,65},{65,129},{129,193},{193,1... | collective-permute-start | bytes 2359304 | tf_op jit(solution)/shard_map/ppermute | solution.py:40
  99.2 19.2 %collective-permute-start.16 = (bf16[4,4,64,384]{3,2,1,0:T(8,128)(2,1)S(1)}, bf16[4,4,64,384]{3,2,1,0:T(8,128)(2,1)S(1)}, u32[]{:S(2)}, u32[]{:S(2)}) collective-permute-start(bf16[4,4,64,384]{3,2,1,0:T(8,128)(2,1)S(1)} %copy-done.15), channel_id=1, source_target_pairs={{0,192},{64,0},{128,64},{192,128},{1,193},{65,1},{129,65},{193,129... | collective-permute-start | bytes 2359304 | tf_op jit(solution)/shard_map/ppermute | solution.py:40
  100.7 20.6 %collective-permute-start.22 = (bf16[4,4,64,384]{3,2,1,0:T(8,128)(2,1)S(1)}, bf16[4,4,64,384]{3,2,1,0:T(8,128)(2,1)S(1)}, u32[]{:S(2)}, u32[]{:S(2)}) collective-permute-start(bf16[4,4,64,384]{3,2,1,0:T(8,128)(2,1)S(1)} %copy-done.14), channel_id=1, source_target_pairs={{0,16},{16,32},{32,48},{48,0},{1,17},{17,33},{33,49},{49,1},{2,18}... | collective-permute-start | bytes 2359304 | tf_op jit(solution)/shard_map/ppermute | solution.py:40
  101.9 20.7 %collective-permute-start.24 = (bf16[4,4,64,384]{3,2,1,0:T(8,128)(2,1)S(1)}, bf16[4,4,64,384]{3,2,1,0:T(8,128)(2,1)S(1)}, u32[]{:S(2)}, u32[]{:S(2)}) collective-permute-start(bf16[4,4,64,384]{3,2,1,0:T(8,128)(2,1)S(1)} %copy-done.13), channel_id=1, source_target_pairs={{0,48},{16,0},{32,16},{48,32},{1,49},{17,1},{33,17},{49,33},{2,50}... | collective-permute-start | bytes 2359304 | tf_op jit(solution)/shard_map/ppermute | solution.py:40
  118.3 11.0 %collective-permute-start.15 = (bf16[2,4,64,384]{3,2,1,0:T(8,128)(2,1)S(1)}, bf16[2,4,64,384]{3,2,1,0:T(8,128)(2,1)S(1)}, u32[]{:S(2)}, u32[]{:S(2)}) collective-permute-start(bf16[2,4,64,384]{3,2,1,0:T(8,128)(2,1)S(1)} %add_convert_fusion.5), channel_id=1, source_target_pairs={{0,64},{64,128},{128,192},{192,0},{1,65},{65,129},{129,193},{193,1... | collective-permute-start | bytes 1179656 | tf_op jit(solution)/shard_map/ppermute | solution.py:40
  118.5 10.8 %collective-permute-start.18 = (bf16[2,4,64,384]{3,2,1,0:T(8,128)(2,1)S(1)}, bf16[2,4,64,384]{3,2,1,0:T(8,128)(2,1)S(1)}, u32[]{:S(2)}, u32[]{:S(2)}) collective-permute-start(bf16[2,4,64,384]{3,2,1,0:T(8,128)(2,1)S(1)} %add_convert_fusion.4), channel_id=1, source_target_pairs={{0,192},{64,0},{128,64},{192,128},{1,193},{65,1},{129,65},{193,129... | collective-permute-start | bytes 1179656 | tf_op jit(solution)/shard_map/ppermute | solution.py:40
  121.3 13.6 %collective-permute-start.23 = (bf16[2,4,64,384]{3,2,1,0:T(8,128)(2,1)S(1)}, bf16[2,4,64,384]{3,2,1,0:T(8,128)(2,1)S(1)}, u32[]{:S(2)}, u32[]{:S(2)}) collective-permute-start(bf16[2,4,64,384]{3,2,1,0:T(8,128)(2,1)S(1)} %add_convert_fusion.2), channel_id=1, source_target_pairs={{0,16},{16,32},{32,48},{48,0},{1,17},{17,33},{33,49},{49,1},{2,18}... | collective-permute-start | bytes 1179656 | tf_op jit(solution)/shard_map/ppermute | solution.py:40
  122.7 12.2 %collective-permute-start.26 = (bf16[2,4,64,384]{3,2,1,0:T(8,128)(2,1)S(1)}, bf16[2,4,64,384]{3,2,1,0:T(8,128)(2,1)S(1)}, u32[]{:S(2)}, u32[]{:S(2)}) collective-permute-start(bf16[2,4,64,384]{3,2,1,0:T(8,128)(2,1)S(1)} %add_convert_fusion.1), channel_id=1, source_target_pairs={{0,48},{16,0},{32,16},{48,32},{1,49},{17,1},{33,17},{49,33},{2,50}... | collective-permute-start | bytes 1179656 | tf_op jit(solution)/shard_map/ppermute | solution.py:40
  129.7 9.6 %collective-permute-start.17 = (bf16[4,64,384]{2,1,0:T(8,128)(2,1)S(1)}, bf16[4,64,384]{2,1,0:T(8,128)(2,1)S(1)}, u32[]{:S(2)}, u32[]{:S(2)}) collective-permute-start(bf16[4,64,384]{2,1,0:T(8,128)(2,1)S(1)} %fusion.7), channel_id=1, source_target_pairs={{0,16},{16,32},{32,48},{48,0},{1,17},{17,33},{33,49},{49,1},{2,18}... | collective-permute-start | bytes 589832 | tf_op jit(solution)/shard_map/ppermute | solution.py:40
  131.2 9.5 %collective-permute-start.19 = (bf16[4,64,384]{2,1,0:T(8,128)(2,1)S(1)}, bf16[4,64,384]{2,1,0:T(8,128)(2,1)S(1)}, u32[]{:S(2)}, u32[]{:S(2)}) collective-permute-start(bf16[4,64,384]{2,1,0:T(8,128)(2,1)S(1)} %get-tuple-element.38), channel_id=1, source_target_pairs={{0,32},{16,48},{32,0},{48,16},{1,33},{17,49},{33,1},{49,17},{2,34}... | collective-permute-start | bytes 589832 | tf_op jit(solution)/shard_map/ppermute | solution.py:40
  133.7 6.9 %collective-permute-start.20 = (bf16[4,64,384]{2,1,0:T(8,128)(2,1)S(1)}, bf16[4,64,384]{2,1,0:T(8,128)(2,1)S(1)}, u32[]{:S(2)}, u32[]{:S(2)}) collective-permute-start(bf16[4,64,384]{2,1,0:T(8,128)(2,1)S(1)} %get-tuple-element.39), channel_id=1, source_target_pairs={{0,48},{16,0},{32,16},{48,32},{1,49},{17,1},{33,17},{49,33},{2,50}... | collective-permute-start | bytes 589832 | tf_op jit(solution)/shard_map/ppermute | solution.py:40
  135.3 8.8 %collective-permute-start.25 = (bf16[4,64,384]{2,1,0:T(8,128)(2,1)S(1)}, bf16[4,64,384]{2,1,0:T(8,128)(2,1)S(1)}, u32[]{:S(2)}, u32[]{:S(2)}) collective-permute-start(bf16[4,64,384]{2,1,0:T(8,128)(2,1)S(1)} %fusion.8), channel_id=1, source_target_pairs={{0,64},{64,128},{128,192},{192,0},{1,65},{65,129},{129,193},{193,1... | collective-permute-start | bytes 589832 | tf_op jit(solution)/shard_map/ppermute | solution.py:40
  135.5 9.7 %collective-permute-start.27 = (bf16[4,64,384]{2,1,0:T(8,128)(2,1)S(1)}, bf16[4,64,384]{2,1,0:T(8,128)(2,1)S(1)}, u32[]{:S(2)}, u32[]{:S(2)}) collective-permute-start(bf16[4,64,384]{2,1,0:T(8,128)(2,1)S(1)} %get-tuple-element.36), channel_id=1, source_target_pairs={{0,128},{64,192},{128,0},{192,64},{1,129},{65,193},{129,1},{193,65... | collective-permute-start | bytes 589832 | tf_op jit(solution)/shard_map/ppermute | solution.py:40
  139.3 5.9 %collective-permute-start.28 = (bf16[4,64,384]{2,1,0:T(8,128)(2,1)S(1)}, bf16[4,64,384]{2,1,0:T(8,128)(2,1)S(1)}, u32[]{:S(2)}, u32[]{:S(2)}) collective-permute-start(bf16[4,64,384]{2,1,0:T(8,128)(2,1)S(1)} %get-tuple-element.37), channel_id=1, source_target_pairs={{0,192},{64,0},{128,64},{192,128},{1,193},{65,1},{129,65},{193,129... | collective-permute-start | bytes 589832 | tf_op jit(solution)/shard_map/ppermute | solution.py:40
  140.8 8.7 %collective-permute-start.21 = (bf16[4,32,384]{2,1,0:T(8,128)(2,1)S(1)}, bf16[4,32,384]{2,1,0:T(8,128)(2,1)S(1)}, u32[]{:S(2)}, u32[]{:S(2)}) collective-permute-start(bf16[4,32,384]{2,1,0:T(8,128)(2,1)S(1)} %select_convert_fusion.1), channel_id=1, source_target_pairs={{0,8},{8,0},{1,9},{9,1},{2,10},{10,2},{3,11},{11,3},{4,12},{12,4},... | collective-permute-start | bytes 294920 | tf_op jit(solution)/shard_map/ppermute | solution.py:29
  145.3 7.0 %collective-permute-start.29 = (bf16[4,32,384]{2,1,0:T(8,128)(2,1)S(1)}, bf16[4,32,384]{2,1,0:T(8,128)(2,1)S(1)}, u32[]{:S(2)}, u32[]{:S(2)}) collective-permute-start(bf16[4,32,384]{2,1,0:T(8,128)(2,1)S(1)} %select_convert_fusion), channel_id=1, source_target_pairs={{0,8},{8,0},{1,9},{9,1},{2,10},{10,2},{3,11},{11,3},{4,12},{12,4},... | collective-permute-start | bytes 294920 | tf_op jit(solution)/shard_map/ppermute | solution.py:29
  151.6 1.9 %collective-permute-start.13 = (bf16[128,1024]{1,0:T(8,128)(2,1)S(1)}, bf16[128,1024]{1,0:T(8,128)(2,1)S(1)}, u32[]{:S(2)}, u32[]{:S(2)}) collective-permute-start(bf16[128,1024]{1,0:T(8,128)(2,1)S(1)} %select_bitcast_fusion), channel_id=1, source_target_pairs={{0,8},{8,0},{1,9},{9,1},{2,10},{10,2},{3,11},{11,3},{4,12},{12,4},... | collective-permute-start | bytes 786440 | tf_op jit(solution)/shard_map/ppermute | solution.py:29
  (17 other events, 236.3 us)
Sparse Core Ops, SparseCore 0:
  10.7 62.5 all-gather.1
  97.0 53.4 reduce-scatter.1

commit v2 on v1

--- a/solution.py
+++ b/solution.py
@@ -59,10 +59,41 @@
     return jnp.concatenate(picks, axis=0)
 
 
+def pack_kernel(tokens, out_grad, ids, gates, out, meta, sems):
+    parts = ((tokens, 0, WIDTH), (out_grad, WIDTH, WIDTH), (meta, 2 * WIDTH, ROWS))
+    copies = [
+        pltpu.make_async_copy(part, out.at[:, pl.ds(at, n)], sems.at[i]) for i, (part, at, n) in enumerate(parts)
+    ]
+    copies[0].start()
+    copies[1].start()
+    both = jnp.concatenate([ids[...].astype(F32), gates[...].astype(F32)], axis=0).astype(BF)
+    meta[:META] = both
+    meta[META:] = jnp.zeros((ROWS - META, ROWS), BF)
+    copies[2].start()
+    for copy in copies:
+        copy.wait()
+
+
+def pack(tokens, out_grad, ids, gates):
+    return pl.pallas_call(
+        pack_kernel,
+        in_specs=[ANYWHERE, ANYWHERE, pl.BlockSpec(memory_space=pltpu.VMEM), pl.BlockSpec(memory_space=pltpu.VMEM)],
+        out_specs=ANYWHERE,
+        out_shape=jax.ShapeDtypeStruct((ROWS, 2 * WIDTH + ROWS), BF),
+        scratch_shapes=[pltpu.VMEM((ROWS, ROWS), BF), pltpu.SemaphoreType.DMA((3,))],
+        compiler_params=PARAMS,
+        cost_estimate=cost(100_000, 1_100_000),
+    )(tokens, out_grad, ids, gates)
+
+
 def layer_kernel(scale, pos, rows, *refs):
     a_in, b_in = refs[0:4], refs[4:8]
     sums, a_out, b_out = refs[8], refs[9:14], refs[14:19]
-    wg, wd, term, xg, gg, weighting, slot_grad, srow, before = refs[19:]
+    wg, wd, term, xg, gg, weighting, slot_grad, srow, before, totals, sems = refs[19:]
+    n = QROWS // ROWS
+    out_copies = [
+        pltpu.make_async_copy(totals.at[q], sums.at[pl.ds(q * n % NZ, n), q * n // NZ], sems.at[q]) for q in range(QUADS)
+    ]
     step_id = pl.program_id(0)
 
     @pl.when(step_id == 0)
@@ -99,15 +130,28 @@
 
     @pl.when(step_id >= QUADS)
     def _():
-        expert_step(scale, pos, step_id - QUADS, a_in, b_in, a_out, b_out, wg, wd, term, xg, gg, weighting, slot_grad)
+        e = step_id - QUADS
+        values = expert_step(pos, e, a_in, b_in, wg, wd, xg, gg, weighting, slot_grad)
+
+        @pl.when(e == EXPERTS_CORE - 1)
+        def _():
+            for q in range(QUADS):
+                total = dot(pick_rows(srow[q]), slot_grad[q], (0, 0)).astype(BF)
+                totals[q] = total.reshape(n, ROWS, WIDTH)
+                out_copies[q].start()
+
+        for rows_in, value, out, y_first in zip((xg, gg), values, (a_out, b_out), (True, False)):
+            term[...] = (dot(rows_in[e], value, (0, 0)) * scale).astype(BF)
+            for k in range(4):
+                for j in range(4):
+                    piece = term[pl.ds(row_of(pos, *((k, j) if y_first else (j, k))), PIECE), :]
+                    to, at = place(k, j)
+                    out[to][at, 0] = piece
 
     @pl.when(step_id == QUADS + EXPERTS_CORE - 1)
     def _():
-        n = QROWS // ROWS
-        for q in range(QUADS):
-            total = dot(pick_rows(srow[q]), slot_grad[q], (0, 0)).astype(BF)
-            z = q * n % NZ
-            sums[z : z + n, q * n // NZ] = total.reshape(n, ROWS, WIDTH)
+        for copy in out_copies:
+            copy.wait()
 
 
 def place(k, j):
@@ -120,7 +164,7 @@
     return (2, j) if j < 2 else (4, j - 2)
 
 
-def expert_step(scale, pos, e, a_in, b_in, a_out, b_out, wg, wd, term, xg, gg, weighting, slot_grad):
+def expert_step(pos, e, a_in, b_in, wg, wd, xg, gg, weighting, slot_grad):
     way = pos[4]
     for ky in range(NY):
         for kx in range(NX):
@@ -136,13 +180,7 @@
     back = dot(grad, wg[...], (1, 1)).astype(BF)
     for q in range(QUADS):
         slot_grad[q, pl.ds(pl.multiple_of(e * QSLOTS, QSLOTS), QSLOTS), :] = back[q * QSLOTS : (q + 1) * QSLOTS]
-    for rows, value, out, y_first in ((xg, grad, a_out, True), (gg, scaled, b_out, False)):
-        term[...] = (dot(rows[e], value, (0, 0)) * scale).astype(BF)
-        for k in range(4):
-            for j in range(4):
-                piece = term[pl.ds(row_of(pos, *((k, j) if y_first else (j, k))), PIECE), :]
-                to, at = place(k, j)
-                out[to][at, 0] = piece
+    return grad, scaled
 
 
 def layer(scale, pos, rows, a_in, b_in):
@@ -158,11 +196,12 @@
             grid=(QUADS + EXPERTS_CORE,),
             in_specs=[pl.BlockSpec((QROWS, rows.shape[1]), lambda i, p: (jnp.minimum(i, QUADS - 1), 0))]
             + [piece(4)] * 8,
-            out_specs=[pl.BlockSpec(by_z, lambda i, p: (0, 0, 0, 0))] + [piece(n) for n in PARTS * 2],
+            out_specs=[ANYWHERE] + [piece(n) for n in PARTS * 2],
             scratch_shapes=[pltpu.VMEM((WIDTH, HID), BF)] * 3
             + [slots(WIDTH, BF), slots(WIDTH, BF), slots(128, F32)]
             + [pltpu.VMEM((QUADS, EXPERTS_CORE * QSLOTS, WIDTH), BF), pltpu.VMEM((QUADS, 8, QROWS), F32)]
-            + [pltpu.VMEM((QROWS, QROWS), BF)],
+            + [pltpu.VMEM((QROWS, QROWS), BF), pltpu.VMEM((QUADS, QROWS // ROWS, ROWS, WIDTH), BF)]
+            + [pltpu.SemaphoreType.DMA((QUADS,))],
         ),
         out_shape=[jax.ShapeDtypeStruct(by_z, BF)] + [grads(n) for n in PARTS * 2],
         compiler_params=PARAMS,
@@ -195,9 +234,8 @@
     scale = 1.0 / math.sqrt(NY * NX * NC * NZ * ROWS * 8 / 64)
     y, x, c, z = (lax.axis_index(a) for a in ("y", "x", "c", "z"))
     pos = jnp.stack([y, x, c, (z * NC + c) * EXPERTS_CORE, 1 - 2 * c]).astype(jnp.int32)
-    meta = jnp.concatenate([expert_ids.T.astype(BF), gate_values.T], axis=0)
-    meta = jnp.pad(meta, ((0, ROWS - META), (0, 0)))
-    rows = lax.all_gather(jnp.concatenate([tokens, out_grad, meta], axis=1), ("c", "z"), axis=0, tiled=True)
+    packed = pack(tokens, out_grad, expert_ids.T, gate_values.T)
+    rows = lax.all_gather(packed, ("c", "z"), axis=0, tiled=True)
 
     def by_core(own, sister):
         return jnp.where(c == 0, own, sister), jnp.where(c == 0, sister, own)
@@ -213,8 +251,9 @@
     a_in = gather_plane(own_a, "x", "y")
     b_in = gather_plane(own_b, "y", "x")
     sums, a_out, b_out = layer(scale, pos, rows, a_in, b_in)
-    keep, send = by_core(*lax.psum_scatter(sums, "z", scatter_dimension=0))
-    input_grad = (keep.astype(F32) + swap(send).astype(F32)).astype(BF)
+    part = lax.psum_scatter(sums, "z", scatter_dimension=0)
+    got = swap(part)
+    input_grad = jnp.where(c == 0, part[0].astype(F32) + got[0].astype(F32), part[1].astype(F32) + got[1].astype(F32)).astype(BF)
 
     def placed(total):
         n = gate_weight.shape[0]

time: 161 us -> 178 us (1.11)
  Pallas kernels: 23.5 us -> 40.6 us
  waiting for transfers between devices: 59.4 us -> 54.8 us
  starting transfers between devices: 52.9 us -> 55.1 us
    pallas_call x0 -> x1, Pallas kernels: none -> 17.7 us  [pack(): pl.pallas_call(pack_kernel, in_specs=[ANYWHERE, ANYWHERE, pl.BlockSpec(me...]
    ppermute x14, waiting for transfers between devices: 22.4 us -> 19.2 us  [shift(): return lax.ppermute(value, axis, [(i, (i + by) % n) for i in range(n)])]
    concatenate x2 -> x0, other arithmetic: 2.56 us -> none  [the longest x1 1.87 us: shards(): jnp.concatenate([tokens, out_grad, meta], axis=1)]
    ppermute x14, starting transfers between devices: 20.1 us -> 22.3 us  [shift(): return lax.ppermute(value, axis, [(i, (i + by) % n) for i in range(n)])]
    convert_element_type x2, other arithmetic: 0.21 us -> 2.22 us  [scatter_plane(): next_down = shift((f32(next_down) + f32(down[n:])).astype(BF), second, -1)]
    convert_element_type x2, other arithmetic: 0.21 us -> 2.22 us  [scatter_plane(): next_up = shift((f32(next_up) + f32(up[n:])).astype(BF), second, 1)]
    all_gather x1, waiting for transfers between devices: 6.16 us -> 4.34 us  [shards(): rows = lax.all_gather(packed, ('c', 'z'), axis=0, tiled=True)]
    unnamed x38 -> x16, local copies, waits for them, and re-layouts: 3.12 us -> 3.89 us
  transfers between devices with their start and end apart: 32 -> 32, of which waited for: 17 -> 18; matrix products, arithmetic and copies ran while one was open for 4% -> 6% of each run, Pallas kernels for 0% -> 0%
where the time goes in v2:
time: 178 us; the launch traced here: 177 us
  starting transfers between devices  55.1 us (31%)
  waiting for transfers between devices  54.8 us (31%)
  Pallas kernels  40.6 us (23%)
  between operations  14.3 us (8%)
  other arithmetic  7.75 us (4%)
  local copies, waits for them, and re-layouts  4.63 us (3%)
    ppermute x12, waiting for transfers between devices, step(): return lax.ppermute(value, (axis, 'c'), pairs)  29.7 us
    pallas_call x1, Pallas kernels, layer(): pl.pallas_call(lambda *refs: layer_kernel(scale, *refs), grid_spec=pltpu....  22.9 us
    ppermute x14, starting transfers between devices, shift(): return lax.ppermute(value, axis, [(i, (i + by) % n) for i in range(n)])  22.3 us
    ppermute x12, starting transfers between devices, step(): return lax.ppermute(value, (axis, 'c'), pairs)  21.3 us
    ppermute x14, waiting for transfers between devices, shift(): return lax.ppermute(value, axis, [(i, (i + by) % n) for i in range(n)])  19.2 us
    pallas_call x1, Pallas kernels, pack(): pl.pallas_call(pack_kernel, in_specs=[ANYWHERE, ANYWHERE, pl.BlockSpec(me...  17.7 us
    ppermute x4, starting transfers between devices, swap(): return lax.ppermute(value, 'c', [(0, 1), (1, 0)])  11.5 us
    all_gather x1, waiting for transfers between devices, shards(): rows = lax.all_gather(packed, ('c', 'z'), axis=0, tiled=True)  4.34 us
  transfers between devices with their start and end apart: 32, of which 18 were waited for; matrix products, arithmetic and copies ran while one was open for 6% of the time, Pallas kernels for 0%

profile of v2, /device:TPU:1, one launch (start us, length us, event | category | flops | bytes accessed | tf_op | source)
XLA Modules:
  0.0 177.2 jit_solution(8845035000802950485)
XLA Ops:
  7.2 17.7 %shard_map.85 = bf16[128,2176]{1,0:T(8,128)(2,1)} custom-call(bf16[128,1024]{1,0:T(8,128)(2,1)} %tokens.1, bf16[128,1024]{1,0:T(8,128)(2,1)} %out_grad.1, s32[8,128]{1,0:T(8,128)} %bitcast.103, bf16[8,128]{1,0:T(8,128)(2,1)} %bitcast.104), custom_call_target="tpu_custom_call" | custom-call | flops 100000 | bytes 1100000 | tf_op jit(solution)/shard_map/pallas_call | solution.py:78
  27.0 3.3 %collective-permute-start = (bf16[2,4,32,384]{3,2,1,0:T(8,128)(2,1)S(1)}, bf16[2,4,32,384]{3,2,1,0:T(8,128)(2,1)S(1)}, u32[]{:S(2)}, u32[]{:S(2)}) collective-permute-start(bf16[2,4,32,384]{3,2,1,0:T(8,128)(2,1)S(1)} %pad_maximum_fusion.2), channel_id=1, source_target_pairs={{0,8},{8,0},{1,9},{9,1},{2,10},{10,2},{3,11},{11,3},{4,12},{12,4},... | collective-permute-start | bytes 589832 | tf_op jit(solution)/shard_map/ppermute | solution.py:29
  34.1 3.0 %collective-permute-start.8 = (bf16[4,64,384]{2,1,0:T(8,128)(2,1)S(1)}, bf16[4,64,384]{2,1,0:T(8,128)(2,1)S(1)}, u32[]{:S(2)}, u32[]{:S(2)}) collective-permute-start(bf16[4,64,384]{2,1,0:T(8,128)(2,1)S(1)} %get-tuple-element.45), channel_id=1, source_target_pairs={{0,128},{8,136},{64,192},{72,200},{128,0},{136,8},{192,64},{200,72... | collective-permute-start | bytes 589832 | tf_op jit(solution)/shard_map/ppermute | solution.py:35
  37.9 1.4 collective-permute-done.2
  39.2 2.6 %collective-permute-done.1 = bf16[4,64,384]{2,1,0:T(8,128)(2,1)S(1)} collective-permute-done((bf16[4,64,384]{2,1,0:T(8,128)(2,1)S(1)}, bf16[4,64,384]{2,1,0:T(8,128)(2,1)S(1)}, u32[]{:S(2)}, u32[]{:S(2)}) %collective-permute-start.1) | collective-permute-done | bytes 196640 | tf_op jit(solution)/shard_map/ppermute | solution.py:35
  41.8 2.4 %collective-permute-done.3 = bf16[4,64,384]{2,1,0:T(8,128)(2,1)S(1)} collective-permute-done((bf16[4,64,384]{2,1,0:T(8,128)(2,1)S(1)}, bf16[4,64,384]{2,1,0:T(8,128)(2,1)S(1)}, u32[]{:S(2)}, u32[]{:S(2)}) %collective-permute-start.3) | collective-permute-done | bytes 196640 | tf_op jit(solution)/shard_map/ppermute | solution.py:35
  45.4 2.0 %collective-permute-done.9 = bf16[4,64,384]{2,1,0:T(8,128)(2,1)S(1)} collective-permute-done((bf16[4,64,384]{2,1,0:T(8,128)(2,1)S(1)}, bf16[4,64,384]{2,1,0:T(8,128)(2,1)S(1)}, u32[]{:S(2)}, u32[]{:S(2)}) %collective-permute-start.9) | collective-permute-done | bytes 196640 | tf_op jit(solution)/shard_map/ppermute | solution.py:35
  47.5 1.7 collective-permute-start.10
  49.2 6.5 %collective-permute-done.4.refs_3_ = bf16[4,4,64,384]{3,2,1,0:T(8,128)(2,1)S(1)} collective-permute-done((bf16[4,4,64,384]{3,2,1,0:T(8,128)(2,1)S(1)}, bf16[4,4,64,384]{3,2,1,0:T(8,128)(2,1)S(1)}, u32[]{:S(2)}, u32[]{:S(2)}) %collective-permute-start.4) | collective-permute-done | bytes 786464 | tf_op jit(solution)/shard_map/ppermute | solution.py:35
  55.7 2.4 %collective-permute-start.5 = (bf16[4,4,64,384]{3,2,1,0:T(8,128)(2,1)S(1)}, bf16[4,4,64,384]{3,2,1,0:T(8,128)(2,1)}, u32[]{:S(2)}, u32[]{:S(2)}) collective-permute-start(bf16[4,4,64,384]{3,2,1,0:T(8,128)(2,1)S(1)} %collective-permute-done.4.refs_3_), channel_id=1, source_target_pairs={{0,64},{8,200},{64,128},{72,8},{128,192},{136,72},{192,0},{200,136... | collective-permute-start | bytes 2359304 | tf_op jit(solution)/shard_map/ppermute | solution.py:35
  58.8 2.8 %collective-permute-start.11 = (bf16[4,4,64,384]{3,2,1,0:T(8,128)(2,1)S(1)}, bf16[4,4,64,384]{3,2,1,0:T(8,128)(2,1)}, u32[]{:S(2)}, u32[]{:S(2)}) collective-permute-start(bf16[4,4,64,384]{3,2,1,0:T(8,128)(2,1)S(1)} %collective-permute-done.10.refs_7_), channel_id=1, source_target_pairs={{0,16},{8,56},{16,32},{24,8},{32,48},{40,24},{48,0},{56,40},{1,17}... | collective-permute-start | bytes 2359304 | tf_op jit(solution)/shard_map/ppermute | solution.py:35
  61.7 5.4 %collective-permute-done.5.refs_4_ = bf16[4,4,64,384]{3,2,1,0:T(8,128)(2,1)} collective-permute-done((bf16[4,4,64,384]{3,2,1,0:T(8,128)(2,1)S(1)}, bf16[4,4,64,384]{3,2,1,0:T(8,128)(2,1)}, u32[]{:S(2)}, u32[]{:S(2)}) %collective-permute-start.5) | collective-permute-done | bytes 786464 | tf_op jit(solution)/shard_map/ppermute | solution.py:35
  67.0 3.5 %collective-permute-start.6 = (bf16[4,4,64,384]{3,2,1,0:T(8,128)(2,1)}, bf16[4,4,64,384]{3,2,1,0:T(8,128)(2,1)}, u32[]{:S(2)}, u32[]{:S(2)}) collective-permute-start(bf16[4,4,64,384]{3,2,1,0:T(8,128)(2,1)} %collective-permute-done.5.refs_4_), channel_id=1, source_target_pairs={{0,64},{8,200},{64,128},{72,8},{128,192},{136,72},{192,0},{200,136... | collective-permute-start | bytes 2359304 | tf_op jit(solution)/shard_map/ppermute | solution.py:35
  70.6 3.5 %collective-permute-start.12 = (bf16[4,4,64,384]{3,2,1,0:T(8,128)(2,1)}, bf16[4,4,64,384]{3,2,1,0:T(8,128)(2,1)}, u32[]{:S(2)}, u32[]{:S(2)}) collective-permute-start(bf16[4,4,64,384]{3,2,1,0:T(8,128)(2,1)} %collective-permute-done.11.refs_8_), channel_id=1, source_target_pairs={{0,16},{8,56},{16,32},{24,8},{32,48},{40,24},{48,0},{56,40},{1,17}... | collective-permute-start | bytes 2359304 | tf_op jit(solution)/shard_map/ppermute | solution.py:35
  74.7 5.1 %collective-permute-done.6.refs_5_ = bf16[4,4,64,384]{3,2,1,0:T(8,128)(2,1)} collective-permute-done((bf16[4,4,64,384]{3,2,1,0:T(8,128)(2,1)}, bf16[4,4,64,384]{3,2,1,0:T(8,128)(2,1)}, u32[]{:S(2)}, u32[]{:S(2)}) %collective-permute-start.6) | collective-permute-done | bytes 786464 | tf_op jit(solution)/shard_map/ppermute | solution.py:35
  79.8 3.6 %collective-permute-done.12.refs_9_ = bf16[4,4,64,384]{3,2,1,0:T(8,128)(2,1)} collective-permute-done((bf16[4,4,64,384]{3,2,1,0:T(8,128)(2,1)}, bf16[4,4,64,384]{3,2,1,0:T(8,128)(2,1)}, u32[]{:S(2)}, u32[]{:S(2)}) %collective-permute-start.12) | collective-permute-done | bytes 786464 | tf_op jit(solution)/shard_map/ppermute | solution.py:35
  83.4 4.3 %all-gather.2.cloned.1.call-done.refs_1_ = bf16[2048,2176]{1,0:T(8,128)(2,1)} async-done(((bf16[128,2176]{1,0:T(8,128)(2,1)}), bf16[2048,2176]{1,0:T(8,128)(2,1)}) %all-gather.2.cloned.1.call-update) | async-done | bytes 8912912 | tf_op jit(solution)/shard_map/all_gather | solution.py:238
  87.7 22.9 %shard_map.86 = (bf16[8,2,128,1024]{3,2,1,0:T(8,128)(2,1)}, bf16[4,4,64,384]{3,2,1,0:T(8,128)(2,1)}, bf16[4,4,64,384]{3,2,1,0:T(8,128)(2,1)}, bf16[4,4,64,384]{3...) custom-call(s32[5]{0:T(128)} %stack.62.refs_0_, ...), custom_call_target="tpu_custom_call" | custom-call | flops 12999999488 | bytes 26000000 | tf_op jit(solution)/shard_map/pallas_call | solution.py:192
  110.7 1.3 collective-permute-start.14
  111.9 1.5 collective-permute-start.16
  114.6 1.5 collective-permute-start.24
  116.1 14.5 %collective-permute-done.14 = bf16[4,4,64,384]{3,2,1,0:T(8,128)(2,1)S(1)} collective-permute-done((bf16[4,4,64,384]{3,2,1,0:T(8,128)(2,1)}, bf16[4,4,64,384]{3,2,1,0:T(8,128)(2,1)S(1)}, u32[]{:S(2)}, u32[]{:S(2)}) %collective-permute-start.14) | collective-permute-done | bytes 786464 | tf_op jit(solution)/shard_map/ppermute | solution.py:40
  132.9 2.7 %collective-permute-start.18 = (bf16[2,4,64,384]{3,2,1,0:T(8,128)(2,1)S(1)}, bf16[2,4,64,384]{3,2,1,0:T(8,128)(2,1)S(1)}, u32[]{:S(2)}, u32[]{:S(2)}) collective-permute-start(bf16[2,4,64,384]{3,2,1,0:T(8,128)(2,1)S(1)} %add_convert_fusion.4), channel_id=1, source_target_pairs={{0,192},{64,0},{128,64},{192,128},{1,193},{65,1},{129,65},{193,129... | collective-permute-start | bytes 1179656 | tf_op jit(solution)/shard_map/ppermute | solution.py:40
  136.7 1.8 %collective-permute-start.23 = (bf16[2,4,64,384]{3,2,1,0:T(8,128)(2,1)S(1)}, bf16[2,4,64,384]{3,2,1,0:T(8,128)(2,1)S(1)}, u32[]{:S(2)}, u32[]{:S(2)}) collective-permute-start(bf16[2,4,64,384]{3,2,1,0:T(8,128)(2,1)S(1)} %add_convert_fusion.2), channel_id=1, source_target_pairs={{0,16},{16,32},{32,48},{48,0},{1,17},{17,33},{33,49},{49,1},{2,18}... | collective-permute-start | bytes 1179656 | tf_op jit(solution)/shard_map/ppermute | solution.py:40
  139.7 1.3 collective-permute-start.26
  142.9 2.3 %collective-permute-start.17 = (bf16[4,64,384]{2,1,0:T(8,128)(2,1)S(1)}, bf16[4,64,384]{2,1,0:T(8,128)(2,1)S(1)}, u32[]{:S(2)}, u32[]{:S(2)}) collective-permute-start(bf16[4,64,384]{2,1,0:T(8,128)(2,1)S(1)} %fusion.8), channel_id=1, source_target_pairs={{0,16},{16,32},{32,48},{48,0},{1,17},{17,33},{33,49},{49,1},{2,18}... | collective-permute-start | bytes 589832 | tf_op jit(solution)/shard_map/ppermute | solution.py:40
  145.2 2.5 %collective-permute-start.19 = (bf16[4,64,384]{2,1,0:T(8,128)(2,1)S(1)}, bf16[4,64,384]{2,1,0:T(8,128)(2,1)S(1)}, u32[]{:S(2)}, u32[]{:S(2)}) collective-permute-start(bf16[4,64,384]{2,1,0:T(8,128)(2,1)S(1)} %get-tuple-element.38), channel_id=1, source_target_pairs={{0,32},{16,48},{32,0},{48,16},{1,33},{17,49},{33,1},{49,17},{2,34}... | collective-permute-start | bytes 589832 | tf_op jit(solution)/shard_map/ppermute | solution.py:40
  150.3 4.0 %collective-permute-start.27 = (bf16[4,64,384]{2,1,0:T(8,128)(2,1)S(1)}, bf16[4,64,384]{2,1,0:T(8,128)(2,1)S(1)}, u32[]{:S(2)}, u32[]{:S(2)}) collective-permute-start(bf16[4,64,384]{2,1,0:T(8,128)(2,1)S(1)} %get-tuple-element.36), channel_id=1, source_target_pairs={{0,128},{64,192},{128,0},{192,64},{1,129},{65,193},{129,1},{193,65... | collective-permute-start | bytes 589832 | tf_op jit(solution)/shard_map/ppermute | solution.py:40
  154.2 3.1 %collective-permute-done.19 = bf16[4,64,384]{2,1,0:T(8,128)(2,1)S(1)} collective-permute-done((bf16[4,64,384]{2,1,0:T(8,128)(2,1)S(1)}, bf16[4,64,384]{2,1,0:T(8,128)(2,1)S(1)}, u32[]{:S(2)}, u32[]{:S(2)}) %collective-permute-start.19) | collective-permute-done | bytes 196640 | tf_op jit(solution)/shard_map/ppermute | solution.py:40
  157.4 2.5 %collective-permute-start.21 = (bf16[4,32,384]{2,1,0:T(8,128)(2,1)S(1)}, bf16[4,32,384]{2,1,0:T(8,128)(2,1)S(1)}, u32[]{:S(2)}, u32[]{:S(2)}) collective-permute-start(bf16[4,32,384]{2,1,0:T(8,128)(2,1)S(1)} %select_convert_fusion.1), channel_id=1, source_target_pairs={{0,8},{8,0},{1,9},{9,1},{2,10},{10,2},{3,11},{11,3},{4,12},{12,4},... | collective-permute-start | bytes 294920 | tf_op jit(solution)/shard_map/ppermute | solution.py:29
  160.2 5.0 %collective-permute-start.29 = (bf16[4,32,384]{2,1,0:T(8,128)(2,1)S(1)}, bf16[4,32,384]{2,1,0:T(8,128)(2,1)S(1)}, u32[]{:S(2)}, u32[]{:S(2)}) collective-permute-start(bf16[4,32,384]{2,1,0:T(8,128)(2,1)S(1)} %select_convert_fusion), channel_id=1, source_target_pairs={{0,8},{8,0},{1,9},{9,1},{2,10},{10,2},{3,11},{11,3},{4,12},{12,4},... | collective-permute-start | bytes 294920 | tf_op jit(solution)/shard_map/ppermute | solution.py:29
  168.5 1.9 %fusion.1 = bf16[128,1024]{1,0:T(8,128)(2,1)} fusion(bf16[2,128,1024]{2,1,0:T(8,128)(2,1)S(1)} %collective-permute-done.13, bf16[1,2,128,1024]{3,2,1,0:T(8,128)(2,1)} %reduce-scatter.2.cloned.1.call-done, pred[]{:T(512)S(6)} %eq.2), kind=kLoop, calls=%fused_computation.12 | loop fusion | flops 1048576 | bytes 1310721 | tf_op jit(solution)/shard_map/convert_element_type | solution.py:256
  (79 shorter events, 23.0 us)
Async XLA Ops:
  7.2 80.5 %all-gather.2.cloned.1.call-start = ((), (), s32[]{:S(2)}) async-start(), calls=%async_computation.1 | async-start | bytes 9469952 | tf_op jit(solution)/shard_map/all_gather | solution.py:238
  25.0 140.8 %reduce-scatter.2.cloned.1.call-start = ((), (), s32[]{:S(2)}) async-start(), calls=%async_computation.2 | async-start | bytes 4718592 | tf_op jit(solution)/shard_map/reduce_scatter | solution.py:254
  27.0 4.4 %collective-permute-start = (bf16[2,4,32,384]{3,2,1,0:T(8,128)(2,1)S(1)}, bf16[2,4,32,384]{3,2,1,0:T(8,128)(2,1)S(1)}, u32[]{:S(2)}, u32[]{:S(2)}) collective-permute-start(bf16[2,4,32,384]{3,2,1,0:T(8,128)(2,1)S(1)} %pad_maximum_fusion.2), channel_id=1, source_target_pairs={{0,8},{8,0},{1,9},{9,1},{2,10},{10,2},{3,11},{11,3},{4,12},{12,4},... | collective-permute-start | bytes 589832 | tf_op jit(solution)/shard_map/ppermute | solution.py:29
  31.5 7.7 %collective-permute-start.2 = (bf16[4,64,384]{2,1,0:T(8,128)(2,1)S(1)}, bf16[4,64,384]{2,1,0:T(8,128)(2,1)S(1)}, u32[]{:S(2)}, u32[]{:S(2)}) collective-permute-start(bf16[4,64,384]{2,1,0:T(8,128)(2,1)S(1)} %get-tuple-element.49), channel_id=1, source_target_pairs={{0,32},{8,40},{16,48},{24,56},{32,0},{40,8},{48,16},{56,24},{1,33}... | collective-permute-start | bytes 589832 | tf_op jit(solution)/shard_map/ppermute | solution.py:35
  32.6 9.2 %collective-permute-start.1 = (bf16[4,64,384]{2,1,0:T(8,128)(2,1)S(1)}, bf16[4,64,384]{2,1,0:T(8,128)(2,1)S(1)}, u32[]{:S(2)}, u32[]{:S(2)}) collective-permute-start(bf16[4,64,384]{2,1,0:T(8,128)(2,1)S(1)} %get-tuple-element.49), channel_id=1, source_target_pairs={{0,16},{8,56},{16,32},{24,8},{32,48},{40,24},{48,0},{56,40},{1,17}... | collective-permute-start | bytes 589832 | tf_op jit(solution)/shard_map/ppermute | solution.py:35
  33.4 10.7 %collective-permute-start.3 = (bf16[4,64,384]{2,1,0:T(8,128)(2,1)S(1)}, bf16[4,64,384]{2,1,0:T(8,128)(2,1)S(1)}, u32[]{:S(2)}, u32[]{:S(2)}) collective-permute-start(bf16[4,64,384]{2,1,0:T(8,128)(2,1)S(1)} %get-tuple-element.49), channel_id=1, source_target_pairs={{0,48},{8,24},{16,0},{24,40},{32,16},{40,56},{48,32},{56,8},{1,49}... | collective-permute-start | bytes 589832 | tf_op jit(solution)/shard_map/ppermute | solution.py:35
  34.1 11.3 %collective-permute-start.8 = (bf16[4,64,384]{2,1,0:T(8,128)(2,1)S(1)}, bf16[4,64,384]{2,1,0:T(8,128)(2,1)S(1)}, u32[]{:S(2)}, u32[]{:S(2)}) collective-permute-start(bf16[4,64,384]{2,1,0:T(8,128)(2,1)S(1)} %get-tuple-element.45), channel_id=1, source_target_pairs={{0,128},{8,136},{64,192},{72,200},{128,0},{136,8},{192,64},{200,72... | collective-permute-start | bytes 589832 | tf_op jit(solution)/shard_map/ppermute | solution.py:35
  37.1 8.3 %collective-permute-start.7 = (bf16[4,64,384]{2,1,0:T(8,128)(2,1)S(1)}, bf16[4,64,384]{2,1,0:T(8,128)(2,1)S(1)}, u32[]{:S(2)}, u32[]{:S(2)}) collective-permute-start(bf16[4,64,384]{2,1,0:T(8,128)(2,1)S(1)} %get-tuple-element.45), channel_id=1, source_target_pairs={{0,64},{8,200},{64,128},{72,8},{128,192},{136,72},{192,0},{200,136... | collective-permute-start | bytes 589832 | tf_op jit(solution)/shard_map/ppermute | solution.py:35
  39.2 8.2 %collective-permute-start.9 = (bf16[4,64,384]{2,1,0:T(8,128)(2,1)S(1)}, bf16[4,64,384]{2,1,0:T(8,128)(2,1)S(1)}, u32[]{:S(2)}, u32[]{:S(2)}) collective-permute-start(bf16[4,64,384]{2,1,0:T(8,128)(2,1)S(1)} %get-tuple-element.45), channel_id=1, source_target_pairs={{0,192},{8,72},{64,0},{72,136},{128,64},{136,200},{192,128},{200,8... | collective-permute-start | bytes 589832 | tf_op jit(solution)/shard_map/ppermute | solution.py:35
  44.3 11.4 %collective-permute-start.4 = (bf16[4,4,64,384]{3,2,1,0:T(8,128)(2,1)S(1)}, bf16[4,4,64,384]{3,2,1,0:T(8,128)(2,1)S(1)}, u32[]{:S(2)}, u32[]{:S(2)}) collective-permute-start(bf16[4,4,64,384]{3,2,1,0:T(8,128)(2,1)S(1)} %pad_maximum_fusion.refs_2_), channel_id=1, source_target_pairs={{0,64},{8,200},{64,128},{72,8},{128,192},{136,72},{192,0},{200,136... | collective-permute-start | bytes 2359304 | tf_op jit(solution)/shard_map/ppermute | solution.py:35
  47.5 11.3 %collective-permute-start.10 = (bf16[4,4,64,384]{3,2,1,0:T(8,128)(2,1)S(1)}, bf16[4,4,64,384]{3,2,1,0:T(8,128)(2,1)S(1)}, u32[]{:S(2)}, u32[]{:S(2)}) collective-permute-start(bf16[4,4,64,384]{3,2,1,0:T(8,128)(2,1)S(1)} %pad_maximum_fusion.1.refs_6_), channel_id=1, source_target_pairs={{0,16},{8,56},{16,32},{24,8},{32,48},{40,24},{48,0},{56,40},{1,17}... | collective-permute-start | bytes 2359304 | tf_op jit(solution)/shard_map/ppermute | solution.py:35
  55.7 11.3 %collective-permute-start.5 = (bf16[4,4,64,384]{3,2,1,0:T(8,128)(2,1)S(1)}, bf16[4,4,64,384]{3,2,1,0:T(8,128)(2,1)}, u32[]{:S(2)}, u32[]{:S(2)}) collective-permute-start(bf16[4,4,64,384]{3,2,1,0:T(8,128)(2,1)S(1)} %collective-permute-done.4.refs_3_), channel_id=1, source_target_pairs={{0,64},{8,200},{64,128},{72,8},{128,192},{136,72},{192,0},{200,136... | collective-permute-start | bytes 2359304 | tf_op jit(solution)/shard_map/ppermute | solution.py:35
  58.8 11.8 %collective-permute-start.11 = (bf16[4,4,64,384]{3,2,1,0:T(8,128)(2,1)S(1)}, bf16[4,4,64,384]{3,2,1,0:T(8,128)(2,1)}, u32[]{:S(2)}, u32[]{:S(2)}) collective-permute-start(bf16[4,4,64,384]{3,2,1,0:T(8,128)(2,1)S(1)} %collective-permute-done.10.refs_7_), channel_id=1, source_target_pairs={{0,16},{8,56},{16,32},{24,8},{32,48},{40,24},{48,0},{56,40},{1,17}... | collective-permute-start | bytes 2359304 | tf_op jit(solution)/shard_map/ppermute | solution.py:35
  67.0 12.8 %collective-permute-start.6 = (bf16[4,4,64,384]{3,2,1,0:T(8,128)(2,1)}, bf16[4,4,64,384]{3,2,1,0:T(8,128)(2,1)}, u32[]{:S(2)}, u32[]{:S(2)}) collective-permute-start(bf16[4,4,64,384]{3,2,1,0:T(8,128)(2,1)} %collective-permute-done.5.refs_4_), channel_id=1, source_target_pairs={{0,64},{8,200},{64,128},{72,8},{128,192},{136,72},{192,0},{200,136... | collective-permute-start | bytes 2359304 | tf_op jit(solution)/shard_map/ppermute | solution.py:35
  70.6 12.8 %collective-permute-start.12 = (bf16[4,4,64,384]{3,2,1,0:T(8,128)(2,1)}, bf16[4,4,64,384]{3,2,1,0:T(8,128)(2,1)}, u32[]{:S(2)}, u32[]{:S(2)}) collective-permute-start(bf16[4,4,64,384]{3,2,1,0:T(8,128)(2,1)} %collective-permute-done.11.refs_8_), channel_id=1, source_target_pairs={{0,16},{8,56},{16,32},{24,8},{32,48},{40,24},{48,0},{56,40},{1,17}... | collective-permute-start | bytes 2359304 | tf_op jit(solution)/shard_map/ppermute | solution.py:35
  110.7 19.9 %collective-permute-start.14 = (bf16[4,4,64,384]{3,2,1,0:T(8,128)(2,1)}, bf16[4,4,64,384]{3,2,1,0:T(8,128)(2,1)S(1)}, u32[]{:S(2)}, u32[]{:S(2)}) collective-permute-start(bf16[4,4,64,384]{3,2,1,0:T(8,128)(2,1)} %get-tuple-element.17), channel_id=1, source_target_pairs={{0,64},{64,128},{128,192},{192,0},{1,65},{65,129},{129,193},{193,1... | collective-permute-start | bytes 2359304 | tf_op jit(solution)/shard_map/ppermute | solution.py:40
  111.9 19.8 %collective-permute-start.16 = (bf16[4,4,64,384]{3,2,1,0:T(8,128)(2,1)}, bf16[4,4,64,384]{3,2,1,0:T(8,128)(2,1)S(1)}, u32[]{:S(2)}, u32[]{:S(2)}) collective-permute-start(bf16[4,4,64,384]{3,2,1,0:T(8,128)(2,1)} %get-tuple-element.18), channel_id=1, source_target_pairs={{0,192},{64,0},{128,64},{192,128},{1,193},{65,1},{129,65},{193,129... | collective-permute-start | bytes 2359304 | tf_op jit(solution)/shard_map/ppermute | solution.py:40
  113.4 22.2 %collective-permute-start.22 = (bf16[4,4,64,384]{3,2,1,0:T(8,128)(2,1)}, bf16[4,4,64,384]{3,2,1,0:T(8,128)(2,1)S(1)}, u32[]{:S(2)}, u32[]{:S(2)}) collective-permute-start(bf16[4,4,64,384]{3,2,1,0:T(8,128)(2,1)} %get-tuple-element.22), channel_id=1, source_target_pairs={{0,16},{16,32},{32,48},{48,0},{1,17},{17,33},{33,49},{49,1},{2,18}... | collective-permute-start | bytes 2359304 | tf_op jit(solution)/shard_map/ppermute | solution.py:40
  114.6 24.0 %collective-permute-start.24 = (bf16[4,4,64,384]{3,2,1,0:T(8,128)(2,1)}, bf16[4,4,64,384]{3,2,1,0:T(8,128)(2,1)S(1)}, u32[]{:S(2)}, u32[]{:S(2)}) collective-permute-start(bf16[4,4,64,384]{3,2,1,0:T(8,128)(2,1)} %get-tuple-element.23), channel_id=1, source_target_pairs={{0,48},{16,0},{32,16},{48,32},{1,49},{17,1},{33,17},{49,33},{2,50}... | collective-permute-start | bytes 2359304 | tf_op jit(solution)/shard_map/ppermute | solution.py:40
  131.7 10.4 %collective-permute-start.15 = (bf16[2,4,64,384]{3,2,1,0:T(8,128)(2,1)S(1)}, bf16[2,4,64,384]{3,2,1,0:T(8,128)(2,1)S(1)}, u32[]{:S(2)}, u32[]{:S(2)}) collective-permute-start(bf16[2,4,64,384]{3,2,1,0:T(8,128)(2,1)S(1)} %add_convert_fusion.5), channel_id=1, source_target_pairs={{0,64},{64,128},{128,192},{192,0},{1,65},{65,129},{129,193},{193,1... | collective-permute-start | bytes 1179656 | tf_op jit(solution)/shard_map/ppermute | solution.py:40
  132.9 9.6 %collective-permute-start.18 = (bf16[2,4,64,384]{3,2,1,0:T(8,128)(2,1)S(1)}, bf16[2,4,64,384]{3,2,1,0:T(8,128)(2,1)S(1)}, u32[]{:S(2)}, u32[]{:S(2)}) collective-permute-start(bf16[2,4,64,384]{3,2,1,0:T(8,128)(2,1)S(1)} %add_convert_fusion.4), channel_id=1, source_target_pairs={{0,192},{64,0},{128,64},{192,128},{1,193},{65,1},{129,65},{193,129... | collective-permute-start | bytes 1179656 | tf_op jit(solution)/shard_map/ppermute | solution.py:40
  136.7 12.2 %collective-permute-start.23 = (bf16[2,4,64,384]{3,2,1,0:T(8,128)(2,1)S(1)}, bf16[2,4,64,384]{3,2,1,0:T(8,128)(2,1)S(1)}, u32[]{:S(2)}, u32[]{:S(2)}) collective-permute-start(bf16[2,4,64,384]{3,2,1,0:T(8,128)(2,1)S(1)} %add_convert_fusion.2), channel_id=1, source_target_pairs={{0,16},{16,32},{32,48},{48,0},{1,17},{17,33},{33,49},{49,1},{2,18}... | collective-permute-start | bytes 1179656 | tf_op jit(solution)/shard_map/ppermute | solution.py:40
  139.7 9.3 %collective-permute-start.26 = (bf16[2,4,64,384]{3,2,1,0:T(8,128)(2,1)S(1)}, bf16[2,4,64,384]{3,2,1,0:T(8,128)(2,1)S(1)}, u32[]{:S(2)}, u32[]{:S(2)}) collective-permute-start(bf16[2,4,64,384]{3,2,1,0:T(8,128)(2,1)S(1)} %add_convert_fusion.1), channel_id=1, source_target_pairs={{0,48},{16,0},{32,16},{48,32},{1,49},{17,1},{33,17},{49,33},{2,50}... | collective-permute-start | bytes 1179656 | tf_op jit(solution)/shard_map/ppermute | solution.py:40
  142.9 11.4 %collective-permute-start.17 = (bf16[4,64,384]{2,1,0:T(8,128)(2,1)S(1)}, bf16[4,64,384]{2,1,0:T(8,128)(2,1)S(1)}, u32[]{:S(2)}, u32[]{:S(2)}) collective-permute-start(bf16[4,64,384]{2,1,0:T(8,128)(2,1)S(1)} %fusion.8), channel_id=1, source_target_pairs={{0,16},{16,32},{32,48},{48,0},{1,17},{17,33},{33,49},{49,1},{2,18}... | collective-permute-start | bytes 589832 | tf_op jit(solution)/shard_map/ppermute | solution.py:40
  145.2 12.1 %collective-permute-start.19 = (bf16[4,64,384]{2,1,0:T(8,128)(2,1)S(1)}, bf16[4,64,384]{2,1,0:T(8,128)(2,1)S(1)}, u32[]{:S(2)}, u32[]{:S(2)}) collective-permute-start(bf16[4,64,384]{2,1,0:T(8,128)(2,1)S(1)} %get-tuple-element.38), channel_id=1, source_target_pairs={{0,32},{16,48},{32,0},{48,16},{1,33},{17,49},{33,1},{49,17},{2,34}... | collective-permute-start | bytes 589832 | tf_op jit(solution)/shard_map/ppermute | solution.py:40
  147.7 9.6 %collective-permute-start.20 = (bf16[4,64,384]{2,1,0:T(8,128)(2,1)S(1)}, bf16[4,64,384]{2,1,0:T(8,128)(2,1)S(1)}, u32[]{:S(2)}, u32[]{:S(2)}) collective-permute-start(bf16[4,64,384]{2,1,0:T(8,128)(2,1)S(1)} %get-tuple-element.39), channel_id=1, source_target_pairs={{0,48},{16,0},{32,16},{48,32},{1,49},{17,1},{33,17},{49,33},{2,50}... | collective-permute-start | bytes 589832 | tf_op jit(solution)/shard_map/ppermute | solution.py:40
  149.3 10.6 %collective-permute-start.25 = (bf16[4,64,384]{2,1,0:T(8,128)(2,1)S(1)}, bf16[4,64,384]{2,1,0:T(8,128)(2,1)S(1)}, u32[]{:S(2)}, u32[]{:S(2)}) collective-permute-start(bf16[4,64,384]{2,1,0:T(8,128)(2,1)S(1)} %fusion.9), channel_id=1, source_target_pairs={{0,64},{64,128},{128,192},{192,0},{1,65},{65,129},{129,193},{193,1... | collective-permute-start | bytes 589832 | tf_op jit(solution)/shard_map/ppermute | solution.py:40
  150.3 9.8 %collective-permute-start.27 = (bf16[4,64,384]{2,1,0:T(8,128)(2,1)S(1)}, bf16[4,64,384]{2,1,0:T(8,128)(2,1)S(1)}, u32[]{:S(2)}, u32[]{:S(2)}) collective-permute-start(bf16[4,64,384]{2,1,0:T(8,128)(2,1)S(1)} %get-tuple-element.36), channel_id=1, source_target_pairs={{0,128},{64,192},{128,0},{192,64},{1,129},{65,193},{129,1},{193,65... | collective-permute-start | bytes 589832 | tf_op jit(solution)/shard_map/ppermute | solution.py:40
  154.2 5.8 %collective-permute-start.28 = (bf16[4,64,384]{2,1,0:T(8,128)(2,1)S(1)}, bf16[4,64,384]{2,1,0:T(8,128)(2,1)S(1)}, u32[]{:S(2)}, u32[]{:S(2)}) collective-permute-start(bf16[4,64,384]{2,1,0:T(8,128)(2,1)S(1)} %get-tuple-element.37), channel_id=1, source_target_pairs={{0,192},{64,0},{128,64},{192,128},{1,193},{65,1},{129,65},{193,129... | collective-permute-start | bytes 589832 | tf_op jit(solution)/shard_map/ppermute | solution.py:40
  157.4 8.9 %collective-permute-start.21 = (bf16[4,32,384]{2,1,0:T(8,128)(2,1)S(1)}, bf16[4,32,384]{2,1,0:T(8,128)(2,1)S(1)}, u32[]{:S(2)}, u32[]{:S(2)}) collective-permute-start(bf16[4,32,384]{2,1,0:T(8,128)(2,1)S(1)} %select_convert_fusion.1), channel_id=1, source_target_pairs={{0,8},{8,0},{1,9},{9,1},{2,10},{10,2},{3,11},{11,3},{4,12},{12,4},... | collective-permute-start | bytes 294920 | tf_op jit(solution)/shard_map/ppermute | solution.py:29
  160.2 7.3 %collective-permute-start.29 = (bf16[4,32,384]{2,1,0:T(8,128)(2,1)S(1)}, bf16[4,32,384]{2,1,0:T(8,128)(2,1)S(1)}, u32[]{:S(2)}, u32[]{:S(2)}) collective-permute-start(bf16[4,32,384]{2,1,0:T(8,128)(2,1)S(1)} %select_convert_fusion), channel_id=1, source_target_pairs={{0,8},{8,0},{1,9},{9,1},{2,10},{10,2},{3,11},{11,3},{4,12},{12,4},... | collective-permute-start | bytes 294920 | tf_op jit(solution)/shard_map/ppermute | solution.py:29
  165.8 2.7 %collective-permute-start.13 = (bf16[2,128,1024]{2,1,0:T(8,128)(2,1)}, bf16[2,128,1024]{2,1,0:T(8,128)(2,1)S(1)}, u32[]{:S(2)}, u32[]{:S(2)}) collective-permute-start(bf16[2,128,1024]{2,1,0:T(8,128)(2,1)} %bitcast.96), channel_id=1, source_target_pairs={{0,8},{8,0},{1,9},{9,1},{2,10},{10,2},{3,11},{11,3},{4,12},{12,4},... | collective-permute-start | bytes 1572872 | tf_op jit(solution)/shard_map/ppermute | solution.py:29
  (6 other events, 214.6 us)
Sparse Core Ops, SparseCore 0:
  25.1 62.5 all-gather.1
  110.8 54.9 reduce-scatter.1

commit v3 on v2

--- a/solution.py
+++ b/solution.py
@@ -57,33 +57,6 @@
     iota = lax.broadcasted_iota(jnp.int32, (QSLOTS, QROWS), 0).astype(F32)
     picks = [(srow[e : e + 1, :] == iota).astype(F32).astype(BF) for e in range(EXPERTS_CORE)]
     return jnp.concatenate(picks, axis=0)
-
-
-def pack_kernel(tokens, out_grad, ids, gates, out, meta, sems):
-    parts = ((tokens, 0, WIDTH), (out_grad, WIDTH, WIDTH), (meta, 2 * WIDTH, ROWS))
-    copies = [
-        pltpu.make_async_copy(part, out.at[:, pl.ds(at, n)], sems.at[i]) for i, (part, at, n) in enumerate(parts)
-    ]
-    copies[0].start()
-    copies[1].start()
-    both = jnp.concatenate([ids[...].astype(F32), gates[...].astype(F32)], axis=0).astype(BF)
-    meta[:META] = both
-    meta[META:] = jnp.zeros((ROWS - META, ROWS), BF)
-    copies[2].start()
-    for copy in copies:
-        copy.wait()
-
-
-def pack(tokens, out_grad, ids, gates):
-    return pl.pallas_call(
-        pack_kernel,
-        in_specs=[ANYWHERE, ANYWHERE, pl.BlockSpec(memory_space=pltpu.VMEM), pl.BlockSpec(memory_space=pltpu.VMEM)],
-        out_specs=ANYWHERE,
-        out_shape=jax.ShapeDtypeStruct((ROWS, 2 * WIDTH + ROWS), BF),
-        scratch_shapes=[pltpu.VMEM((ROWS, ROWS), BF), pltpu.SemaphoreType.DMA((3,))],
-        compiler_params=PARAMS,
-        cost_estimate=cost(100_000, 1_100_000),
-    )(tokens, out_grad, ids, gates)
 
 
 def layer_kernel(scale, pos, rows, *refs):
@@ -234,8 +207,11 @@
     scale = 1.0 / math.sqrt(NY * NX * NC * NZ * ROWS * 8 / 64)
     y, x, c, z = (lax.axis_index(a) for a in ("y", "x", "c", "z"))
     pos = jnp.stack([y, x, c, (z * NC + c) * EXPERTS_CORE, 1 - 2 * c]).astype(jnp.int32)
-    packed = pack(tokens, out_grad, expert_ids.T, gate_values.T)
-    rows = lax.all_gather(packed, ("c", "z"), axis=0, tiled=True)
+    ids, gates = expert_ids.T.astype(F32), gate_values.T.astype(F32)
+    first = jnp.arange(META)[:, None] < META // 2
+    meta = jnp.where(first, jnp.concatenate([ids, ids]), jnp.concatenate([gates, gates])).astype(BF)
+    meta = jnp.pad(meta, ((0, ROWS - META), (0, 0)))
+    rows = lax.all_gather(jnp.concatenate([tokens, out_grad, meta], axis=1), ("c", "z"), axis=0, tiled=True)
 
     def by_core(own, sister):
         return jnp.where(c == 0, own, sister), jnp.where(c == 0, sister, own)

time: 178 us -> 161 us (0.904)
  Pallas kernels: 40.6 us -> 22.9 us
  waiting for transfers between devices: 54.8 us -> 60.4 us
  starting transfers between devices: 55.1 us -> 52.8 us
    pallas_call x1 -> x0, Pallas kernels: 17.7 us -> none  [pack(): pl.pallas_call(pack_kernel, in_specs=[ANYWHERE, ANYWHERE, pl.BlockSpec(me...]
    ppermute x14, waiting for transfers between devices: 19.2 us -> 22.4 us  [shift(): return lax.ppermute(value, axis, [(i, (i + by) % n) for i in range(n)])]
    ppermute x14, starting transfers between devices: 22.3 us -> 20.1 us  [shift(): return lax.ppermute(value, axis, [(i, (i + by) % n) for i in range(n)])]
    convert_element_type x2, other arithmetic: 2.22 us -> 0.21 us  [scatter_plane(): next_down = shift((f32(next_down) + f32(down[n:])).astype(BF), second, -1)]
    convert_element_type x2, other arithmetic: 2.22 us -> 0.21 us  [scatter_plane(): next_up = shift((f32(next_up) + f32(up[n:])).astype(BF), second, 1)]
    concatenate x0 -> x1, other arithmetic: none -> 1.87 us  [shards(): jnp.concatenate([tokens, out_grad, meta], axis=1)]
    all_gather x1, waiting for transfers between devices: 4.34 us -> 6.16 us  [shards(): lax.all_gather(jnp.concatenate([tokens, out_grad, meta], axis=1), ('c', '...]
    unnamed x16 -> x38, local copies, waits for them, and re-layouts: 3.89 us -> 3.12 us
  transfers between devices with their start and end apart: 32 -> 32, of which waited for: 18 -> 17; matrix products, arithmetic and copies ran while one was open for 6% -> 3% of each run, Pallas kernels for 0% -> 0%
where the time goes in v3:
time: 161 us
  waiting for transfers between devices  60.4 us (38%)
  starting transfers between devices  52.8 us (33%)
  Pallas kernels  22.9 us (14%)
  between operations  14.4 us (9%)
  other arithmetic  6.23 us (4%)
  local copies, waits for them, and re-layouts  3.86 us (2%)
    ppermute x12, waiting for transfers between devices, step(): return lax.ppermute(value, (axis, 'c'), pairs)  29.7 us
    pallas_call x1, Pallas kernels, layer(): pl.pallas_call(lambda *refs: layer_kernel(scale, *refs), grid_spec=pltpu....  22.9 us
    ppermute x14, waiting for transfers between devices, shift(): return lax.ppermute(value, axis, [(i, (i + by) % n) for i in range(n)])  22.4 us
    ppermute x12, starting transfers between devices, step(): return lax.ppermute(value, (axis, 'c'), pairs)  21.3 us
    ppermute x14, starting transfers between devices, shift(): return lax.ppermute(value, axis, [(i, (i + by) % n) for i in range(n)])  20.1 us
    ppermute x4, starting transfers between devices, swap(): return lax.ppermute(value, 'c', [(0, 1), (1, 0)])  11.4 us
    all_gather x1, waiting for transfers between devices, shards(): lax.all_gather(jnp.concatenate([tokens, out_grad, meta], axis=1), ('c', '...  6.16 us
  transfers between devices with their start and end apart: 32, of which 17 were waited for; matrix products, arithmetic and copies ran while one was open for 3% of the time, Pallas kernels for 0%

profile of v3, /device:TPU:1, one launch (start us, length us, event | category | flops | bytes accessed | tf_op | source)
XLA Modules:
  0.0 160.6 jit_solution(233276507479561322)
XLA Ops:
  8.9 1.9 %fusion.1 = bf16[128,2176]{1,0:T(8,128)(2,1)} fusion(bf16[16,128]{1,0:T(8,128)(2,1)S(1)} %fusion.12, bf16[128,1024]{1,0:T(8,128)(2,1)} %param.7, bf16[128,1024]{1,0:T(8,128)(2,1)} %param.6), kind=kLoop, calls=%fused_computation.12 | loop fusion | flops 2228224 | bytes 1085440 | tf_op jit(solution)/shard_map/concatenate | solution.py:214
  11.0 3.3 %collective-permute-start = (bf16[2,4,32,384]{3,2,1,0:T(8,128)(2,1)S(1)}, bf16[2,4,32,384]{3,2,1,0:T(8,128)(2,1)S(1)}, u32[]{:S(2)}, u32[]{:S(2)}) collective-permute-start(bf16[2,4,32,384]{3,2,1,0:T(8,128)(2,1)S(1)} %pad_maximum_fusion.2), channel_id=1, source_target_pairs={{0,8},{8,0},{1,9},{9,1},{2,10},{10,2},{3,11},{11,3},{4,12},{12,4},... | collective-permute-start | bytes 589832 | tf_op jit(solution)/shard_map/ppermute | solution.py:29
  18.1 3.0 %collective-permute-start.8 = (bf16[4,64,384]{2,1,0:T(8,128)(2,1)S(1)}, bf16[4,64,384]{2,1,0:T(8,128)(2,1)S(1)}, u32[]{:S(2)}, u32[]{:S(2)}) collective-permute-start(bf16[4,64,384]{2,1,0:T(8,128)(2,1)S(1)} %get-tuple-element.45), channel_id=1, source_target_pairs={{0,128},{8,136},{64,192},{72,200},{128,0},{136,8},{192,64},{200,72... | collective-permute-start | bytes 589832 | tf_op jit(solution)/shard_map/ppermute | solution.py:35
  21.9 1.4 collective-permute-done.2
  23.2 2.6 %collective-permute-done.1 = bf16[4,64,384]{2,1,0:T(8,128)(2,1)S(1)} collective-permute-done((bf16[4,64,384]{2,1,0:T(8,128)(2,1)S(1)}, bf16[4,64,384]{2,1,0:T(8,128)(2,1)S(1)}, u32[]{:S(2)}, u32[]{:S(2)}) %collective-permute-start.1) | collective-permute-done | bytes 196640 | tf_op jit(solution)/shard_map/ppermute | solution.py:35
  25.8 2.4 %collective-permute-done.3 = bf16[4,64,384]{2,1,0:T(8,128)(2,1)S(1)} collective-permute-done((bf16[4,64,384]{2,1,0:T(8,128)(2,1)S(1)}, bf16[4,64,384]{2,1,0:T(8,128)(2,1)S(1)}, u32[]{:S(2)}, u32[]{:S(2)}) %collective-permute-start.3) | collective-permute-done | bytes 196640 | tf_op jit(solution)/shard_map/ppermute | solution.py:35
  29.4 2.0 %collective-permute-done.9 = bf16[4,64,384]{2,1,0:T(8,128)(2,1)S(1)} collective-permute-done((bf16[4,64,384]{2,1,0:T(8,128)(2,1)S(1)}, bf16[4,64,384]{2,1,0:T(8,128)(2,1)S(1)}, u32[]{:S(2)}, u32[]{:S(2)}) %collective-permute-start.9) | collective-permute-done | bytes 196640 | tf_op jit(solution)/shard_map/ppermute | solution.py:35
  31.5 1.7 %collective-permute-start.10 = (bf16[4,4,64,384]{3,2,1,0:T(8,128)(2,1)S(1)}, bf16[4,4,64,384]{3,2,1,0:T(8,128)(2,1)S(1)}, u32[]{:S(2)}, u32[]{:S(2)}) collective-permute-start(bf16[4,4,64,384]{3,2,1,0:T(8,128)(2,1)S(1)} %pad_maximum_fusion.1.refs_6_), channel_id=1, source_target_pairs={{0,16},{8,56},{16,32},{24,8},{32,48},{40,24},{48,0},{56,40},{1,17}... | collective-permute-start | bytes 2359304 | tf_op jit(solution)/shard_map/ppermute | solution.py:35
  33.2 6.5 %collective-permute-done.4.refs_3_ = bf16[4,4,64,384]{3,2,1,0:T(8,128)(2,1)S(1)} collective-permute-done((bf16[4,4,64,384]{3,2,1,0:T(8,128)(2,1)S(1)}, bf16[4,4,64,384]{3,2,1,0:T(8,128)(2,1)S(1)}, u32[]{:S(2)}, u32[]{:S(2)}) %collective-permute-start.4) | collective-permute-done | bytes 786464 | tf_op jit(solution)/shard_map/ppermute | solution.py:35
  39.7 2.4 %collective-permute-start.5 = (bf16[4,4,64,384]{3,2,1,0:T(8,128)(2,1)S(1)}, bf16[4,4,64,384]{3,2,1,0:T(8,128)(2,1)}, u32[]{:S(2)}, u32[]{:S(2)}) collective-permute-start(bf16[4,4,64,384]{3,2,1,0:T(8,128)(2,1)S(1)} %collective-permute-done.4.refs_3_), channel_id=1, source_target_pairs={{0,64},{8,200},{64,128},{72,8},{128,192},{136,72},{192,0},{200,136... | collective-permute-start | bytes 2359304 | tf_op jit(solution)/shard_map/ppermute | solution.py:35
  42.8 2.8 %collective-permute-start.11 = (bf16[4,4,64,384]{3,2,1,0:T(8,128)(2,1)S(1)}, bf16[4,4,64,384]{3,2,1,0:T(8,128)(2,1)}, u32[]{:S(2)}, u32[]{:S(2)}) collective-permute-start(bf16[4,4,64,384]{3,2,1,0:T(8,128)(2,1)S(1)} %collective-permute-done.10.refs_7_), channel_id=1, source_target_pairs={{0,16},{8,56},{16,32},{24,8},{32,48},{40,24},{48,0},{56,40},{1,17}... | collective-permute-start | bytes 2359304 | tf_op jit(solution)/shard_map/ppermute | solution.py:35
  45.7 5.4 %collective-permute-done.5.refs_4_ = bf16[4,4,64,384]{3,2,1,0:T(8,128)(2,1)} collective-permute-done((bf16[4,4,64,384]{3,2,1,0:T(8,128)(2,1)S(1)}, bf16[4,4,64,384]{3,2,1,0:T(8,128)(2,1)}, u32[]{:S(2)}, u32[]{:S(2)}) %collective-permute-start.5) | collective-permute-done | bytes 786464 | tf_op jit(solution)/shard_map/ppermute | solution.py:35
  51.0 3.5 %collective-permute-start.6 = (bf16[4,4,64,384]{3,2,1,0:T(8,128)(2,1)}, bf16[4,4,64,384]{3,2,1,0:T(8,128)(2,1)}, u32[]{:S(2)}, u32[]{:S(2)}) collective-permute-start(bf16[4,4,64,384]{3,2,1,0:T(8,128)(2,1)} %collective-permute-done.5.refs_4_), channel_id=1, source_target_pairs={{0,64},{8,200},{64,128},{72,8},{128,192},{136,72},{192,0},{200,136... | collective-permute-start | bytes 2359304 | tf_op jit(solution)/shard_map/ppermute | solution.py:35
  54.6 3.5 %collective-permute-start.12 = (bf16[4,4,64,384]{3,2,1,0:T(8,128)(2,1)}, bf16[4,4,64,384]{3,2,1,0:T(8,128)(2,1)}, u32[]{:S(2)}, u32[]{:S(2)}) collective-permute-start(bf16[4,4,64,384]{3,2,1,0:T(8,128)(2,1)} %collective-permute-done.11.refs_8_), channel_id=1, source_target_pairs={{0,16},{8,56},{16,32},{24,8},{32,48},{40,24},{48,0},{56,40},{1,17}... | collective-permute-start | bytes 2359304 | tf_op jit(solution)/shard_map/ppermute | solution.py:35
  58.7 5.1 %collective-permute-done.6.refs_5_ = bf16[4,4,64,384]{3,2,1,0:T(8,128)(2,1)} collective-permute-done((bf16[4,4,64,384]{3,2,1,0:T(8,128)(2,1)}, bf16[4,4,64,384]{3,2,1,0:T(8,128)(2,1)}, u32[]{:S(2)}, u32[]{:S(2)}) %collective-permute-start.6) | collective-permute-done | bytes 786464 | tf_op jit(solution)/shard_map/ppermute | solution.py:35
  63.8 3.6 %collective-permute-done.12.refs_9_ = bf16[4,4,64,384]{3,2,1,0:T(8,128)(2,1)} collective-permute-done((bf16[4,4,64,384]{3,2,1,0:T(8,128)(2,1)}, bf16[4,4,64,384]{3,2,1,0:T(8,128)(2,1)}, u32[]{:S(2)}, u32[]{:S(2)}) %collective-permute-start.12) | collective-permute-done | bytes 786464 | tf_op jit(solution)/shard_map/ppermute | solution.py:35
  67.4 6.2 %all-gather.2.cloned.1.call-done.refs_1_ = bf16[2048,2176]{1,0:T(8,128)(2,1)} async-done(((bf16[128,2176]{1,0:T(8,128)(2,1)}), bf16[2048,2176]{1,0:T(8,128)(2,1)}) %all-gather.2.cloned.1.call-update) | async-done | bytes 8912912 | tf_op jit(solution)/shard_map/all_gather | solution.py:214
  73.5 22.9 %shard_map.85 = (bf16[8,2,128,1024]{3,2,1,0:T(8,128)(2,1)}, bf16[4,4,64,384]{3,2,1,0:T(8,128)(2,1)}, bf16[4,4,64,384]{3,2,1,0:T(8,128)(2,1)}, bf16[4,4,64,384]{3...) custom-call(s32[5]{0:T(128)} %stack.62.refs_0_, ...), custom_call_target="tpu_custom_call" | custom-call | flops 12999999488 | bytes 26000000 | tf_op jit(solution)/shard_map/pallas_call | solution.py:165
  97.6 1.2 collective-permute-start.14
  98.8 1.5 collective-permute-start.16
  101.5 1.5 collective-permute-start.24
  102.9 14.8 %collective-permute-done.14 = bf16[4,4,64,384]{3,2,1,0:T(8,128)(2,1)S(1)} collective-permute-done((bf16[4,4,64,384]{3,2,1,0:T(8,128)(2,1)S(1)}, bf16[4,4,64,384]{3,2,1,0:T(8,128)(2,1)S(1)}, u32[]{:S(2)}, u32[]{:S(2)}) %collective-permute-start.14) | collective-permute-done | bytes 786464 | tf_op jit(solution)/shard_map/ppermute | solution.py:40
  118.1 2.7 %collective-permute-start.18 = (bf16[2,4,64,384]{3,2,1,0:T(8,128)(2,1)S(1)}, bf16[2,4,64,384]{3,2,1,0:T(8,128)(2,1)S(1)}, u32[]{:S(2)}, u32[]{:S(2)}) collective-permute-start(bf16[2,4,64,384]{3,2,1,0:T(8,128)(2,1)S(1)} %add_convert_fusion.4), channel_id=1, source_target_pairs={{0,192},{64,0},{128,64},{192,128},{1,193},{65,1},{129,65},{193,129... | collective-permute-start | bytes 1179656 | tf_op jit(solution)/shard_map/ppermute | solution.py:40
  120.9 1.3 collective-permute-start.23
  122.3 1.5 collective-permute-start.26
  123.9 5.0 %collective-permute-done.15 = bf16[2,4,64,384]{3,2,1,0:T(8,128)(2,1)S(1)} collective-permute-done((bf16[2,4,64,384]{3,2,1,0:T(8,128)(2,1)S(1)}, bf16[2,4,64,384]{3,2,1,0:T(8,128)(2,1)S(1)}, u32[]{:S(2)}, u32[]{:S(2)}) %collective-permute-start.15) | collective-permute-done | bytes 393248 | tf_op jit(solution)/shard_map/ppermute | solution.py:40
  129.3 1.5 collective-permute-start.17
  130.9 2.5 %collective-permute-start.19 = (bf16[4,64,384]{2,1,0:T(8,128)(2,1)S(1)}, bf16[4,64,384]{2,1,0:T(8,128)(2,1)S(1)}, u32[]{:S(2)}, u32[]{:S(2)}) collective-permute-start(bf16[4,64,384]{2,1,0:T(8,128)(2,1)S(1)} %get-tuple-element.38), channel_id=1, source_target_pairs={{0,32},{16,48},{32,0},{48,16},{1,33},{17,49},{33,1},{49,17},{2,34}... | collective-permute-start | bytes 589832 | tf_op jit(solution)/shard_map/ppermute | solution.py:40
  135.0 3.8 %collective-permute-start.27 = (bf16[4,64,384]{2,1,0:T(8,128)(2,1)S(1)}, bf16[4,64,384]{2,1,0:T(8,128)(2,1)S(1)}, u32[]{:S(2)}, u32[]{:S(2)}) collective-permute-start(bf16[4,64,384]{2,1,0:T(8,128)(2,1)S(1)} %get-tuple-element.36), channel_id=1, source_target_pairs={{0,128},{64,192},{128,0},{192,64},{1,129},{65,193},{129,1},{193,65... | collective-permute-start | bytes 589832 | tf_op jit(solution)/shard_map/ppermute | solution.py:40
  138.9 1.5 collective-permute-done.19
  140.4 3.2 %collective-permute-start.21 = (bf16[4,32,384]{2,1,0:T(8,128)(2,1)S(1)}, bf16[4,32,384]{2,1,0:T(8,128)(2,1)S(1)}, u32[]{:S(2)}, u32[]{:S(2)}) collective-permute-start(bf16[4,32,384]{2,1,0:T(8,128)(2,1)S(1)} %select_convert_fusion.1), channel_id=1, source_target_pairs={{0,8},{8,0},{1,9},{9,1},{2,10},{10,2},{3,11},{11,3},{4,12},{12,4},... | collective-permute-start | bytes 294920 | tf_op jit(solution)/shard_map/ppermute | solution.py:29
  144.9 4.2 %collective-permute-start.29 = (bf16[4,32,384]{2,1,0:T(8,128)(2,1)S(1)}, bf16[4,32,384]{2,1,0:T(8,128)(2,1)S(1)}, u32[]{:S(2)}, u32[]{:S(2)}) collective-permute-start(bf16[4,32,384]{2,1,0:T(8,128)(2,1)S(1)} %select_convert_fusion), channel_id=1, source_target_pairs={{0,8},{8,0},{1,9},{9,1},{2,10},{10,2},{3,11},{11,3},{4,12},{12,4},... | collective-permute-start | bytes 294920 | tf_op jit(solution)/shard_map/ppermute | solution.py:29
  (104 shorter events, 19.9 us)
Async XLA Ops:
  7.2 66.3 %all-gather.2.cloned.1.call-start = ((), (), s32[]{:S(2)}) async-start(), calls=%async_computation.1 | async-start | bytes 9469952 | tf_op jit(solution)/shard_map/all_gather | solution.py:214
  10.8 139.4 %reduce-scatter.2.cloned.1.call-start = ((), (), s32[]{:S(2)}) async-start(), calls=%async_computation.2 | async-start | bytes 4718592 | tf_op jit(solution)/shard_map/reduce_scatter | solution.py:230
  11.0 4.4 %collective-permute-start = (bf16[2,4,32,384]{3,2,1,0:T(8,128)(2,1)S(1)}, bf16[2,4,32,384]{3,2,1,0:T(8,128)(2,1)S(1)}, u32[]{:S(2)}, u32[]{:S(2)}) collective-permute-start(bf16[2,4,32,384]{3,2,1,0:T(8,128)(2,1)S(1)} %pad_maximum_fusion.2), channel_id=1, source_target_pairs={{0,8},{8,0},{1,9},{9,1},{2,10},{10,2},{3,11},{11,3},{4,12},{12,4},... | collective-permute-start | bytes 589832 | tf_op jit(solution)/shard_map/ppermute | solution.py:29
  15.5 7.7 %collective-permute-start.2 = (bf16[4,64,384]{2,1,0:T(8,128)(2,1)S(1)}, bf16[4,64,384]{2,1,0:T(8,128)(2,1)S(1)}, u32[]{:S(2)}, u32[]{:S(2)}) collective-permute-start(bf16[4,64,384]{2,1,0:T(8,128)(2,1)S(1)} %get-tuple-element.49), channel_id=1, source_target_pairs={{0,32},{8,40},{16,48},{24,56},{32,0},{40,8},{48,16},{56,24},{1,33}... | collective-permute-start | bytes 589832 | tf_op jit(solution)/shard_map/ppermute | solution.py:35
  16.6 9.2 %collective-permute-start.1 = (bf16[4,64,384]{2,1,0:T(8,128)(2,1)S(1)}, bf16[4,64,384]{2,1,0:T(8,128)(2,1)S(1)}, u32[]{:S(2)}, u32[]{:S(2)}) collective-permute-start(bf16[4,64,384]{2,1,0:T(8,128)(2,1)S(1)} %get-tuple-element.49), channel_id=1, source_target_pairs={{0,16},{8,56},{16,32},{24,8},{32,48},{40,24},{48,0},{56,40},{1,17}... | collective-permute-start | bytes 589832 | tf_op jit(solution)/shard_map/ppermute | solution.py:35
  17.4 10.7 %collective-permute-start.3 = (bf16[4,64,384]{2,1,0:T(8,128)(2,1)S(1)}, bf16[4,64,384]{2,1,0:T(8,128)(2,1)S(1)}, u32[]{:S(2)}, u32[]{:S(2)}) collective-permute-start(bf16[4,64,384]{2,1,0:T(8,128)(2,1)S(1)} %get-tuple-element.49), channel_id=1, source_target_pairs={{0,48},{8,24},{16,0},{24,40},{32,16},{40,56},{48,32},{56,8},{1,49}... | collective-permute-start | bytes 589832 | tf_op jit(solution)/shard_map/ppermute | solution.py:35
  18.1 11.3 %collective-permute-start.8 = (bf16[4,64,384]{2,1,0:T(8,128)(2,1)S(1)}, bf16[4,64,384]{2,1,0:T(8,128)(2,1)S(1)}, u32[]{:S(2)}, u32[]{:S(2)}) collective-permute-start(bf16[4,64,384]{2,1,0:T(8,128)(2,1)S(1)} %get-tuple-element.45), channel_id=1, source_target_pairs={{0,128},{8,136},{64,192},{72,200},{128,0},{136,8},{192,64},{200,72... | collective-permute-start | bytes 589832 | tf_op jit(solution)/shard_map/ppermute | solution.py:35
  21.1 8.3 %collective-permute-start.7 = (bf16[4,64,384]{2,1,0:T(8,128)(2,1)S(1)}, bf16[4,64,384]{2,1,0:T(8,128)(2,1)S(1)}, u32[]{:S(2)}, u32[]{:S(2)}) collective-permute-start(bf16[4,64,384]{2,1,0:T(8,128)(2,1)S(1)} %get-tuple-element.45), channel_id=1, source_target_pairs={{0,64},{8,200},{64,128},{72,8},{128,192},{136,72},{192,0},{200,136... | collective-permute-start | bytes 589832 | tf_op jit(solution)/shard_map/ppermute | solution.py:35
  23.2 8.2 %collective-permute-start.9 = (bf16[4,64,384]{2,1,0:T(8,128)(2,1)S(1)}, bf16[4,64,384]{2,1,0:T(8,128)(2,1)S(1)}, u32[]{:S(2)}, u32[]{:S(2)}) collective-permute-start(bf16[4,64,384]{2,1,0:T(8,128)(2,1)S(1)} %get-tuple-element.45), channel_id=1, source_target_pairs={{0,192},{8,72},{64,0},{72,136},{128,64},{136,200},{192,128},{200,8... | collective-permute-start | bytes 589832 | tf_op jit(solution)/shard_map/ppermute | solution.py:35
  28.3 11.4 %collective-permute-start.4 = (bf16[4,4,64,384]{3,2,1,0:T(8,128)(2,1)S(1)}, bf16[4,4,64,384]{3,2,1,0:T(8,128)(2,1)S(1)}, u32[]{:S(2)}, u32[]{:S(2)}) collective-permute-start(bf16[4,4,64,384]{3,2,1,0:T(8,128)(2,1)S(1)} %pad_maximum_fusion.refs_2_), channel_id=1, source_target_pairs={{0,64},{8,200},{64,128},{72,8},{128,192},{136,72},{192,0},{200,136... | collective-permute-start | bytes 2359304 | tf_op jit(solution)/shard_map/ppermute | solution.py:35
  31.5 11.3 %collective-permute-start.10 = (bf16[4,4,64,384]{3,2,1,0:T(8,128)(2,1)S(1)}, bf16[4,4,64,384]{3,2,1,0:T(8,128)(2,1)S(1)}, u32[]{:S(2)}, u32[]{:S(2)}) collective-permute-start(bf16[4,4,64,384]{3,2,1,0:T(8,128)(2,1)S(1)} %pad_maximum_fusion.1.refs_6_), channel_id=1, source_target_pairs={{0,16},{8,56},{16,32},{24,8},{32,48},{40,24},{48,0},{56,40},{1,17}... | collective-permute-start | bytes 2359304 | tf_op jit(solution)/shard_map/ppermute | solution.py:35
  39.7 11.3 %collective-permute-start.5 = (bf16[4,4,64,384]{3,2,1,0:T(8,128)(2,1)S(1)}, bf16[4,4,64,384]{3,2,1,0:T(8,128)(2,1)}, u32[]{:S(2)}, u32[]{:S(2)}) collective-permute-start(bf16[4,4,64,384]{3,2,1,0:T(8,128)(2,1)S(1)} %collective-permute-done.4.refs_3_), channel_id=1, source_target_pairs={{0,64},{8,200},{64,128},{72,8},{128,192},{136,72},{192,0},{200,136... | collective-permute-start | bytes 2359304 | tf_op jit(solution)/shard_map/ppermute | solution.py:35
  42.8 11.8 %collective-permute-start.11 = (bf16[4,4,64,384]{3,2,1,0:T(8,128)(2,1)S(1)}, bf16[4,4,64,384]{3,2,1,0:T(8,128)(2,1)}, u32[]{:S(2)}, u32[]{:S(2)}) collective-permute-start(bf16[4,4,64,384]{3,2,1,0:T(8,128)(2,1)S(1)} %collective-permute-done.10.refs_7_), channel_id=1, source_target_pairs={{0,16},{8,56},{16,32},{24,8},{32,48},{40,24},{48,0},{56,40},{1,17}... | collective-permute-start | bytes 2359304 | tf_op jit(solution)/shard_map/ppermute | solution.py:35
  51.0 12.8 %collective-permute-start.6 = (bf16[4,4,64,384]{3,2,1,0:T(8,128)(2,1)}, bf16[4,4,64,384]{3,2,1,0:T(8,128)(2,1)}, u32[]{:S(2)}, u32[]{:S(2)}) collective-permute-start(bf16[4,4,64,384]{3,2,1,0:T(8,128)(2,1)} %collective-permute-done.5.refs_4_), channel_id=1, source_target_pairs={{0,64},{8,200},{64,128},{72,8},{128,192},{136,72},{192,0},{200,136... | collective-permute-start | bytes 2359304 | tf_op jit(solution)/shard_map/ppermute | solution.py:35
  54.6 12.8 %collective-permute-start.12 = (bf16[4,4,64,384]{3,2,1,0:T(8,128)(2,1)}, bf16[4,4,64,384]{3,2,1,0:T(8,128)(2,1)}, u32[]{:S(2)}, u32[]{:S(2)}) collective-permute-start(bf16[4,4,64,384]{3,2,1,0:T(8,128)(2,1)} %collective-permute-done.11.refs_8_), channel_id=1, source_target_pairs={{0,16},{8,56},{16,32},{24,8},{32,48},{40,24},{48,0},{56,40},{1,17}... | collective-permute-start | bytes 2359304 | tf_op jit(solution)/shard_map/ppermute | solution.py:35
  97.6 20.2 %collective-permute-start.14 = (bf16[4,4,64,384]{3,2,1,0:T(8,128)(2,1)S(1)}, bf16[4,4,64,384]{3,2,1,0:T(8,128)(2,1)S(1)}, u32[]{:S(2)}, u32[]{:S(2)}) collective-permute-start(bf16[4,4,64,384]{3,2,1,0:T(8,128)(2,1)S(1)} %copy-done.16), channel_id=1, source_target_pairs={{0,64},{64,128},{128,192},{192,0},{1,65},{65,129},{129,193},{193,1... | collective-permute-start | bytes 2359304 | tf_op jit(solution)/shard_map/ppermute | solution.py:40
  98.8 19.2 %collective-permute-start.16 = (bf16[4,4,64,384]{3,2,1,0:T(8,128)(2,1)S(1)}, bf16[4,4,64,384]{3,2,1,0:T(8,128)(2,1)S(1)}, u32[]{:S(2)}, u32[]{:S(2)}) collective-permute-start(bf16[4,4,64,384]{3,2,1,0:T(8,128)(2,1)S(1)} %copy-done.15), channel_id=1, source_target_pairs={{0,192},{64,0},{128,64},{192,128},{1,193},{65,1},{129,65},{193,129... | collective-permute-start | bytes 2359304 | tf_op jit(solution)/shard_map/ppermute | solution.py:40
  100.3 20.6 %collective-permute-start.22 = (bf16[4,4,64,384]{3,2,1,0:T(8,128)(2,1)S(1)}, bf16[4,4,64,384]{3,2,1,0:T(8,128)(2,1)S(1)}, u32[]{:S(2)}, u32[]{:S(2)}) collective-permute-start(bf16[4,4,64,384]{3,2,1,0:T(8,128)(2,1)S(1)} %copy-done.14), channel_id=1, source_target_pairs={{0,16},{16,32},{32,48},{48,0},{1,17},{17,33},{33,49},{49,1},{2,18}... | collective-permute-start | bytes 2359304 | tf_op jit(solution)/shard_map/ppermute | solution.py:40
  101.5 20.8 %collective-permute-start.24 = (bf16[4,4,64,384]{3,2,1,0:T(8,128)(2,1)S(1)}, bf16[4,4,64,384]{3,2,1,0:T(8,128)(2,1)S(1)}, u32[]{:S(2)}, u32[]{:S(2)}) collective-permute-start(bf16[4,4,64,384]{3,2,1,0:T(8,128)(2,1)S(1)} %copy-done.13), channel_id=1, source_target_pairs={{0,48},{16,0},{32,16},{48,32},{1,49},{17,1},{33,17},{49,33},{2,50}... | collective-permute-start | bytes 2359304 | tf_op jit(solution)/shard_map/ppermute | solution.py:40
  117.9 11.0 %collective-permute-start.15 = (bf16[2,4,64,384]{3,2,1,0:T(8,128)(2,1)S(1)}, bf16[2,4,64,384]{3,2,1,0:T(8,128)(2,1)S(1)}, u32[]{:S(2)}, u32[]{:S(2)}) collective-permute-start(bf16[2,4,64,384]{3,2,1,0:T(8,128)(2,1)S(1)} %add_convert_fusion.5), channel_id=1, source_target_pairs={{0,64},{64,128},{128,192},{192,0},{1,65},{65,129},{129,193},{193,1... | collective-permute-start | bytes 1179656 | tf_op jit(solution)/shard_map/ppermute | solution.py:40
  118.1 10.8 %collective-permute-start.18 = (bf16[2,4,64,384]{3,2,1,0:T(8,128)(2,1)S(1)}, bf16[2,4,64,384]{3,2,1,0:T(8,128)(2,1)S(1)}, u32[]{:S(2)}, u32[]{:S(2)}) collective-permute-start(bf16[2,4,64,384]{3,2,1,0:T(8,128)(2,1)S(1)} %add_convert_fusion.4), channel_id=1, source_target_pairs={{0,192},{64,0},{128,64},{192,128},{1,193},{65,1},{129,65},{193,129... | collective-permute-start | bytes 1179656 | tf_op jit(solution)/shard_map/ppermute | solution.py:40
  120.9 13.6 %collective-permute-start.23 = (bf16[2,4,64,384]{3,2,1,0:T(8,128)(2,1)S(1)}, bf16[2,4,64,384]{3,2,1,0:T(8,128)(2,1)S(1)}, u32[]{:S(2)}, u32[]{:S(2)}) collective-permute-start(bf16[2,4,64,384]{3,2,1,0:T(8,128)(2,1)S(1)} %add_convert_fusion.2), channel_id=1, source_target_pairs={{0,16},{16,32},{32,48},{48,0},{1,17},{17,33},{33,49},{49,1},{2,18}... | collective-permute-start | bytes 1179656 | tf_op jit(solution)/shard_map/ppermute | solution.py:40
  122.3 12.2 %collective-permute-start.26 = (bf16[2,4,64,384]{3,2,1,0:T(8,128)(2,1)S(1)}, bf16[2,4,64,384]{3,2,1,0:T(8,128)(2,1)S(1)}, u32[]{:S(2)}, u32[]{:S(2)}) collective-permute-start(bf16[2,4,64,384]{3,2,1,0:T(8,128)(2,1)S(1)} %add_convert_fusion.1), channel_id=1, source_target_pairs={{0,48},{16,0},{32,16},{48,32},{1,49},{17,1},{33,17},{49,33},{2,50}... | collective-permute-start | bytes 1179656 | tf_op jit(solution)/shard_map/ppermute | solution.py:40
  129.3 9.6 %collective-permute-start.17 = (bf16[4,64,384]{2,1,0:T(8,128)(2,1)S(1)}, bf16[4,64,384]{2,1,0:T(8,128)(2,1)S(1)}, u32[]{:S(2)}, u32[]{:S(2)}) collective-permute-start(bf16[4,64,384]{2,1,0:T(8,128)(2,1)S(1)} %fusion.10), channel_id=1, source_target_pairs={{0,16},{16,32},{32,48},{48,0},{1,17},{17,33},{33,49},{49,1},{2,18}... | collective-permute-start | bytes 589832 | tf_op jit(solution)/shard_map/ppermute | solution.py:40
  130.9 9.4 %collective-permute-start.19 = (bf16[4,64,384]{2,1,0:T(8,128)(2,1)S(1)}, bf16[4,64,384]{2,1,0:T(8,128)(2,1)S(1)}, u32[]{:S(2)}, u32[]{:S(2)}) collective-permute-start(bf16[4,64,384]{2,1,0:T(8,128)(2,1)S(1)} %get-tuple-element.38), channel_id=1, source_target_pairs={{0,32},{16,48},{32,0},{48,16},{1,33},{17,49},{33,1},{49,17},{2,34}... | collective-permute-start | bytes 589832 | tf_op jit(solution)/shard_map/ppermute | solution.py:40
  133.4 7.0 %collective-permute-start.20 = (bf16[4,64,384]{2,1,0:T(8,128)(2,1)S(1)}, bf16[4,64,384]{2,1,0:T(8,128)(2,1)S(1)}, u32[]{:S(2)}, u32[]{:S(2)}) collective-permute-start(bf16[4,64,384]{2,1,0:T(8,128)(2,1)S(1)} %get-tuple-element.39), channel_id=1, source_target_pairs={{0,48},{16,0},{32,16},{48,32},{1,49},{17,1},{33,17},{49,33},{2,50}... | collective-permute-start | bytes 589832 | tf_op jit(solution)/shard_map/ppermute | solution.py:40
  134.9 8.8 %collective-permute-start.25 = (bf16[4,64,384]{2,1,0:T(8,128)(2,1)S(1)}, bf16[4,64,384]{2,1,0:T(8,128)(2,1)S(1)}, u32[]{:S(2)}, u32[]{:S(2)}) collective-permute-start(bf16[4,64,384]{2,1,0:T(8,128)(2,1)S(1)} %fusion.11), channel_id=1, source_target_pairs={{0,64},{64,128},{128,192},{192,0},{1,65},{65,129},{129,193},{193,1... | collective-permute-start | bytes 589832 | tf_op jit(solution)/shard_map/ppermute | solution.py:40
  135.0 9.7 %collective-permute-start.27 = (bf16[4,64,384]{2,1,0:T(8,128)(2,1)S(1)}, bf16[4,64,384]{2,1,0:T(8,128)(2,1)S(1)}, u32[]{:S(2)}, u32[]{:S(2)}) collective-permute-start(bf16[4,64,384]{2,1,0:T(8,128)(2,1)S(1)} %get-tuple-element.36), channel_id=1, source_target_pairs={{0,128},{64,192},{128,0},{192,64},{1,129},{65,193},{129,1},{193,65... | collective-permute-start | bytes 589832 | tf_op jit(solution)/shard_map/ppermute | solution.py:40
  138.9 5.9 %collective-permute-start.28 = (bf16[4,64,384]{2,1,0:T(8,128)(2,1)S(1)}, bf16[4,64,384]{2,1,0:T(8,128)(2,1)S(1)}, u32[]{:S(2)}, u32[]{:S(2)}) collective-permute-start(bf16[4,64,384]{2,1,0:T(8,128)(2,1)S(1)} %get-tuple-element.37), channel_id=1, source_target_pairs={{0,192},{64,0},{128,64},{192,128},{1,193},{65,1},{129,65},{193,129... | collective-permute-start | bytes 589832 | tf_op jit(solution)/shard_map/ppermute | solution.py:40
  140.4 10.3 %collective-permute-start.21 = (bf16[4,32,384]{2,1,0:T(8,128)(2,1)S(1)}, bf16[4,32,384]{2,1,0:T(8,128)(2,1)S(1)}, u32[]{:S(2)}, u32[]{:S(2)}) collective-permute-start(bf16[4,32,384]{2,1,0:T(8,128)(2,1)S(1)} %select_convert_fusion.1), channel_id=1, source_target_pairs={{0,8},{8,0},{1,9},{9,1},{2,10},{10,2},{3,11},{11,3},{4,12},{12,4},... | collective-permute-start | bytes 294920 | tf_op jit(solution)/shard_map/ppermute | solution.py:29
  144.9 7.0 %collective-permute-start.29 = (bf16[4,32,384]{2,1,0:T(8,128)(2,1)S(1)}, bf16[4,32,384]{2,1,0:T(8,128)(2,1)S(1)}, u32[]{:S(2)}, u32[]{:S(2)}) collective-permute-start(bf16[4,32,384]{2,1,0:T(8,128)(2,1)S(1)} %select_convert_fusion), channel_id=1, source_target_pairs={{0,8},{8,0},{1,9},{9,1},{2,10},{10,2},{3,11},{11,3},{4,12},{12,4},... | collective-permute-start | bytes 294920 | tf_op jit(solution)/shard_map/ppermute | solution.py:29
  150.2 2.7 %collective-permute-start.13 = (bf16[2,128,1024]{2,1,0:T(8,128)(2,1)}, bf16[2,128,1024]{2,1,0:T(8,128)(2,1)S(1)}, u32[]{:S(2)}, u32[]{:S(2)}) collective-permute-start(bf16[2,128,1024]{2,1,0:T(8,128)(2,1)} %bitcast.97), channel_id=1, source_target_pairs={{0,8},{8,0},{1,9},{9,1},{2,10},{10,2},{3,11},{11,3},{4,12},{12,4},... | collective-permute-start | bytes 1572872 | tf_op jit(solution)/shard_map/ppermute | solution.py:29
  (17 other events, 235.8 us)
Sparse Core Ops, SparseCore 0:
  10.9 62.5 all-gather.1
  96.6 53.4 reduce-scatter.1

commit v4 on v3

--- a/solution.py
+++ b/solution.py
@@ -22,7 +22,7 @@
 PARTS = (4, 4, 4, 2, 2)
 SIZES = {"y": NY, "x": NX}
 ANYWHERE = pl.BlockSpec(memory_space=pl.ANY)
-PARAMS = pltpu.CompilerParams(vmem_limit_bytes=60 * 2**20)
+PARAMS = pltpu.CompilerParams(vmem_limit_bytes=54 * 2**20)
 
 
 def swap(value):
@@ -159,7 +159,7 @@
 def layer(scale, pos, rows, a_in, b_in):
     expert = lambda i: jnp.maximum(i - QUADS, 0)
     piece = lambda n: pl.BlockSpec((n, 1, PIECE, HID), lambda i, p: (0, expert(i), 0, 0))
-    grads = lambda n: jax.ShapeDtypeStruct((n, EXPERTS_CORE, PIECE, HID), BF)
+    grads = lambda n, near: (pltpu.VMEM if near else jax.ShapeDtypeStruct)((n, EXPERTS_CORE, PIECE, HID), BF)
     by_z = (NZ, NC, ROWS, WIDTH)
     slots = lambda n, dtype: pltpu.VMEM((EXPERTS_CORE, SLOTS, n), dtype)
     out = pl.pallas_call(
@@ -176,7 +176,7 @@
             + [pltpu.VMEM((QROWS, QROWS), BF), pltpu.VMEM((QUADS, QROWS // ROWS, ROWS, WIDTH), BF)]
             + [pltpu.SemaphoreType.DMA((QUADS,))],
         ),
-        out_shape=[jax.ShapeDtypeStruct(by_z, BF)] + [grads(n) for n in PARTS * 2],
+        out_shape=[jax.ShapeDtypeStruct(by_z, BF)] + [grads(n, i % 5 in (0, 3, 4)) for i, n in enumerate(PARTS * 2)],
         compiler_params=PARAMS,
         cost_estimate=cost(13_000_000_000, 26_000_000, 600_000),
     )(pos, rows, *a_in, *b_in)
@@ -207,10 +207,9 @@
     scale = 1.0 / math.sqrt(NY * NX * NC * NZ * ROWS * 8 / 64)
     y, x, c, z = (lax.axis_index(a) for a in ("y", "x", "c", "z"))
     pos = jnp.stack([y, x, c, (z * NC + c) * EXPERTS_CORE, 1 - 2 * c]).astype(jnp.int32)
-    ids, gates = expert_ids.T.astype(F32), gate_values.T.astype(F32)
-    first = jnp.arange(META)[:, None] < META // 2
-    meta = jnp.where(first, jnp.concatenate([ids, ids]), jnp.concatenate([gates, gates])).astype(BF)
-    meta = jnp.pad(meta, ((0, ROWS - META), (0, 0)))
+    ids = jnp.pad(expert_ids.T.astype(BF), ((0, ROWS - META // 2), (0, 0)))
+    gates = jnp.pad(gate_values.T, ((META // 2, ROWS - META), (0, 0)))
+    meta = jnp.maximum(ids, gates)
     rows = lax.all_gather(jnp.concatenate([tokens, out_grad, meta], axis=1), ("c", "z"), axis=0, tiled=True)
 
     def by_core(own, sister):

time: 161 us -> 160 us (level)
    unnamed x38 -> x26, local copies, waits for them, and re-layouts: 3.12 us -> 3.82 us
  transfers between devices with their start and end apart: 32 -> 32, of which waited for: 17 -> 16; matrix products, arithmetic and copies ran while one was open for 3% -> 3% of each run, Pallas kernels for 0% -> 0%
where the time goes in v4:
time: 160 us
  waiting for transfers between devices  60.7 us (38%)
  starting transfers between devices  52 us (32%)
  Pallas kernels  22.8 us (14%)
  between operations  14.3 us (9%)
  other arithmetic  5.38 us (3%)
  local copies, waits for them, and re-layouts  4.55 us (3%)
    ppermute x12, waiting for transfers between devices, step(): return lax.ppermute(value, (axis, 'c'), pairs)  29.4 us
    pallas_call x1, Pallas kernels, layer(): pl.pallas_call(lambda *refs: layer_kernel(scale, *refs), grid_spec=pltpu....  22.8 us
    ppermute x14, waiting for transfers between devices, shift(): return lax.ppermute(value, axis, [(i, (i + by) % n) for i in range(n)])  22.6 us
    ppermute x12, starting transfers between devices, step(): return lax.ppermute(value, (axis, 'c'), pairs)  20.3 us
    ppermute x14, starting transfers between devices, shift(): return lax.ppermute(value, axis, [(i, (i + by) % n) for i in range(n)])  20.1 us
    ppermute x4, starting transfers between devices, swap(): return lax.ppermute(value, 'c', [(0, 1), (1, 0)])  11.4 us
    all_gather x1, waiting for transfers between devices, shards(): lax.all_gather(jnp.concatenate([tokens, out_grad, meta], axis=1), ('c', '...  5.57 us
    unnamed x26, local copies, waits for them, and re-layouts  3.82 us
  transfers between devices with their start and end apart: 32, of which 16 were waited for; matrix products, arithmetic and copies ran while one was open for 3% of the time, Pallas kernels for 0%

profile of v4, /device:TPU:1, one launch (start us, length us, event | category | flops | bytes accessed | tf_op | source)
XLA Modules:
  0.0 159.7 jit_solution(15193028815573480815)
XLA Ops:
  8.0 1.9 %fusion.3 = bf16[128,2176]{1,0:T(8,128)(2,1)} fusion(bf16[8,128]{1,0:T(8,128)(2,1)} %bitcast.104, bf16[8,128]{1,0:T(8,128)(2,1)S(1)} %convert_bitcast_fusion, bf16[128,1024]{1,0:T(8,128)(2,1)} %param.7, bf16[128,1024]{1,0:T(8,128)(2,1)} %param.6), kind=kLoop, calls=%fused_computation.14 | loop fusion | flops 3063808 | bytes 1085440 | tf_op jit(solution)/shard_map/concatenate | solution.py:213
  10.1 3.3 %collective-permute-start = (bf16[2,4,32,384]{3,2,1,0:T(8,128)(2,1)S(1)}, bf16[2,4,32,384]{3,2,1,0:T(8,128)(2,1)S(1)}, u32[]{:S(2)}, u32[]{:S(2)}) collective-permute-start(bf16[2,4,32,384]{3,2,1,0:T(8,128)(2,1)S(1)} %pad_maximum_fusion.2), channel_id=1, source_target_pairs={{0,8},{8,0},{1,9},{9,1},{2,10},{10,2},{3,11},{11,3},{4,12},{12,4},... | collective-permute-start | bytes 589832 | tf_op jit(solution)/shard_map/ppermute | solution.py:29
  17.2 3.0 %collective-permute-start.8 = (bf16[4,64,384]{2,1,0:T(8,128)(2,1)S(1)}, bf16[4,64,384]{2,1,0:T(8,128)(2,1)S(1)}, u32[]{:S(2)}, u32[]{:S(2)}) collective-permute-start(bf16[4,64,384]{2,1,0:T(8,128)(2,1)S(1)} %get-tuple-element.45), channel_id=1, source_target_pairs={{0,128},{8,136},{64,192},{72,200},{128,0},{136,8},{192,64},{200,72... | collective-permute-start | bytes 589832 | tf_op jit(solution)/shard_map/ppermute | solution.py:35
  21.0 1.4 collective-permute-done.2
  22.4 2.6 %collective-permute-done.1 = bf16[4,64,384]{2,1,0:T(8,128)(2,1)S(1)} collective-permute-done((bf16[4,64,384]{2,1,0:T(8,128)(2,1)S(1)}, bf16[4,64,384]{2,1,0:T(8,128)(2,1)S(1)}, u32[]{:S(2)}, u32[]{:S(2)}) %collective-permute-start.1) | collective-permute-done | bytes 196640 | tf_op jit(solution)/shard_map/ppermute | solution.py:35
  25.0 2.4 %collective-permute-done.3 = bf16[4,64,384]{2,1,0:T(8,128)(2,1)S(1)} collective-permute-done((bf16[4,64,384]{2,1,0:T(8,128)(2,1)S(1)}, bf16[4,64,384]{2,1,0:T(8,128)(2,1)S(1)}, u32[]{:S(2)}, u32[]{:S(2)}) %collective-permute-start.3) | collective-permute-done | bytes 196640 | tf_op jit(solution)/shard_map/ppermute | solution.py:35
  30.7 1.7 %collective-permute-start.10 = (bf16[4,4,64,384]{3,2,1,0:T(8,128)(2,1)S(1)}, bf16[4,4,64,384]{3,2,1,0:T(8,128)(2,1)S(1)}, u32[]{:S(2)}, u32[]{:S(2)}) collective-permute-start(bf16[4,4,64,384]{3,2,1,0:T(8,128)(2,1)S(1)} %pad_maximum_fusion.1.refs_6_), channel_id=1, source_target_pairs={{0,16},{8,56},{16,32},{24,8},{32,48},{40,24},{48,0},{56,40},{1,17}... | collective-permute-start | bytes 2359304 | tf_op jit(solution)/shard_map/ppermute | solution.py:35
  32.4 7.3 %collective-permute-done.4.refs_3_ = bf16[4,4,64,384]{3,2,1,0:T(8,128)(2,1)S(1)} collective-permute-done((bf16[4,4,64,384]{3,2,1,0:T(8,128)(2,1)S(1)}, bf16[4,4,64,384]{3,2,1,0:T(8,128)(2,1)S(1)}, u32[]{:S(2)}, u32[]{:S(2)}) %collective-permute-start.4) | collective-permute-done | bytes 786464 | tf_op jit(solution)/shard_map/ppermute | solution.py:35
  39.6 2.2 %collective-permute-start.5 = (bf16[4,4,64,384]{3,2,1,0:T(8,128)(2,1)S(1)}, bf16[4,4,64,384]{3,2,1,0:T(8,128)(2,1)S(1)}, u32[]{:S(2)}, u32[]{:S(2)}) collective-permute-start(bf16[4,4,64,384]{3,2,1,0:T(8,128)(2,1)S(1)} %collective-permute-done.4.refs_3_), channel_id=1, source_target_pairs={{0,64},{8,200},{64,128},{72,8},{128,192},{136,72},{192,0},{200,136... | collective-permute-start | bytes 2359304 | tf_op jit(solution)/shard_map/ppermute | solution.py:35
  42.0 2.8 %collective-permute-start.11 = (bf16[4,4,64,384]{3,2,1,0:T(8,128)(2,1)S(1)}, bf16[4,4,64,384]{3,2,1,0:T(8,128)(2,1)S(1)}, u32[]{:S(2)}, u32[]{:S(2)}) collective-permute-start(bf16[4,4,64,384]{3,2,1,0:T(8,128)(2,1)S(1)} %collective-permute-done.10.refs_7_), channel_id=1, source_target_pairs={{0,16},{8,56},{16,32},{24,8},{32,48},{40,24},{48,0},{56,40},{1,17}... | collective-permute-start | bytes 2359304 | tf_op jit(solution)/shard_map/ppermute | solution.py:35
  44.8 6.0 %collective-permute-done.5.refs_4_ = bf16[4,4,64,384]{3,2,1,0:T(8,128)(2,1)S(1)} collective-permute-done((bf16[4,4,64,384]{3,2,1,0:T(8,128)(2,1)S(1)}, bf16[4,4,64,384]{3,2,1,0:T(8,128)(2,1)S(1)}, u32[]{:S(2)}, u32[]{:S(2)}) %collective-permute-start.5) | collective-permute-done | bytes 786464 | tf_op jit(solution)/shard_map/ppermute | solution.py:35
  50.9 3.4 %collective-permute-start.6 = (bf16[4,4,64,384]{3,2,1,0:T(8,128)(2,1)S(1)}, bf16[4,4,64,384]{3,2,1,0:T(8,128)(2,1)S(1)}, u32[]{:S(2)}, u32[]{:S(2)}) collective-permute-start(bf16[4,4,64,384]{3,2,1,0:T(8,128)(2,1)S(1)} %collective-permute-done.5.refs_4_), channel_id=1, source_target_pairs={{0,64},{8,200},{64,128},{72,8},{128,192},{136,72},{192,0},{200,136... | collective-permute-start | bytes 2359304 | tf_op jit(solution)/shard_map/ppermute | solution.py:35
  54.2 3.0 %collective-permute-start.12 = (bf16[4,4,64,384]{3,2,1,0:T(8,128)(2,1)S(1)}, bf16[4,4,64,384]{3,2,1,0:T(8,128)(2,1)S(1)}, u32[]{:S(2)}, u32[]{:S(2)}) collective-permute-start(bf16[4,4,64,384]{3,2,1,0:T(8,128)(2,1)S(1)} %collective-permute-done.11.refs_8_), channel_id=1, source_target_pairs={{0,16},{8,56},{16,32},{24,8},{32,48},{40,24},{48,0},{56,40},{1,17}... | collective-permute-start | bytes 2359304 | tf_op jit(solution)/shard_map/ppermute | solution.py:35
  57.9 5.3 %collective-permute-done.6.refs_5_ = bf16[4,4,64,384]{3,2,1,0:T(8,128)(2,1)S(1)} collective-permute-done((bf16[4,4,64,384]{3,2,1,0:T(8,128)(2,1)S(1)}, bf16[4,4,64,384]{3,2,1,0:T(8,128)(2,1)S(1)}, u32[]{:S(2)}, u32[]{:S(2)}) %collective-permute-start.6) | collective-permute-done | bytes 786464 | tf_op jit(solution)/shard_map/ppermute | solution.py:35
  63.2 3.0 %collective-permute-done.12.refs_9_ = bf16[4,4,64,384]{3,2,1,0:T(8,128)(2,1)S(1)} collective-permute-done((bf16[4,4,64,384]{3,2,1,0:T(8,128)(2,1)S(1)}, bf16[4,4,64,384]{3,2,1,0:T(8,128)(2,1)S(1)}, u32[]{:S(2)}, u32[]{:S(2)}) %collective-permute-start.12) | collective-permute-done | bytes 786464 | tf_op jit(solution)/shard_map/ppermute | solution.py:35
  67.1 5.6 %all-gather.2.cloned.1.call-done.refs_1_ = bf16[2048,2176]{1,0:T(8,128)(2,1)} async-done(((bf16[128,2176]{1,0:T(8,128)(2,1)}), bf16[2048,2176]{1,0:T(8,128)(2,1)}) %all-gather.2.cloned.1.call-update) | async-done | bytes 8912912 | tf_op jit(solution)/shard_map/all_gather | solution.py:213
  72.7 22.8 %shard_map.85 = (bf16[8,2,128,1024]{3,2,1,0:T(8,128)(2,1)}, bf16[4,4,64,384]{3,2,1,0:T(8,128)(2,1)S(1)}, bf16[4,4,64,384]{3,2,1,0:T(8,128)(2,1)}, bf16[4,4,64,38...) custom-call(s32[5]{0:T(128)} %stack.62.refs_0_, ...), custom_call_target="tpu_custom_call" | custom-call | flops 12999999488 | bytes 26000000 | tf_op jit(solution)/shard_map/pallas_call | solution.py:165
  95.5 1.3 collective-permute-start.14
  96.8 1.5 collective-permute-start.16
  99.5 1.5 collective-permute-start.24
  100.9 15.0 %collective-permute-done.14 = bf16[4,4,64,384]{3,2,1,0:T(8,128)(2,1)S(1)} collective-permute-done((bf16[4,4,64,384]{3,2,1,0:T(8,128)(2,1)}, bf16[4,4,64,384]{3,2,1,0:T(8,128)(2,1)S(1)}, u32[]{:S(2)}, u32[]{:S(2)}) %collective-permute-start.14) | collective-permute-done | bytes 786464 | tf_op jit(solution)/shard_map/ppermute | solution.py:40
  116.3 2.7 %collective-permute-start.18 = (bf16[2,4,64,384]{3,2,1,0:T(8,128)(2,1)S(1)}, bf16[2,4,64,384]{3,2,1,0:T(8,128)(2,1)S(1)}, u32[]{:S(2)}, u32[]{:S(2)}) collective-permute-start(bf16[2,4,64,384]{3,2,1,0:T(8,128)(2,1)S(1)} %add_convert_fusion.4), channel_id=1, source_target_pairs={{0,192},{64,0},{128,64},{192,128},{1,193},{65,1},{129,65},{193,129... | collective-permute-start | bytes 1179656 | tf_op jit(solution)/shard_map/ppermute | solution.py:40
  119.1 1.3 collective-permute-start.23
  120.5 1.5 collective-permute-start.26
  122.1 5.0 %collective-permute-done.15 = bf16[2,4,64,384]{3,2,1,0:T(8,128)(2,1)S(1)} collective-permute-done((bf16[2,4,64,384]{3,2,1,0:T(8,128)(2,1)S(1)}, bf16[2,4,64,384]{3,2,1,0:T(8,128)(2,1)S(1)}, u32[]{:S(2)}, u32[]{:S(2)}) %collective-permute-start.15) | collective-permute-done | bytes 393248 | tf_op jit(solution)/shard_map/ppermute | solution.py:40
  127.5 1.5 collective-permute-start.17
  129.1 2.5 %collective-permute-start.19 = (bf16[4,64,384]{2,1,0:T(8,128)(2,1)S(1)}, bf16[4,64,384]{2,1,0:T(8,128)(2,1)S(1)}, u32[]{:S(2)}, u32[]{:S(2)}) collective-permute-start(bf16[4,64,384]{2,1,0:T(8,128)(2,1)S(1)} %get-tuple-element.38), channel_id=1, source_target_pairs={{0,32},{16,48},{32,0},{48,16},{1,33},{17,49},{33,1},{49,17},{2,34}... | collective-permute-start | bytes 589832 | tf_op jit(solution)/shard_map/ppermute | solution.py:40
  133.2 3.8 %collective-permute-start.27 = (bf16[4,64,384]{2,1,0:T(8,128)(2,1)S(1)}, bf16[4,64,384]{2,1,0:T(8,128)(2,1)S(1)}, u32[]{:S(2)}, u32[]{:S(2)}) collective-permute-start(bf16[4,64,384]{2,1,0:T(8,128)(2,1)S(1)} %get-tuple-element.36), channel_id=1, source_target_pairs={{0,128},{64,192},{128,0},{192,64},{1,129},{65,193},{129,1},{193,65... | collective-permute-start | bytes 589832 | tf_op jit(solution)/shard_map/ppermute | solution.py:40
  137.0 1.4 collective-permute-done.19
  138.6 3.3 %collective-permute-start.21 = (bf16[4,32,384]{2,1,0:T(8,128)(2,1)S(1)}, bf16[4,32,384]{2,1,0:T(8,128)(2,1)S(1)}, u32[]{:S(2)}, u32[]{:S(2)}) collective-permute-start(bf16[4,32,384]{2,1,0:T(8,128)(2,1)S(1)} %select_convert_fusion.1), channel_id=1, source_target_pairs={{0,8},{8,0},{1,9},{9,1},{2,10},{10,2},{3,11},{11,3},{4,12},{12,4},... | collective-permute-start | bytes 294920 | tf_op jit(solution)/shard_map/ppermute | solution.py:29
  143.0 4.2 %collective-permute-start.29 = (bf16[4,32,384]{2,1,0:T(8,128)(2,1)S(1)}, bf16[4,32,384]{2,1,0:T(8,128)(2,1)S(1)}, u32[]{:S(2)}, u32[]{:S(2)}) collective-permute-start(bf16[4,32,384]{2,1,0:T(8,128)(2,1)S(1)} %select_convert_fusion), channel_id=1, source_target_pairs={{0,8},{8,0},{1,9},{9,1},{2,10},{10,2},{3,11},{11,3},{4,12},{12,4},... | collective-permute-start | bytes 294920 | tf_op jit(solution)/shard_map/ppermute | solution.py:29
  147.2 2.1 %reduce-scatter.2.cloned.1.call-done = bf16[1,2,128,1024]{3,2,1,0:T(8,128)(2,1)} async-done(((bf16[8,2,128,1024]{3,2,1,0:T(8,128)(2,1)}), bf16[1,2,128,1024]{3,2,1,0:T(8,128)(2,1)}) %reduce-scatter.2.cloned.1.call-update) | async-done | bytes 524304 | tf_op jit(solution)/shard_map/reduce_scatter | solution.py:229
  (90 shorter events, 19.1 us)
Async XLA Ops:
  7.2 65.5 %all-gather.2.cloned.1.call-start = ((), (), s32[]{:S(2)}) async-start(), calls=%async_computation.1 | async-start | bytes 9469952 | tf_op jit(solution)/shard_map/all_gather | solution.py:213
  9.9 139.4 %reduce-scatter.2.cloned.1.call-start = ((), (), s32[]{:S(2)}) async-start(), calls=%async_computation.2 | async-start | bytes 4718592 | tf_op jit(solution)/shard_map/reduce_scatter | solution.py:229
  10.1 4.4 %collective-permute-start = (bf16[2,4,32,384]{3,2,1,0:T(8,128)(2,1)S(1)}, bf16[2,4,32,384]{3,2,1,0:T(8,128)(2,1)S(1)}, u32[]{:S(2)}, u32[]{:S(2)}) collective-permute-start(bf16[2,4,32,384]{3,2,1,0:T(8,128)(2,1)S(1)} %pad_maximum_fusion.2), channel_id=1, source_target_pairs={{0,8},{8,0},{1,9},{9,1},{2,10},{10,2},{3,11},{11,3},{4,12},{12,4},... | collective-permute-start | bytes 589832 | tf_op jit(solution)/shard_map/ppermute | solution.py:29
  14.6 7.7 %collective-permute-start.2 = (bf16[4,64,384]{2,1,0:T(8,128)(2,1)S(1)}, bf16[4,64,384]{2,1,0:T(8,128)(2,1)S(1)}, u32[]{:S(2)}, u32[]{:S(2)}) collective-permute-start(bf16[4,64,384]{2,1,0:T(8,128)(2,1)S(1)} %get-tuple-element.49), channel_id=1, source_target_pairs={{0,32},{8,40},{16,48},{24,56},{32,0},{40,8},{48,16},{56,24},{1,33}... | collective-permute-start | bytes 589832 | tf_op jit(solution)/shard_map/ppermute | solution.py:35
  15.7 9.2 %collective-permute-start.1 = (bf16[4,64,384]{2,1,0:T(8,128)(2,1)S(1)}, bf16[4,64,384]{2,1,0:T(8,128)(2,1)S(1)}, u32[]{:S(2)}, u32[]{:S(2)}) collective-permute-start(bf16[4,64,384]{2,1,0:T(8,128)(2,1)S(1)} %get-tuple-element.49), channel_id=1, source_target_pairs={{0,16},{8,56},{16,32},{24,8},{32,48},{40,24},{48,0},{56,40},{1,17}... | collective-permute-start | bytes 589832 | tf_op jit(solution)/shard_map/ppermute | solution.py:35
  16.6 10.7 %collective-permute-start.3 = (bf16[4,64,384]{2,1,0:T(8,128)(2,1)S(1)}, bf16[4,64,384]{2,1,0:T(8,128)(2,1)S(1)}, u32[]{:S(2)}, u32[]{:S(2)}) collective-permute-start(bf16[4,64,384]{2,1,0:T(8,128)(2,1)S(1)} %get-tuple-element.49), channel_id=1, source_target_pairs={{0,48},{8,24},{16,0},{24,40},{32,16},{40,56},{48,32},{56,8},{1,49}... | collective-permute-start | bytes 589832 | tf_op jit(solution)/shard_map/ppermute | solution.py:35
  17.2 12.1 %collective-permute-start.8 = (bf16[4,64,384]{2,1,0:T(8,128)(2,1)S(1)}, bf16[4,64,384]{2,1,0:T(8,128)(2,1)S(1)}, u32[]{:S(2)}, u32[]{:S(2)}) collective-permute-start(bf16[4,64,384]{2,1,0:T(8,128)(2,1)S(1)} %get-tuple-element.45), channel_id=1, source_target_pairs={{0,128},{8,136},{64,192},{72,200},{128,0},{136,8},{192,64},{200,72... | collective-permute-start | bytes 589832 | tf_op jit(solution)/shard_map/ppermute | solution.py:35
  20.2 9.1 %collective-permute-start.7 = (bf16[4,64,384]{2,1,0:T(8,128)(2,1)S(1)}, bf16[4,64,384]{2,1,0:T(8,128)(2,1)S(1)}, u32[]{:S(2)}, u32[]{:S(2)}) collective-permute-start(bf16[4,64,384]{2,1,0:T(8,128)(2,1)S(1)} %get-tuple-element.45), channel_id=1, source_target_pairs={{0,64},{8,200},{64,128},{72,8},{128,192},{136,72},{192,0},{200,136... | collective-permute-start | bytes 589832 | tf_op jit(solution)/shard_map/ppermute | solution.py:35
  22.4 8.2 %collective-permute-start.9 = (bf16[4,64,384]{2,1,0:T(8,128)(2,1)S(1)}, bf16[4,64,384]{2,1,0:T(8,128)(2,1)S(1)}, u32[]{:S(2)}, u32[]{:S(2)}) collective-permute-start(bf16[4,64,384]{2,1,0:T(8,128)(2,1)S(1)} %get-tuple-element.45), channel_id=1, source_target_pairs={{0,192},{8,72},{64,0},{72,136},{128,64},{136,200},{192,128},{200,8... | collective-permute-start | bytes 589832 | tf_op jit(solution)/shard_map/ppermute | solution.py:35
  28.4 11.2 %collective-permute-start.4 = (bf16[4,4,64,384]{3,2,1,0:T(8,128)(2,1)S(1)}, bf16[4,4,64,384]{3,2,1,0:T(8,128)(2,1)S(1)}, u32[]{:S(2)}, u32[]{:S(2)}) collective-permute-start(bf16[4,4,64,384]{3,2,1,0:T(8,128)(2,1)S(1)} %pad_maximum_fusion.refs_2_), channel_id=1, source_target_pairs={{0,64},{8,200},{64,128},{72,8},{128,192},{136,72},{192,0},{200,136... | collective-permute-start | bytes 2359304 | tf_op jit(solution)/shard_map/ppermute | solution.py:35
  30.7 11.3 %collective-permute-start.10 = (bf16[4,4,64,384]{3,2,1,0:T(8,128)(2,1)S(1)}, bf16[4,4,64,384]{3,2,1,0:T(8,128)(2,1)S(1)}, u32[]{:S(2)}, u32[]{:S(2)}) collective-permute-start(bf16[4,4,64,384]{3,2,1,0:T(8,128)(2,1)S(1)} %pad_maximum_fusion.1.refs_6_), channel_id=1, source_target_pairs={{0,16},{8,56},{16,32},{24,8},{32,48},{40,24},{48,0},{56,40},{1,17}... | collective-permute-start | bytes 2359304 | tf_op jit(solution)/shard_map/ppermute | solution.py:35
  39.6 11.2 %collective-permute-start.5 = (bf16[4,4,64,384]{3,2,1,0:T(8,128)(2,1)S(1)}, bf16[4,4,64,384]{3,2,1,0:T(8,128)(2,1)S(1)}, u32[]{:S(2)}, u32[]{:S(2)}) collective-permute-start(bf16[4,4,64,384]{3,2,1,0:T(8,128)(2,1)S(1)} %collective-permute-done.4.refs_3_), channel_id=1, source_target_pairs={{0,64},{8,200},{64,128},{72,8},{128,192},{136,72},{192,0},{200,136... | collective-permute-start | bytes 2359304 | tf_op jit(solution)/shard_map/ppermute | solution.py:35
  42.0 12.2 %collective-permute-start.11 = (bf16[4,4,64,384]{3,2,1,0:T(8,128)(2,1)S(1)}, bf16[4,4,64,384]{3,2,1,0:T(8,128)(2,1)S(1)}, u32[]{:S(2)}, u32[]{:S(2)}) collective-permute-start(bf16[4,4,64,384]{3,2,1,0:T(8,128)(2,1)S(1)} %collective-permute-done.10.refs_7_), channel_id=1, source_target_pairs={{0,16},{8,56},{16,32},{24,8},{32,48},{40,24},{48,0},{56,40},{1,17}... | collective-permute-start | bytes 2359304 | tf_op jit(solution)/shard_map/ppermute | solution.py:35
  50.9 12.3 %collective-permute-start.6 = (bf16[4,4,64,384]{3,2,1,0:T(8,128)(2,1)S(1)}, bf16[4,4,64,384]{3,2,1,0:T(8,128)(2,1)S(1)}, u32[]{:S(2)}, u32[]{:S(2)}) collective-permute-start(bf16[4,4,64,384]{3,2,1,0:T(8,128)(2,1)S(1)} %collective-permute-done.5.refs_4_), channel_id=1, source_target_pairs={{0,64},{8,200},{64,128},{72,8},{128,192},{136,72},{192,0},{200,136... | collective-permute-start | bytes 2359304 | tf_op jit(solution)/shard_map/ppermute | solution.py:35
  54.2 12.0 %collective-permute-start.12 = (bf16[4,4,64,384]{3,2,1,0:T(8,128)(2,1)S(1)}, bf16[4,4,64,384]{3,2,1,0:T(8,128)(2,1)S(1)}, u32[]{:S(2)}, u32[]{:S(2)}) collective-permute-start(bf16[4,4,64,384]{3,2,1,0:T(8,128)(2,1)S(1)} %collective-permute-done.11.refs_8_), channel_id=1, source_target_pairs={{0,16},{8,56},{16,32},{24,8},{32,48},{40,24},{48,0},{56,40},{1,17}... | collective-permute-start | bytes 2359304 | tf_op jit(solution)/shard_map/ppermute | solution.py:35
  95.5 20.5 %collective-permute-start.14 = (bf16[4,4,64,384]{3,2,1,0:T(8,128)(2,1)}, bf16[4,4,64,384]{3,2,1,0:T(8,128)(2,1)S(1)}, u32[]{:S(2)}, u32[]{:S(2)}) collective-permute-start(bf16[4,4,64,384]{3,2,1,0:T(8,128)(2,1)} %get-tuple-element.17), channel_id=1, source_target_pairs={{0,64},{64,128},{128,192},{192,0},{1,65},{65,129},{129,193},{193,1... | collective-permute-start | bytes 2359304 | tf_op jit(solution)/shard_map/ppermute | solution.py:40
  96.8 19.4 %collective-permute-start.16 = (bf16[4,4,64,384]{3,2,1,0:T(8,128)(2,1)}, bf16[4,4,64,384]{3,2,1,0:T(8,128)(2,1)S(1)}, u32[]{:S(2)}, u32[]{:S(2)}) collective-permute-start(bf16[4,4,64,384]{3,2,1,0:T(8,128)(2,1)} %get-tuple-element.18), channel_id=1, source_target_pairs={{0,192},{64,0},{128,64},{192,128},{1,193},{65,1},{129,65},{193,129... | collective-permute-start | bytes 2359304 | tf_op jit(solution)/shard_map/ppermute | solution.py:40
  98.3 20.8 %collective-permute-start.22 = (bf16[4,4,64,384]{3,2,1,0:T(8,128)(2,1)}, bf16[4,4,64,384]{3,2,1,0:T(8,128)(2,1)S(1)}, u32[]{:S(2)}, u32[]{:S(2)}) collective-permute-start(bf16[4,4,64,384]{3,2,1,0:T(8,128)(2,1)} %get-tuple-element.22), channel_id=1, source_target_pairs={{0,16},{16,32},{32,48},{48,0},{1,17},{17,33},{33,49},{49,1},{2,18}... | collective-permute-start | bytes 2359304 | tf_op jit(solution)/shard_map/ppermute | solution.py:40
  99.5 21.0 %collective-permute-start.24 = (bf16[4,4,64,384]{3,2,1,0:T(8,128)(2,1)}, bf16[4,4,64,384]{3,2,1,0:T(8,128)(2,1)S(1)}, u32[]{:S(2)}, u32[]{:S(2)}) collective-permute-start(bf16[4,4,64,384]{3,2,1,0:T(8,128)(2,1)} %get-tuple-element.23), channel_id=1, source_target_pairs={{0,48},{16,0},{32,16},{48,32},{1,49},{17,1},{33,17},{49,33},{2,50}... | collective-permute-start | bytes 2359304 | tf_op jit(solution)/shard_map/ppermute | solution.py:40
  116.1 11.0 %collective-permute-start.15 = (bf16[2,4,64,384]{3,2,1,0:T(8,128)(2,1)S(1)}, bf16[2,4,64,384]{3,2,1,0:T(8,128)(2,1)S(1)}, u32[]{:S(2)}, u32[]{:S(2)}) collective-permute-start(bf16[2,4,64,384]{3,2,1,0:T(8,128)(2,1)S(1)} %add_convert_fusion.5), channel_id=1, source_target_pairs={{0,64},{64,128},{128,192},{192,0},{1,65},{65,129},{129,193},{193,1... | collective-permute-start | bytes 1179656 | tf_op jit(solution)/shard_map/ppermute | solution.py:40
  116.3 10.8 %collective-permute-start.18 = (bf16[2,4,64,384]{3,2,1,0:T(8,128)(2,1)S(1)}, bf16[2,4,64,384]{3,2,1,0:T(8,128)(2,1)S(1)}, u32[]{:S(2)}, u32[]{:S(2)}) collective-permute-start(bf16[2,4,64,384]{3,2,1,0:T(8,128)(2,1)S(1)} %add_convert_fusion.4), channel_id=1, source_target_pairs={{0,192},{64,0},{128,64},{192,128},{1,193},{65,1},{129,65},{193,129... | collective-permute-start | bytes 1179656 | tf_op jit(solution)/shard_map/ppermute | solution.py:40
  119.1 13.5 %collective-permute-start.23 = (bf16[2,4,64,384]{3,2,1,0:T(8,128)(2,1)S(1)}, bf16[2,4,64,384]{3,2,1,0:T(8,128)(2,1)S(1)}, u32[]{:S(2)}, u32[]{:S(2)}) collective-permute-start(bf16[2,4,64,384]{3,2,1,0:T(8,128)(2,1)S(1)} %add_convert_fusion.2), channel_id=1, source_target_pairs={{0,16},{16,32},{32,48},{48,0},{1,17},{17,33},{33,49},{49,1},{2,18}... | collective-permute-start | bytes 1179656 | tf_op jit(solution)/shard_map/ppermute | solution.py:40
  120.5 12.1 %collective-permute-start.26 = (bf16[2,4,64,384]{3,2,1,0:T(8,128)(2,1)S(1)}, bf16[2,4,64,384]{3,2,1,0:T(8,128)(2,1)S(1)}, u32[]{:S(2)}, u32[]{:S(2)}) collective-permute-start(bf16[2,4,64,384]{3,2,1,0:T(8,128)(2,1)S(1)} %add_convert_fusion.1), channel_id=1, source_target_pairs={{0,48},{16,0},{32,16},{48,32},{1,49},{17,1},{33,17},{49,33},{2,50}... | collective-permute-start | bytes 1179656 | tf_op jit(solution)/shard_map/ppermute | solution.py:40
  127.5 9.6 %collective-permute-start.17 = (bf16[4,64,384]{2,1,0:T(8,128)(2,1)S(1)}, bf16[4,64,384]{2,1,0:T(8,128)(2,1)S(1)}, u32[]{:S(2)}, u32[]{:S(2)}) collective-permute-start(bf16[4,64,384]{2,1,0:T(8,128)(2,1)S(1)} %fusion.12), channel_id=1, source_target_pairs={{0,16},{16,32},{32,48},{48,0},{1,17},{17,33},{33,49},{49,1},{2,18}... | collective-permute-start | bytes 589832 | tf_op jit(solution)/shard_map/ppermute | solution.py:40
  129.1 9.4 %collective-permute-start.19 = (bf16[4,64,384]{2,1,0:T(8,128)(2,1)S(1)}, bf16[4,64,384]{2,1,0:T(8,128)(2,1)S(1)}, u32[]{:S(2)}, u32[]{:S(2)}) collective-permute-start(bf16[4,64,384]{2,1,0:T(8,128)(2,1)S(1)} %get-tuple-element.38), channel_id=1, source_target_pairs={{0,32},{16,48},{32,0},{48,16},{1,33},{17,49},{33,1},{49,17},{2,34}... | collective-permute-start | bytes 589832 | tf_op jit(solution)/shard_map/ppermute | solution.py:40
  131.5 6.9 %collective-permute-start.20 = (bf16[4,64,384]{2,1,0:T(8,128)(2,1)S(1)}, bf16[4,64,384]{2,1,0:T(8,128)(2,1)S(1)}, u32[]{:S(2)}, u32[]{:S(2)}) collective-permute-start(bf16[4,64,384]{2,1,0:T(8,128)(2,1)S(1)} %get-tuple-element.39), channel_id=1, source_target_pairs={{0,48},{16,0},{32,16},{48,32},{1,49},{17,1},{33,17},{49,33},{2,50}... | collective-permute-start | bytes 589832 | tf_op jit(solution)/shard_map/ppermute | solution.py:40
  133.1 8.8 %collective-permute-start.25 = (bf16[4,64,384]{2,1,0:T(8,128)(2,1)S(1)}, bf16[4,64,384]{2,1,0:T(8,128)(2,1)S(1)}, u32[]{:S(2)}, u32[]{:S(2)}) collective-permute-start(bf16[4,64,384]{2,1,0:T(8,128)(2,1)S(1)} %fusion.13), channel_id=1, source_target_pairs={{0,64},{64,128},{128,192},{192,0},{1,65},{65,129},{129,193},{193,1... | collective-permute-start | bytes 589832 | tf_op jit(solution)/shard_map/ppermute | solution.py:40
  133.2 9.7 %collective-permute-start.27 = (bf16[4,64,384]{2,1,0:T(8,128)(2,1)S(1)}, bf16[4,64,384]{2,1,0:T(8,128)(2,1)S(1)}, u32[]{:S(2)}, u32[]{:S(2)}) collective-permute-start(bf16[4,64,384]{2,1,0:T(8,128)(2,1)S(1)} %get-tuple-element.36), channel_id=1, source_target_pairs={{0,128},{64,192},{128,0},{192,64},{1,129},{65,193},{129,1},{193,65... | collective-permute-start | bytes 589832 | tf_op jit(solution)/shard_map/ppermute | solution.py:40
  137.0 5.9 %collective-permute-start.28 = (bf16[4,64,384]{2,1,0:T(8,128)(2,1)S(1)}, bf16[4,64,384]{2,1,0:T(8,128)(2,1)S(1)}, u32[]{:S(2)}, u32[]{:S(2)}) collective-permute-start(bf16[4,64,384]{2,1,0:T(8,128)(2,1)S(1)} %get-tuple-element.37), channel_id=1, source_target_pairs={{0,192},{64,0},{128,64},{192,128},{1,193},{65,1},{129,65},{193,129... | collective-permute-start | bytes 589832 | tf_op jit(solution)/shard_map/ppermute | solution.py:40
  138.6 11.3 %collective-permute-start.21 = (bf16[4,32,384]{2,1,0:T(8,128)(2,1)S(1)}, bf16[4,32,384]{2,1,0:T(8,128)(2,1)S(1)}, u32[]{:S(2)}, u32[]{:S(2)}) collective-permute-start(bf16[4,32,384]{2,1,0:T(8,128)(2,1)S(1)} %select_convert_fusion.1), channel_id=1, source_target_pairs={{0,8},{8,0},{1,9},{9,1},{2,10},{10,2},{3,11},{11,3},{4,12},{12,4},... | collective-permute-start | bytes 294920 | tf_op jit(solution)/shard_map/ppermute | solution.py:29
  143.0 7.9 %collective-permute-start.29 = (bf16[4,32,384]{2,1,0:T(8,128)(2,1)S(1)}, bf16[4,32,384]{2,1,0:T(8,128)(2,1)S(1)}, u32[]{:S(2)}, u32[]{:S(2)}) collective-permute-start(bf16[4,32,384]{2,1,0:T(8,128)(2,1)S(1)} %select_convert_fusion), channel_id=1, source_target_pairs={{0,8},{8,0},{1,9},{9,1},{2,10},{10,2},{3,11},{11,3},{4,12},{12,4},... | collective-permute-start | bytes 294920 | tf_op jit(solution)/shard_map/ppermute | solution.py:29
  149.3 2.7 %collective-permute-start.13 = (bf16[2,128,1024]{2,1,0:T(8,128)(2,1)}, bf16[2,128,1024]{2,1,0:T(8,128)(2,1)S(1)}, u32[]{:S(2)}, u32[]{:S(2)}) collective-permute-start(bf16[2,128,1024]{2,1,0:T(8,128)(2,1)} %bitcast.97), channel_id=1, source_target_pairs={{0,8},{8,0},{1,9},{9,1},{2,10},{10,2},{3,11},{11,3},{4,12},{12,4},... | collective-permute-start | bytes 1572872 | tf_op jit(solution)/shard_map/ppermute | solution.py:29
  (11 other events, 59.1 us)
Sparse Core Ops, SparseCore 0:
  10.0 62.5 all-gather.1
  95.6 53.6 reduce-scatter.1

commit v5 on v4

--- a/solution.py
+++ b/solution.py
@@ -61,8 +61,8 @@
 
 def layer_kernel(scale, pos, rows, *refs):
     a_in, b_in = refs[0:4], refs[4:8]
-    sums, a_out, b_out = refs[8], refs[9:14], refs[14:19]
-    wg, wd, term, xg, gg, weighting, slot_grad, srow, before, totals, sems = refs[19:]
+    sums, a_out, gg_out, scaled_out = refs[8], refs[9:14], refs[14], refs[15]
+    wg, wd, term, xg, gg, weighting, slot_grad, srow, before, totals, sems = refs[16:]
     n = QROWS // ROWS
     out_copies = [
         pltpu.make_async_copy(totals.at[q], sums.at[pl.ds(q * n % NZ, n), q * n // NZ], sems.at[q]) for q in range(QUADS)
@@ -104,7 +104,7 @@
     @pl.when(step_id >= QUADS)
     def _():
         e = step_id - QUADS
-        values = expert_step(pos, e, a_in, b_in, wg, wd, xg, gg, weighting, slot_grad)
+        grad, scaled = expert_step(pos, e, a_in, b_in, wg, wd, xg, gg, weighting, slot_grad)
 
         @pl.when(e == EXPERTS_CORE - 1)
         def _():
@@ -113,18 +113,49 @@
                 totals[q] = total.reshape(n, ROWS, WIDTH)
                 out_copies[q].start()
 
-        for rows_in, value, out, y_first in zip((xg, gg), values, (a_out, b_out), (True, False)):
-            term[...] = (dot(rows_in[e], value, (0, 0)) * scale).astype(BF)
-            for k in range(4):
-                for j in range(4):
-                    piece = term[pl.ds(row_of(pos, *((k, j) if y_first else (j, k))), PIECE), :]
-                    to, at = place(k, j)
-                    out[to][at, 0] = piece
+        gg_out[0] = gg[e]
+        scaled_out[0] = scaled
+        write_terms(scale, pos, xg[e], grad, a_out, term, True)
 
     @pl.when(step_id == QUADS + EXPERTS_CORE - 1)
     def _():
         for copy in out_copies:
             copy.wait()
+
+
+def write_terms(scale, pos, rows, value, out, term, y_first):
+    term[...] = (dot(rows, value, (0, 0)) * scale).astype(BF)
+    for k in range(4):
+        for j in range(4):
+            piece = term[pl.ds(row_of(pos, *((k, j) if y_first else (j, k))), PIECE), :]
+            to, at = place(k, j)
+            out[to][at, 0] = piece
+
+
+def down_kernel(scale, pos, gg, scaled, *refs):
+    write_terms(scale, pos, gg[0], scaled[0], refs[:5], refs[5], False)
+
+
+def grads_of(i):
+    kind = pltpu.VMEM if i in (0, 3, 4) else jax.ShapeDtypeStruct
+    return kind((PARTS[i], EXPERTS_CORE, PIECE, HID), BF)
+
+
+def down_terms(scale, pos, gg, scaled):
+    slots = lambda n: pl.BlockSpec((1, SLOTS, n), lambda e, p: (e, 0, 0))
+    return pl.pallas_call(
+        lambda *refs: down_kernel(scale, *refs),
+        grid_spec=pltpu.PrefetchScalarGridSpec(
+            num_scalar_prefetch=1,
+            grid=(EXPERTS_CORE,),
+            in_specs=[slots(WIDTH), slots(HID)],
+            out_specs=[pl.BlockSpec((n, 1, PIECE, HID), lambda e, p: (0, e, 0, 0)) for n in PARTS],
+            scratch_shapes=[pltpu.VMEM((WIDTH, HID), BF)],
+        ),
+        out_shape=[grads_of(i) for i in range(5)],
+        compiler_params=PARAMS,
+        cost_estimate=cost(2_000_000_000, 7_000_000),
+    )(pos, gg, scaled)
 
 
 def place(k, j):
@@ -159,7 +190,7 @@
 def layer(scale, pos, rows, a_in, b_in):
     expert = lambda i: jnp.maximum(i - QUADS, 0)
     piece = lambda n: pl.BlockSpec((n, 1, PIECE, HID), lambda i, p: (0, expert(i), 0, 0))
-    grads = lambda n, near: (pltpu.VMEM if near else jax.ShapeDtypeStruct)((n, EXPERTS_CORE, PIECE, HID), BF)
+    slots_out = lambda n: pl.BlockSpec((1, SLOTS, n), lambda i, p: (expert(i), 0, 0))
     by_z = (NZ, NC, ROWS, WIDTH)
     slots = lambda n, dtype: pltpu.VMEM((EXPERTS_CORE, SLOTS, n), dtype)
     out = pl.pallas_call(
@@ -169,18 +200,19 @@
             grid=(QUADS + EXPERTS_CORE,),
             in_specs=[pl.BlockSpec((QROWS, rows.shape[1]), lambda i, p: (jnp.minimum(i, QUADS - 1), 0))]
             + [piece(4)] * 8,
-            out_specs=[ANYWHERE] + [piece(n) for n in PARTS * 2],
+            out_specs=[ANYWHERE] + [piece(n) for n in PARTS] + [slots_out(WIDTH), slots_out(HID)],
             scratch_shapes=[pltpu.VMEM((WIDTH, HID), BF)] * 3
             + [slots(WIDTH, BF), slots(WIDTH, BF), slots(128, F32)]
             + [pltpu.VMEM((QUADS, EXPERTS_CORE * QSLOTS, WIDTH), BF), pltpu.VMEM((QUADS, 8, QROWS), F32)]
             + [pltpu.VMEM((QROWS, QROWS), BF), pltpu.VMEM((QUADS, QROWS // ROWS, ROWS, WIDTH), BF)]
             + [pltpu.SemaphoreType.DMA((QUADS,))],
         ),
-        out_shape=[jax.ShapeDtypeStruct(by_z, BF)] + [grads(n, i % 5 in (0, 3, 4)) for i, n in enumerate(PARTS * 2)],
+        out_shape=[jax.ShapeDtypeStruct(by_z, BF)] + [grads_of(i) for i in range(5)]
+        + [jax.ShapeDtypeStruct((EXPERTS_CORE, SLOTS, n), BF) for n in (WIDTH, HID)],
         compiler_params=PARAMS,
         cost_estimate=cost(13_000_000_000, 26_000_000, 600_000),
     )(pos, rows, *a_in, *b_in)
-    return out[0], out[1:6], out[6:11]
+    return out[0], out[1:6], out[6], out[7]
 
 
 def gather_plane(own, first, second):
@@ -225,7 +257,8 @@
     own_b = jnp.concatenate(by_core(keep_b, got[1]), axis=1)
     a_in = gather_plane(own_a, "x", "y")
     b_in = gather_plane(own_b, "y", "x")
-    sums, a_out, b_out = layer(scale, pos, rows, a_in, b_in)
+    sums, a_out, gg, scaled = layer(scale, pos, rows, a_in, b_in)
+    b_out = down_terms(scale, pos, gg, scaled)
     part = lax.psum_scatter(sums, "z", scatter_dimension=0)
     got = swap(part)
     input_grad = jnp.where(c == 0, part[0].astype(F32) + got[0].astype(F32), part[1].astype(F32) + got[1].astype(F32)).astype(BF)

time: 160 us -> 164 us (1.025)
  Pallas kernels: 22.8 us -> 27.5 us
  waiting for transfers between devices: 60.7 us -> 57.5 us
  starting transfers between devices: 52 us -> 54.7 us
    pallas_call x0 -> x1, Pallas kernels: none -> 6.37 us  [down_terms(): pl.pallas_call(lambda *refs: down_kernel(scale, *refs), grid_spec=pltpu.P...]
    ppermute x4, starting transfers between devices: 11.4 us -> 14.1 us  [swap(): return lax.ppermute(value, 'c', [(0, 1), (1, 0)])]
    reduce_scatter x1, waiting for transfers between devices: 2.06 us -> 0.01 us  [shards(): part = lax.psum_scatter(sums, 'z', scatter_dimension=0)]
    ppermute x14, waiting for transfers between devices: 22.6 us -> 20.6 us  [shift(): return lax.ppermute(value, axis, [(i, (i + by) % n) for i in range(n)])]
    pallas_call x1, Pallas kernels: 22.8 us -> 21.1 us  [layer(): pl.pallas_call(lambda *refs: layer_kernel(scale, *refs), grid_spec=pltpu....]
  transfers between devices with their start and end apart: 32 -> 32, of which waited for: 16 -> 18; matrix products, arithmetic and copies ran while one was open for 3% -> 3% of each run, Pallas kernels for 0% -> 4%
where the time goes in v5:
time: 164 us; the launch traced here: 163 us
  waiting for transfers between devices  57.5 us (35%)
  starting transfers between devices  54.7 us (33%)
  Pallas kernels  27.5 us (17%)
  between operations  14.4 us (9%)
  other arithmetic  5.36 us (3%)
  local copies, waits for them, and re-layouts  3.89 us (2%)
    ppermute x12, waiting for transfers between devices, step(): return lax.ppermute(value, (axis, 'c'), pairs)  29.3 us
    ppermute x12, starting transfers between devices, step(): return lax.ppermute(value, (axis, 'c'), pairs)  21.3 us
    pallas_call x1, Pallas kernels, layer(): pl.pallas_call(lambda *refs: layer_kernel(scale, *refs), grid_spec=pltpu....  21.1 us
    ppermute x14, waiting for transfers between devices, shift(): return lax.ppermute(value, axis, [(i, (i + by) % n) for i in range(n)])  20.6 us
    ppermute x14, starting transfers between devices, shift(): return lax.ppermute(value, axis, [(i, (i + by) % n) for i in range(n)])  19.3 us
    ppermute x4, starting transfers between devices, swap(): return lax.ppermute(value, 'c', [(0, 1), (1, 0)])  14.1 us
    all_gather x1, waiting for transfers between devices, shards(): lax.all_gather(jnp.concatenate([tokens, out_grad, meta], axis=1), ('c', '...  6.46 us
    pallas_call x1, Pallas kernels, down_terms(): pl.pallas_call(lambda *refs: down_kernel(scale, *refs), grid_spec=pltpu.P...  6.37 us
  transfers between devices with their start and end apart: 32, of which 18 were waited for; matrix products, arithmetic and copies ran while one was open for 3% of the time, Pallas kernels for 4%

profile of v5, /device:TPU:1, one launch (start us, length us, event | category | flops | bytes accessed | tf_op | source)
XLA Modules:
  0.0 163.3 jit_solution(7149375289059591491)
XLA Ops:
  8.0 1.9 %fusion.3 = bf16[128,2176]{1,0:T(8,128)(2,1)} fusion(bf16[8,128]{1,0:T(8,128)(2,1)} %bitcast.104, bf16[8,128]{1,0:T(8,128)(2,1)S(1)} %convert_bitcast_fusion, bf16[128,1024]{1,0:T(8,128)(2,1)} %param.7, bf16[128,1024]{1,0:T(8,128)(2,1)} %param.6), kind=kLoop, calls=%fused_computation.14 | loop fusion | flops 3063808 | bytes 1085440 | tf_op jit(solution)/shard_map/concatenate | solution.py:245
  10.2 3.3 %collective-permute-start = (bf16[2,4,32,384]{3,2,1,0:T(8,128)(2,1)S(1)}, bf16[2,4,32,384]{3,2,1,0:T(8,128)(2,1)S(1)}, u32[]{:S(2)}, u32[]{:S(2)}) collective-permute-start(bf16[2,4,32,384]{3,2,1,0:T(8,128)(2,1)S(1)} %pad_maximum_fusion.2), channel_id=1, source_target_pairs={{0,8},{8,0},{1,9},{9,1},{2,10},{10,2},{3,11},{11,3},{4,12},{12,4},... | collective-permute-start | bytes 589832 | tf_op jit(solution)/shard_map/ppermute | solution.py:29
  17.3 3.0 %collective-permute-start.8 = (bf16[4,64,384]{2,1,0:T(8,128)(2,1)S(1)}, bf16[4,64,384]{2,1,0:T(8,128)(2,1)S(1)}, u32[]{:S(2)}, u32[]{:S(2)}) collective-permute-start(bf16[4,64,384]{2,1,0:T(8,128)(2,1)S(1)} %get-tuple-element.49), channel_id=1, source_target_pairs={{0,128},{8,136},{64,192},{72,200},{128,0},{136,8},{192,64},{200,72... | collective-permute-start | bytes 589832 | tf_op jit(solution)/shard_map/ppermute | solution.py:35
  21.0 1.4 collective-permute-done.2
  22.4 2.6 %collective-permute-done.1 = bf16[4,64,384]{2,1,0:T(8,128)(2,1)S(1)} collective-permute-done((bf16[4,64,384]{2,1,0:T(8,128)(2,1)S(1)}, bf16[4,64,384]{2,1,0:T(8,128)(2,1)S(1)}, u32[]{:S(2)}, u32[]{:S(2)}) %collective-permute-start.1) | collective-permute-done | bytes 196640 | tf_op jit(solution)/shard_map/ppermute | solution.py:35
  25.0 2.4 %collective-permute-done.3 = bf16[4,64,384]{2,1,0:T(8,128)(2,1)S(1)} collective-permute-done((bf16[4,64,384]{2,1,0:T(8,128)(2,1)S(1)}, bf16[4,64,384]{2,1,0:T(8,128)(2,1)S(1)}, u32[]{:S(2)}, u32[]{:S(2)}) %collective-permute-start.3) | collective-permute-done | bytes 196640 | tf_op jit(solution)/shard_map/ppermute | solution.py:35
  28.5 2.0 %collective-permute-done.9 = bf16[4,64,384]{2,1,0:T(8,128)(2,1)S(1)} collective-permute-done((bf16[4,64,384]{2,1,0:T(8,128)(2,1)S(1)}, bf16[4,64,384]{2,1,0:T(8,128)(2,1)S(1)}, u32[]{:S(2)}, u32[]{:S(2)}) %collective-permute-start.9) | collective-permute-done | bytes 196640 | tf_op jit(solution)/shard_map/ppermute | solution.py:35
  30.7 1.7 %collective-permute-start.10 = (bf16[4,4,64,384]{3,2,1,0:T(8,128)(2,1)S(1)}, bf16[4,4,64,384]{3,2,1,0:T(8,128)(2,1)S(1)}, u32[]{:S(2)}, u32[]{:S(2)}) collective-permute-start(bf16[4,4,64,384]{3,2,1,0:T(8,128)(2,1)S(1)} %pad_maximum_fusion.1.refs_6_), channel_id=1, source_target_pairs={{0,16},{8,56},{16,32},{24,8},{32,48},{40,24},{48,0},{56,40},{1,17}... | collective-permute-start | bytes 2359304 | tf_op jit(solution)/shard_map/ppermute | solution.py:35
  32.4 6.5 %collective-permute-done.4.refs_3_ = bf16[4,4,64,384]{3,2,1,0:T(8,128)(2,1)S(1)} collective-permute-done((bf16[4,4,64,384]{3,2,1,0:T(8,128)(2,1)S(1)}, bf16[4,4,64,384]{3,2,1,0:T(8,128)(2,1)S(1)}, u32[]{:S(2)}, u32[]{:S(2)}) %collective-permute-start.4) | collective-permute-done | bytes 786464 | tf_op jit(solution)/shard_map/ppermute | solution.py:35
  38.9 2.4 %collective-permute-start.5 = (bf16[4,4,64,384]{3,2,1,0:T(8,128)(2,1)S(1)}, bf16[4,4,64,384]{3,2,1,0:T(8,128)(2,1)S(1)}, u32[]{:S(2)}, u32[]{:S(2)}) collective-permute-start(bf16[4,4,64,384]{3,2,1,0:T(8,128)(2,1)S(1)} %collective-permute-done.4.refs_3_), channel_id=1, source_target_pairs={{0,64},{8,200},{64,128},{72,8},{128,192},{136,72},{192,0},{200,136... | collective-permute-start | bytes 2359304 | tf_op jit(solution)/shard_map/ppermute | solution.py:35
  42.0 2.8 %collective-permute-start.11 = (bf16[4,4,64,384]{3,2,1,0:T(8,128)(2,1)S(1)}, bf16[4,4,64,384]{3,2,1,0:T(8,128)(2,1)S(1)}, u32[]{:S(2)}, u32[]{:S(2)}) collective-permute-start(bf16[4,4,64,384]{3,2,1,0:T(8,128)(2,1)S(1)} %collective-permute-done.10.refs_7_), channel_id=1, source_target_pairs={{0,16},{8,56},{16,32},{24,8},{32,48},{40,24},{48,0},{56,40},{1,17}... | collective-permute-start | bytes 2359304 | tf_op jit(solution)/shard_map/ppermute | solution.py:35
  44.8 5.4 %collective-permute-done.5.refs_4_ = bf16[4,4,64,384]{3,2,1,0:T(8,128)(2,1)S(1)} collective-permute-done((bf16[4,4,64,384]{3,2,1,0:T(8,128)(2,1)S(1)}, bf16[4,4,64,384]{3,2,1,0:T(8,128)(2,1)S(1)}, u32[]{:S(2)}, u32[]{:S(2)}) %collective-permute-start.5) | collective-permute-done | bytes 786464 | tf_op jit(solution)/shard_map/ppermute | solution.py:35
  50.2 3.5 %collective-permute-start.6 = (bf16[4,4,64,384]{3,2,1,0:T(8,128)(2,1)S(1)}, bf16[4,4,64,384]{3,2,1,0:T(8,128)(2,1)}, u32[]{:S(2)}, u32[]{:S(2)}) collective-permute-start(bf16[4,4,64,384]{3,2,1,0:T(8,128)(2,1)S(1)} %collective-permute-done.5.refs_4_), channel_id=1, source_target_pairs={{0,64},{8,200},{64,128},{72,8},{128,192},{136,72},{192,0},{200,136... | collective-permute-start | bytes 2359304 | tf_op jit(solution)/shard_map/ppermute | solution.py:35
  53.8 3.5 %collective-permute-start.12 = (bf16[4,4,64,384]{3,2,1,0:T(8,128)(2,1)S(1)}, bf16[4,4,64,384]{3,2,1,0:T(8,128)(2,1)}, u32[]{:S(2)}, u32[]{:S(2)}) collective-permute-start(bf16[4,4,64,384]{3,2,1,0:T(8,128)(2,1)S(1)} %collective-permute-done.11.refs_8_), channel_id=1, source_target_pairs={{0,16},{8,56},{16,32},{24,8},{32,48},{40,24},{48,0},{56,40},{1,17}... | collective-permute-start | bytes 2359304 | tf_op jit(solution)/shard_map/ppermute | solution.py:35
  57.9 4.7 %collective-permute-done.6.refs_5_ = bf16[4,4,64,384]{3,2,1,0:T(8,128)(2,1)} collective-permute-done((bf16[4,4,64,384]{3,2,1,0:T(8,128)(2,1)S(1)}, bf16[4,4,64,384]{3,2,1,0:T(8,128)(2,1)}, u32[]{:S(2)}, u32[]{:S(2)}) %collective-permute-start.6) | collective-permute-done | bytes 786464 | tf_op jit(solution)/shard_map/ppermute | solution.py:35
  62.6 3.6 %collective-permute-done.12.refs_9_ = bf16[4,4,64,384]{3,2,1,0:T(8,128)(2,1)} collective-permute-done((bf16[4,4,64,384]{3,2,1,0:T(8,128)(2,1)S(1)}, bf16[4,4,64,384]{3,2,1,0:T(8,128)(2,1)}, u32[]{:S(2)}, u32[]{:S(2)}) %collective-permute-start.12) | collective-permute-done | bytes 786464 | tf_op jit(solution)/shard_map/ppermute | solution.py:35
  66.2 6.5 %all-gather.2.cloned.1.call-done.refs_1_ = bf16[2048,2176]{1,0:T(8,128)(2,1)} async-done(((bf16[128,2176]{1,0:T(8,128)(2,1)}), bf16[2048,2176]{1,0:T(8,128)(2,1)}) %all-gather.2.cloned.1.call-update) | async-done | bytes 8912912 | tf_op jit(solution)/shard_map/all_gather | solution.py:245
  72.7 21.1 %shard_map.85 = (bf16[8,2,128,1024]{3,2,1,0:T(8,128)(2,1)}, bf16[4,4,64,384]{3,2,1,0:T(8,128)(2,1)S(1)}, bf16[4,4,64,384]{3,2,1,0:T(8,128)(2,1)}, bf16[4,4,64,38...) custom-call(s32[5]{0:T(128)} %stack.62.refs_0_, ...), custom_call_target="tpu_custom_call" | custom-call | flops 12999999488 | bytes 26000000 | tf_op jit(solution)/shard_map/pallas_call | solution.py:196
  96.1 1.5 collective-permute-start.16
  97.6 6.4 %shard_map.86 = (bf16[4,4,64,384]{3,2,1,0:T(8,128)(2,1)S(1)}, bf16[4,4,64,384]{3,2,1,0:T(8,128)(2,1)}, bf16[4,4,64,384]{3,2,1,0:T(8,128)(2,1)}, bf16[2,4,64,384]...) custom-call(s32[5]{0:T(128)} %stack.62.refs_0_, bf16[4,320,1024]{2,1,0:T(8,128)(2,1)} %get-tuple-element.22.refs_1_, ...), custom_call_target="tpu_custom_call" | custom-call | flops 2000000000 | bytes 7000000 | tf_op jit(solution)/shard_map/pallas_call | solution.py:146
  105.2 1.5 collective-permute-start.24
  106.7 8.4 %collective-permute-done.14 = bf16[4,4,64,384]{3,2,1,0:T(8,128)(2,1)S(1)} collective-permute-done((bf16[4,4,64,384]{3,2,1,0:T(8,128)(2,1)S(1)}, bf16[4,4,64,384]{3,2,1,0:T(8,128)(2,1)S(1)}, u32[]{:S(2)}, u32[]{:S(2)}) %collective-permute-start.14) | collective-permute-done | bytes 786464 | tf_op jit(solution)/shard_map/ppermute | solution.py:40
  115.4 2.7 %collective-permute-start.18 = (bf16[2,4,64,384]{3,2,1,0:T(8,128)(2,1)S(1)}, bf16[2,4,64,384]{3,2,1,0:T(8,128)(2,1)S(1)}, u32[]{:S(2)}, u32[]{:S(2)}) collective-permute-start(bf16[2,4,64,384]{3,2,1,0:T(8,128)(2,1)S(1)} %add_convert_fusion.4), channel_id=1, source_target_pairs={{0,192},{64,0},{128,64},{192,128},{1,193},{65,1},{129,65},{193,129... | collective-permute-start | bytes 1179656 | tf_op jit(solution)/shard_map/ppermute | solution.py:40
  118.2 5.6 %collective-permute-done.22 = bf16[4,4,64,384]{3,2,1,0:T(8,128)(2,1)S(1)} collective-permute-done((bf16[4,4,64,384]{3,2,1,0:T(8,128)(2,1)}, bf16[4,4,64,384]{3,2,1,0:T(8,128)(2,1)S(1)}, u32[]{:S(2)}, u32[]{:S(2)}) %collective-permute-start.22) | collective-permute-done | bytes 786464 | tf_op jit(solution)/shard_map/ppermute | solution.py:40
  124.1 2.9 %collective-permute-start.26 = (bf16[2,4,64,384]{3,2,1,0:T(8,128)(2,1)S(1)}, bf16[2,4,64,384]{3,2,1,0:T(8,128)(2,1)S(1)}, u32[]{:S(2)}, u32[]{:S(2)}) collective-permute-start(bf16[2,4,64,384]{3,2,1,0:T(8,128)(2,1)S(1)} %add_convert_fusion.1), channel_id=1, source_target_pairs={{0,48},{16,0},{32,16},{48,32},{1,49},{17,1},{33,17},{49,33},{2,50}... | collective-permute-start | bytes 1179656 | tf_op jit(solution)/shard_map/ppermute | solution.py:40
  128.0 2.5 %collective-permute-start.19 = (bf16[4,64,384]{2,1,0:T(8,128)(2,1)S(1)}, bf16[4,64,384]{2,1,0:T(8,128)(2,1)S(1)}, u32[]{:S(2)}, u32[]{:S(2)}) collective-permute-start(bf16[4,64,384]{2,1,0:T(8,128)(2,1)S(1)} %get-tuple-element.42), channel_id=1, source_target_pairs={{0,32},{16,48},{32,0},{48,16},{1,33},{17,49},{33,1},{49,17},{2,34}... | collective-permute-start | bytes 589832 | tf_op jit(solution)/shard_map/ppermute | solution.py:40
  131.6 2.7 %collective-permute-done.23 = bf16[2,4,64,384]{3,2,1,0:T(8,128)(2,1)S(1)} collective-permute-done((bf16[2,4,64,384]{3,2,1,0:T(8,128)(2,1)S(1)}, bf16[2,4,64,384]{3,2,1,0:T(8,128)(2,1)S(1)}, u32[]{:S(2)}, u32[]{:S(2)}) %collective-permute-start.23) | collective-permute-done | bytes 393248 | tf_op jit(solution)/shard_map/ppermute | solution.py:40
  135.0 2.5 %collective-permute-start.27 = (bf16[4,64,384]{2,1,0:T(8,128)(2,1)S(1)}, bf16[4,64,384]{2,1,0:T(8,128)(2,1)S(1)}, u32[]{:S(2)}, u32[]{:S(2)}) collective-permute-start(bf16[4,64,384]{2,1,0:T(8,128)(2,1)S(1)} %get-tuple-element.40), channel_id=1, source_target_pairs={{0,128},{64,192},{128,0},{192,64},{1,129},{65,193},{129,1},{193,65... | collective-permute-start | bytes 589832 | tf_op jit(solution)/shard_map/ppermute | solution.py:40
  138.7 1.3 collective-permute-start.28
  140.0 2.4 %collective-permute-done.19 = bf16[4,64,384]{2,1,0:T(8,128)(2,1)S(1)} collective-permute-done((bf16[4,64,384]{2,1,0:T(8,128)(2,1)S(1)}, bf16[4,64,384]{2,1,0:T(8,128)(2,1)S(1)}, u32[]{:S(2)}, u32[]{:S(2)}) %collective-permute-start.19) | collective-permute-done | bytes 196640 | tf_op jit(solution)/shard_map/ppermute | solution.py:40
  142.5 5.4 %collective-permute-start.21 = (bf16[4,32,384]{2,1,0:T(8,128)(2,1)S(1)}, bf16[4,32,384]{2,1,0:T(8,128)(2,1)S(1)}, u32[]{:S(2)}, u32[]{:S(2)}) collective-permute-start(bf16[4,32,384]{2,1,0:T(8,128)(2,1)S(1)} %select_convert_fusion.1), channel_id=1, source_target_pairs={{0,8},{8,0},{1,9},{9,1},{2,10},{10,2},{3,11},{11,3},{4,12},{12,4},... | collective-permute-start | bytes 294920 | tf_op jit(solution)/shard_map/ppermute | solution.py:29
  148.0 5.3 %collective-permute-start.29 = (bf16[4,32,384]{2,1,0:T(8,128)(2,1)S(1)}, bf16[4,32,384]{2,1,0:T(8,128)(2,1)S(1)}, u32[]{:S(2)}, u32[]{:S(2)}) collective-permute-start(bf16[4,32,384]{2,1,0:T(8,128)(2,1)S(1)} %select_convert_fusion), channel_id=1, source_target_pairs={{0,8},{8,0},{1,9},{9,1},{2,10},{10,2},{3,11},{11,3},{4,12},{12,4},... | collective-permute-start | bytes 294920 | tf_op jit(solution)/shard_map/ppermute | solution.py:29
  (91 shorter events, 19.6 us)
Async XLA Ops:
  7.2 65.5 %all-gather.2.cloned.1.call-start = ((), (), s32[]{:S(2)}) async-start(), calls=%async_computation.1 | async-start | bytes 9469952 | tf_op jit(solution)/shard_map/all_gather | solution.py:245
  9.9 143.4 %reduce-scatter.2.cloned.1.call-start = ((), (), s32[]{:S(2)}) async-start(), calls=%async_computation.2 | async-start | bytes 4718592 | tf_op jit(solution)/shard_map/reduce_scatter | solution.py:262
  10.2 4.4 %collective-permute-start = (bf16[2,4,32,384]{3,2,1,0:T(8,128)(2,1)S(1)}, bf16[2,4,32,384]{3,2,1,0:T(8,128)(2,1)S(1)}, u32[]{:S(2)}, u32[]{:S(2)}) collective-permute-start(bf16[2,4,32,384]{3,2,1,0:T(8,128)(2,1)S(1)} %pad_maximum_fusion.2), channel_id=1, source_target_pairs={{0,8},{8,0},{1,9},{9,1},{2,10},{10,2},{3,11},{11,3},{4,12},{12,4},... | collective-permute-start | bytes 589832 | tf_op jit(solution)/shard_map/ppermute | solution.py:29
  14.7 7.7 %collective-permute-start.2 = (bf16[4,64,384]{2,1,0:T(8,128)(2,1)S(1)}, bf16[4,64,384]{2,1,0:T(8,128)(2,1)S(1)}, u32[]{:S(2)}, u32[]{:S(2)}) collective-permute-start(bf16[4,64,384]{2,1,0:T(8,128)(2,1)S(1)} %get-tuple-element.53), channel_id=1, source_target_pairs={{0,32},{8,40},{16,48},{24,56},{32,0},{40,8},{48,16},{56,24},{1,33}... | collective-permute-start | bytes 589832 | tf_op jit(solution)/shard_map/ppermute | solution.py:35
  15.8 9.2 %collective-permute-start.1 = (bf16[4,64,384]{2,1,0:T(8,128)(2,1)S(1)}, bf16[4,64,384]{2,1,0:T(8,128)(2,1)S(1)}, u32[]{:S(2)}, u32[]{:S(2)}) collective-permute-start(bf16[4,64,384]{2,1,0:T(8,128)(2,1)S(1)} %get-tuple-element.53), channel_id=1, source_target_pairs={{0,16},{8,56},{16,32},{24,8},{32,48},{40,24},{48,0},{56,40},{1,17}... | collective-permute-start | bytes 589832 | tf_op jit(solution)/shard_map/ppermute | solution.py:35
  16.6 10.7 %collective-permute-start.3 = (bf16[4,64,384]{2,1,0:T(8,128)(2,1)S(1)}, bf16[4,64,384]{2,1,0:T(8,128)(2,1)S(1)}, u32[]{:S(2)}, u32[]{:S(2)}) collective-permute-start(bf16[4,64,384]{2,1,0:T(8,128)(2,1)S(1)} %get-tuple-element.53), channel_id=1, source_target_pairs={{0,48},{8,24},{16,0},{24,40},{32,16},{40,56},{48,32},{56,8},{1,49}... | collective-permute-start | bytes 589832 | tf_op jit(solution)/shard_map/ppermute | solution.py:35
  17.3 11.3 %collective-permute-start.8 = (bf16[4,64,384]{2,1,0:T(8,128)(2,1)S(1)}, bf16[4,64,384]{2,1,0:T(8,128)(2,1)S(1)}, u32[]{:S(2)}, u32[]{:S(2)}) collective-permute-start(bf16[4,64,384]{2,1,0:T(8,128)(2,1)S(1)} %get-tuple-element.49), channel_id=1, source_target_pairs={{0,128},{8,136},{64,192},{72,200},{128,0},{136,8},{192,64},{200,72... | collective-permute-start | bytes 589832 | tf_op jit(solution)/shard_map/ppermute | solution.py:35
  20.3 8.3 %collective-permute-start.7 = (bf16[4,64,384]{2,1,0:T(8,128)(2,1)S(1)}, bf16[4,64,384]{2,1,0:T(8,128)(2,1)S(1)}, u32[]{:S(2)}, u32[]{:S(2)}) collective-permute-start(bf16[4,64,384]{2,1,0:T(8,128)(2,1)S(1)} %get-tuple-element.49), channel_id=1, source_target_pairs={{0,64},{8,200},{64,128},{72,8},{128,192},{136,72},{192,0},{200,136... | collective-permute-start | bytes 589832 | tf_op jit(solution)/shard_map/ppermute | solution.py:35
  22.4 8.2 %collective-permute-start.9 = (bf16[4,64,384]{2,1,0:T(8,128)(2,1)S(1)}, bf16[4,64,384]{2,1,0:T(8,128)(2,1)S(1)}, u32[]{:S(2)}, u32[]{:S(2)}) collective-permute-start(bf16[4,64,384]{2,1,0:T(8,128)(2,1)S(1)} %get-tuple-element.49), channel_id=1, source_target_pairs={{0,192},{8,72},{64,0},{72,136},{128,64},{136,200},{192,128},{200,8... | collective-permute-start | bytes 589832 | tf_op jit(solution)/shard_map/ppermute | solution.py:35
  27.5 11.4 %collective-permute-start.4 = (bf16[4,4,64,384]{3,2,1,0:T(8,128)(2,1)S(1)}, bf16[4,4,64,384]{3,2,1,0:T(8,128)(2,1)S(1)}, u32[]{:S(2)}, u32[]{:S(2)}) collective-permute-start(bf16[4,4,64,384]{3,2,1,0:T(8,128)(2,1)S(1)} %pad_maximum_fusion.refs_2_), channel_id=1, source_target_pairs={{0,64},{8,200},{64,128},{72,8},{128,192},{136,72},{192,0},{200,136... | collective-permute-start | bytes 2359304 | tf_op jit(solution)/shard_map/ppermute | solution.py:35
  30.7 11.3 %collective-permute-start.10 = (bf16[4,4,64,384]{3,2,1,0:T(8,128)(2,1)S(1)}, bf16[4,4,64,384]{3,2,1,0:T(8,128)(2,1)S(1)}, u32[]{:S(2)}, u32[]{:S(2)}) collective-permute-start(bf16[4,4,64,384]{3,2,1,0:T(8,128)(2,1)S(1)} %pad_maximum_fusion.1.refs_6_), channel_id=1, source_target_pairs={{0,16},{8,56},{16,32},{24,8},{32,48},{40,24},{48,0},{56,40},{1,17}... | collective-permute-start | bytes 2359304 | tf_op jit(solution)/shard_map/ppermute | solution.py:35
  38.9 11.3 %collective-permute-start.5 = (bf16[4,4,64,384]{3,2,1,0:T(8,128)(2,1)S(1)}, bf16[4,4,64,384]{3,2,1,0:T(8,128)(2,1)S(1)}, u32[]{:S(2)}, u32[]{:S(2)}) collective-permute-start(bf16[4,4,64,384]{3,2,1,0:T(8,128)(2,1)S(1)} %collective-permute-done.4.refs_3_), channel_id=1, source_target_pairs={{0,64},{8,200},{64,128},{72,8},{128,192},{136,72},{192,0},{200,136... | collective-permute-start | bytes 2359304 | tf_op jit(solution)/shard_map/ppermute | solution.py:35
  42.0 11.8 %collective-permute-start.11 = (bf16[4,4,64,384]{3,2,1,0:T(8,128)(2,1)S(1)}, bf16[4,4,64,384]{3,2,1,0:T(8,128)(2,1)S(1)}, u32[]{:S(2)}, u32[]{:S(2)}) collective-permute-start(bf16[4,4,64,384]{3,2,1,0:T(8,128)(2,1)S(1)} %collective-permute-done.10.refs_7_), channel_id=1, source_target_pairs={{0,16},{8,56},{16,32},{24,8},{32,48},{40,24},{48,0},{56,40},{1,17}... | collective-permute-start | bytes 2359304 | tf_op jit(solution)/shard_map/ppermute | solution.py:35
  50.2 12.5 %collective-permute-start.6 = (bf16[4,4,64,384]{3,2,1,0:T(8,128)(2,1)S(1)}, bf16[4,4,64,384]{3,2,1,0:T(8,128)(2,1)}, u32[]{:S(2)}, u32[]{:S(2)}) collective-permute-start(bf16[4,4,64,384]{3,2,1,0:T(8,128)(2,1)S(1)} %collective-permute-done.5.refs_4_), channel_id=1, source_target_pairs={{0,64},{8,200},{64,128},{72,8},{128,192},{136,72},{192,0},{200,136... | collective-permute-start | bytes 2359304 | tf_op jit(solution)/shard_map/ppermute | solution.py:35
  53.8 12.5 %collective-permute-start.12 = (bf16[4,4,64,384]{3,2,1,0:T(8,128)(2,1)S(1)}, bf16[4,4,64,384]{3,2,1,0:T(8,128)(2,1)}, u32[]{:S(2)}, u32[]{:S(2)}) collective-permute-start(bf16[4,4,64,384]{3,2,1,0:T(8,128)(2,1)S(1)} %collective-permute-done.11.refs_8_), channel_id=1, source_target_pairs={{0,16},{8,56},{16,32},{24,8},{32,48},{40,24},{48,0},{56,40},{1,17}... | collective-permute-start | bytes 2359304 | tf_op jit(solution)/shard_map/ppermute | solution.py:35
  94.9 20.2 %collective-permute-start.14 = (bf16[4,4,64,384]{3,2,1,0:T(8,128)(2,1)S(1)}, bf16[4,4,64,384]{3,2,1,0:T(8,128)(2,1)S(1)}, u32[]{:S(2)}, u32[]{:S(2)}) collective-permute-start(bf16[4,4,64,384]{3,2,1,0:T(8,128)(2,1)S(1)} %copy-done.10), channel_id=1, source_target_pairs={{0,64},{64,128},{128,192},{192,0},{1,65},{65,129},{129,193},{193,1... | collective-permute-start | bytes 2359304 | tf_op jit(solution)/shard_map/ppermute | solution.py:40
  96.1 19.2 %collective-permute-start.16 = (bf16[4,4,64,384]{3,2,1,0:T(8,128)(2,1)S(1)}, bf16[4,4,64,384]{3,2,1,0:T(8,128)(2,1)S(1)}, u32[]{:S(2)}, u32[]{:S(2)}) collective-permute-start(bf16[4,4,64,384]{3,2,1,0:T(8,128)(2,1)S(1)} %copy-done.9), channel_id=1, source_target_pairs={{0,192},{64,0},{128,64},{192,128},{1,193},{65,1},{129,65},{193,129... | collective-permute-start | bytes 2359304 | tf_op jit(solution)/shard_map/ppermute | solution.py:40
  104.0 19.8 %collective-permute-start.22 = (bf16[4,4,64,384]{3,2,1,0:T(8,128)(2,1)}, bf16[4,4,64,384]{3,2,1,0:T(8,128)(2,1)S(1)}, u32[]{:S(2)}, u32[]{:S(2)}) collective-permute-start(bf16[4,4,64,384]{3,2,1,0:T(8,128)(2,1)} %get-tuple-element.26), channel_id=1, source_target_pairs={{0,16},{16,32},{32,48},{48,0},{1,17},{17,33},{33,49},{49,1},{2,18}... | collective-permute-start | bytes 2359304 | tf_op jit(solution)/shard_map/ppermute | solution.py:40
  105.2 18.8 %collective-permute-start.24 = (bf16[4,4,64,384]{3,2,1,0:T(8,128)(2,1)}, bf16[4,4,64,384]{3,2,1,0:T(8,128)(2,1)S(1)}, u32[]{:S(2)}, u32[]{:S(2)}) collective-permute-start(bf16[4,4,64,384]{3,2,1,0:T(8,128)(2,1)} %get-tuple-element.27), channel_id=1, source_target_pairs={{0,48},{16,0},{32,16},{48,32},{1,49},{17,1},{33,17},{49,33},{2,50}... | collective-permute-start | bytes 2359304 | tf_op jit(solution)/shard_map/ppermute | solution.py:40
  115.2 11.8 %collective-permute-start.15 = (bf16[2,4,64,384]{3,2,1,0:T(8,128)(2,1)S(1)}, bf16[2,4,64,384]{3,2,1,0:T(8,128)(2,1)S(1)}, u32[]{:S(2)}, u32[]{:S(2)}) collective-permute-start(bf16[2,4,64,384]{3,2,1,0:T(8,128)(2,1)S(1)} %add_convert_fusion.5), channel_id=1, source_target_pairs={{0,64},{64,128},{128,192},{192,0},{1,65},{65,129},{129,193},{193,1... | collective-permute-start | bytes 1179656 | tf_op jit(solution)/shard_map/ppermute | solution.py:40
  115.4 11.6 %collective-permute-start.18 = (bf16[2,4,64,384]{3,2,1,0:T(8,128)(2,1)S(1)}, bf16[2,4,64,384]{3,2,1,0:T(8,128)(2,1)S(1)}, u32[]{:S(2)}, u32[]{:S(2)}) collective-permute-start(bf16[2,4,64,384]{3,2,1,0:T(8,128)(2,1)S(1)} %add_convert_fusion.4), channel_id=1, source_target_pairs={{0,192},{64,0},{128,64},{192,128},{1,193},{65,1},{129,65},{193,129... | collective-permute-start | bytes 1179656 | tf_op jit(solution)/shard_map/ppermute | solution.py:40
  123.9 10.4 %collective-permute-start.23 = (bf16[2,4,64,384]{3,2,1,0:T(8,128)(2,1)S(1)}, bf16[2,4,64,384]{3,2,1,0:T(8,128)(2,1)S(1)}, u32[]{:S(2)}, u32[]{:S(2)}) collective-permute-start(bf16[2,4,64,384]{3,2,1,0:T(8,128)(2,1)S(1)} %add_convert_fusion.2), channel_id=1, source_target_pairs={{0,16},{16,32},{32,48},{48,0},{1,17},{17,33},{33,49},{49,1},{2,18}... | collective-permute-start | bytes 1179656 | tf_op jit(solution)/shard_map/ppermute | solution.py:40
  124.1 10.4 %collective-permute-start.26 = (bf16[2,4,64,384]{3,2,1,0:T(8,128)(2,1)S(1)}, bf16[2,4,64,384]{3,2,1,0:T(8,128)(2,1)S(1)}, u32[]{:S(2)}, u32[]{:S(2)}) collective-permute-start(bf16[2,4,64,384]{3,2,1,0:T(8,128)(2,1)S(1)} %add_convert_fusion.1), channel_id=1, source_target_pairs={{0,48},{16,0},{32,16},{48,32},{1,49},{17,1},{33,17},{49,33},{2,50}... | collective-permute-start | bytes 1179656 | tf_op jit(solution)/shard_map/ppermute | solution.py:40
  127.4 11.3 %collective-permute-start.17 = (bf16[4,64,384]{2,1,0:T(8,128)(2,1)S(1)}, bf16[4,64,384]{2,1,0:T(8,128)(2,1)S(1)}, u32[]{:S(2)}, u32[]{:S(2)}) collective-permute-start(bf16[4,64,384]{2,1,0:T(8,128)(2,1)S(1)} %fusion.12), channel_id=1, source_target_pairs={{0,16},{16,32},{32,48},{48,0},{1,17},{17,33},{33,49},{49,1},{2,18}... | collective-permute-start | bytes 589832 | tf_op jit(solution)/shard_map/ppermute | solution.py:40
  128.0 14.4 %collective-permute-start.19 = (bf16[4,64,384]{2,1,0:T(8,128)(2,1)S(1)}, bf16[4,64,384]{2,1,0:T(8,128)(2,1)S(1)}, u32[]{:S(2)}, u32[]{:S(2)}) collective-permute-start(bf16[4,64,384]{2,1,0:T(8,128)(2,1)S(1)} %get-tuple-element.42), channel_id=1, source_target_pairs={{0,32},{16,48},{32,0},{48,16},{1,33},{17,49},{33,1},{49,17},{2,34}... | collective-permute-start | bytes 589832 | tf_op jit(solution)/shard_map/ppermute | solution.py:40
  130.5 11.9 %collective-permute-start.20 = (bf16[4,64,384]{2,1,0:T(8,128)(2,1)S(1)}, bf16[4,64,384]{2,1,0:T(8,128)(2,1)S(1)}, u32[]{:S(2)}, u32[]{:S(2)}) collective-permute-start(bf16[4,64,384]{2,1,0:T(8,128)(2,1)S(1)} %get-tuple-element.43), channel_id=1, source_target_pairs={{0,48},{16,0},{32,16},{48,32},{1,49},{17,1},{33,17},{49,33},{2,50}... | collective-permute-start | bytes 589832 | tf_op jit(solution)/shard_map/ppermute | solution.py:40
  134.8 13.0 %collective-permute-start.25 = (bf16[4,64,384]{2,1,0:T(8,128)(2,1)S(1)}, bf16[4,64,384]{2,1,0:T(8,128)(2,1)S(1)}, u32[]{:S(2)}, u32[]{:S(2)}) collective-permute-start(bf16[4,64,384]{2,1,0:T(8,128)(2,1)S(1)} %fusion.13), channel_id=1, source_target_pairs={{0,64},{64,128},{128,192},{192,0},{1,65},{65,129},{129,193},{193,1... | collective-permute-start | bytes 589832 | tf_op jit(solution)/shard_map/ppermute | solution.py:40
  135.0 12.9 %collective-permute-start.27 = (bf16[4,64,384]{2,1,0:T(8,128)(2,1)S(1)}, bf16[4,64,384]{2,1,0:T(8,128)(2,1)S(1)}, u32[]{:S(2)}, u32[]{:S(2)}) collective-permute-start(bf16[4,64,384]{2,1,0:T(8,128)(2,1)S(1)} %get-tuple-element.40), channel_id=1, source_target_pairs={{0,128},{64,192},{128,0},{192,64},{1,129},{65,193},{129,1},{193,65... | collective-permute-start | bytes 589832 | tf_op jit(solution)/shard_map/ppermute | solution.py:40
  138.7 9.2 %collective-permute-start.28 = (bf16[4,64,384]{2,1,0:T(8,128)(2,1)S(1)}, bf16[4,64,384]{2,1,0:T(8,128)(2,1)S(1)}, u32[]{:S(2)}, u32[]{:S(2)}) collective-permute-start(bf16[4,64,384]{2,1,0:T(8,128)(2,1)S(1)} %get-tuple-element.41), channel_id=1, source_target_pairs={{0,192},{64,0},{128,64},{192,128},{1,193},{65,1},{129,65},{193,129... | collective-permute-start | bytes 589832 | tf_op jit(solution)/shard_map/ppermute | solution.py:40
  142.5 10.9 %collective-permute-start.21 = (bf16[4,32,384]{2,1,0:T(8,128)(2,1)S(1)}, bf16[4,32,384]{2,1,0:T(8,128)(2,1)S(1)}, u32[]{:S(2)}, u32[]{:S(2)}) collective-permute-start(bf16[4,32,384]{2,1,0:T(8,128)(2,1)S(1)} %select_convert_fusion.1), channel_id=1, source_target_pairs={{0,8},{8,0},{1,9},{9,1},{2,10},{10,2},{3,11},{11,3},{4,12},{12,4},... | collective-permute-start | bytes 294920 | tf_op jit(solution)/shard_map/ppermute | solution.py:29
  148.0 6.5 %collective-permute-start.29 = (bf16[4,32,384]{2,1,0:T(8,128)(2,1)S(1)}, bf16[4,32,384]{2,1,0:T(8,128)(2,1)S(1)}, u32[]{:S(2)}, u32[]{:S(2)}) collective-permute-start(bf16[4,32,384]{2,1,0:T(8,128)(2,1)S(1)} %select_convert_fusion), channel_id=1, source_target_pairs={{0,8},{8,0},{1,9},{9,1},{2,10},{10,2},{3,11},{11,3},{4,12},{12,4},... | collective-permute-start | bytes 294920 | tf_op jit(solution)/shard_map/ppermute | solution.py:29
  153.3 2.2 %collective-permute-start.13 = (bf16[2,128,1024]{2,1,0:T(8,128)(2,1)}, bf16[2,128,1024]{2,1,0:T(8,128)(2,1)S(1)}, u32[]{:S(2)}, u32[]{:S(2)}) collective-permute-start(bf16[2,128,1024]{2,1,0:T(8,128)(2,1)} %bitcast.97), channel_id=1, source_target_pairs={{0,8},{8,0},{1,9},{9,1},{2,10},{10,2},{3,11},{11,3},{4,12},{12,4},... | collective-permute-start | bytes 1572872 | tf_op jit(solution)/shard_map/ppermute | solution.py:29
  (11 other events, 137.3 us)
Sparse Core Ops, SparseCore 0:
  10.1 62.5 all-gather.1
  94.0 53.4 reduce-scatter.1

commit v6 on v4

--- a/solution.py
+++ b/solution.py
@@ -62,7 +62,7 @@
 def layer_kernel(scale, pos, rows, *refs):
     a_in, b_in = refs[0:4], refs[4:8]
     sums, a_out, b_out = refs[8], refs[9:14], refs[14:19]
-    wg, wd, term, xg, gg, weighting, slot_grad, srow, before, totals, sems = refs[19:]
+    wg, wd, term, xg, gg, weighting, slot_grad, kept, before, totals, sems = refs[19:]
     n = QROWS // ROWS
     out_copies = [
         pltpu.make_async_copy(totals.at[q], sums.at[pl.ds(q * n % NZ, n), q * n // NZ], sems.at[q]) for q in range(QUADS)
@@ -86,8 +86,8 @@
             member = jnp.where(hit, 1.0, member)
             gates = jnp.where(hit, meta[8 + k : 9 + k, :], gates)
         slot = jnp.where(member > 0.0, dot(member.astype(BF), before[...], (1, 0)), -1.0)
-        srow[step_id] = slot
         picks = pick_rows(slot)
+        kept[step_id] = picks
         at = pl.ds(pl.multiple_of(step_id * QSLOTS, QSLOTS), QSLOTS)
         for half, to in enumerate((xg, gg)):
             to[:, at, :] = (
@@ -109,7 +109,7 @@
         @pl.when(e == EXPERTS_CORE - 1)
         def _():
             for q in range(QUADS):
-                total = dot(pick_rows(srow[q]), slot_grad[q], (0, 0)).astype(BF)
+                total = dot(kept[q], slot_grad[q], (0, 0)).astype(BF)
                 totals[q] = total.reshape(n, ROWS, WIDTH)
                 out_copies[q].start()
 
@@ -172,7 +172,7 @@
             out_specs=[ANYWHERE] + [piece(n) for n in PARTS * 2],
             scratch_shapes=[pltpu.VMEM((WIDTH, HID), BF)] * 3
             + [slots(WIDTH, BF), slots(WIDTH, BF), slots(128, F32)]
-            + [pltpu.VMEM((QUADS, EXPERTS_CORE * QSLOTS, WIDTH), BF), pltpu.VMEM((QUADS, 8, QROWS), F32)]
+            + [pltpu.VMEM((QUADS, EXPERTS_CORE * QSLOTS, WIDTH), BF), pltpu.VMEM((QUADS, EXPERTS_CORE * QSLOTS, QROWS), BF)]
             + [pltpu.VMEM((QROWS, QROWS), BF), pltpu.VMEM((QUADS, QROWS // ROWS, ROWS, WIDTH), BF)]
             + [pltpu.SemaphoreType.DMA((QUADS,))],
         ),

time: 160 us -> 160 us (level)
  no operation moved by 1% of the time
where the time goes in v6:
time: 160 us
  waiting for transfers between devices  60.7 us (38%)
  starting transfers between devices  52 us (32%)
  Pallas kernels  22.8 us (14%)
  between operations  14.3 us (9%)
  other arithmetic  5.38 us (3%)
  local copies, waits for them, and re-layouts  4.55 us (3%)
    ppermute x12, waiting for transfers between devices, step(): return lax.ppermute(value, (axis, 'c'), pairs)  29.4 us
    pallas_call x1, Pallas kernels, layer(): pl.pallas_call(lambda *refs: layer_kernel(scale, *refs), grid_spec=pltpu....  22.8 us
    ppermute x14, waiting for transfers between devices, shift(): return lax.ppermute(value, axis, [(i, (i + by) % n) for i in range(n)])  22.6 us
    ppermute x12, starting transfers between devices, step(): return lax.ppermute(value, (axis, 'c'), pairs)  20.3 us
    ppermute x14, starting transfers between devices, shift(): return lax.ppermute(value, axis, [(i, (i + by) % n) for i in range(n)])  20.1 us
    ppermute x4, starting transfers between devices, swap(): return lax.ppermute(value, 'c', [(0, 1), (1, 0)])  11.4 us
    all_gather x1, waiting for transfers between devices, shards(): lax.all_gather(jnp.concatenate([tokens, out_grad, meta], axis=1), ('c', '...  5.57 us
    unnamed x26, local copies, waits for them, and re-layouts  3.82 us
  transfers between devices with their start and end apart: 32, of which 16 were waited for; matrix products, arithmetic and copies ran while one was open for 3% of the time, Pallas kernels for 0%

profile of v6, /device:TPU:1, one launch (start us, length us, event | category | flops | bytes accessed | tf_op | source)
XLA Modules:
  0.0 159.8 jit_solution(5365604039439117363)
XLA Ops:
  8.0 1.9 %fusion.3 = bf16[128,2176]{1,0:T(8,128)(2,1)} fusion(bf16[8,128]{1,0:T(8,128)(2,1)} %bitcast.104, bf16[8,128]{1,0:T(8,128)(2,1)S(1)} %convert_bitcast_fusion, bf16[128,1024]{1,0:T(8,128)(2,1)} %param.7, bf16[128,1024]{1,0:T(8,128)(2,1)} %param.6), kind=kLoop, calls=%fused_computation.14 | loop fusion | flops 3063808 | bytes 1085440 | tf_op jit(solution)/shard_map/concatenate | solution.py:213
  10.1 3.3 %collective-permute-start = (bf16[2,4,32,384]{3,2,1,0:T(8,128)(2,1)S(1)}, bf16[2,4,32,384]{3,2,1,0:T(8,128)(2,1)S(1)}, u32[]{:S(2)}, u32[]{:S(2)}) collective-permute-start(bf16[2,4,32,384]{3,2,1,0:T(8,128)(2,1)S(1)} %pad_maximum_fusion.2), channel_id=1, source_target_pairs={{0,8},{8,0},{1,9},{9,1},{2,10},{10,2},{3,11},{11,3},{4,12},{12,4},... | collective-permute-start | bytes 589832 | tf_op jit(solution)/shard_map/ppermute | solution.py:29
  17.2 3.0 %collective-permute-start.8 = (bf16[4,64,384]{2,1,0:T(8,128)(2,1)S(1)}, bf16[4,64,384]{2,1,0:T(8,128)(2,1)S(1)}, u32[]{:S(2)}, u32[]{:S(2)}) collective-permute-start(bf16[4,64,384]{2,1,0:T(8,128)(2,1)S(1)} %get-tuple-element.45), channel_id=1, source_target_pairs={{0,128},{8,136},{64,192},{72,200},{128,0},{136,8},{192,64},{200,72... | collective-permute-start | bytes 589832 | tf_op jit(solution)/shard_map/ppermute | solution.py:35
  21.0 1.4 collective-permute-done.2
  22.4 2.6 %collective-permute-done.1 = bf16[4,64,384]{2,1,0:T(8,128)(2,1)S(1)} collective-permute-done((bf16[4,64,384]{2,1,0:T(8,128)(2,1)S(1)}, bf16[4,64,384]{2,1,0:T(8,128)(2,1)S(1)}, u32[]{:S(2)}, u32[]{:S(2)}) %collective-permute-start.1) | collective-permute-done | bytes 196640 | tf_op jit(solution)/shard_map/ppermute | solution.py:35
  25.0 2.4 %collective-permute-done.3 = bf16[4,64,384]{2,1,0:T(8,128)(2,1)S(1)} collective-permute-done((bf16[4,64,384]{2,1,0:T(8,128)(2,1)S(1)}, bf16[4,64,384]{2,1,0:T(8,128)(2,1)S(1)}, u32[]{:S(2)}, u32[]{:S(2)}) %collective-permute-start.3) | collective-permute-done | bytes 196640 | tf_op jit(solution)/shard_map/ppermute | solution.py:35
  30.7 1.7 %collective-permute-start.10 = (bf16[4,4,64,384]{3,2,1,0:T(8,128)(2,1)S(1)}, bf16[4,4,64,384]{3,2,1,0:T(8,128)(2,1)S(1)}, u32[]{:S(2)}, u32[]{:S(2)}) collective-permute-start(bf16[4,4,64,384]{3,2,1,0:T(8,128)(2,1)S(1)} %pad_maximum_fusion.1.refs_6_), channel_id=1, source_target_pairs={{0,16},{8,56},{16,32},{24,8},{32,48},{40,24},{48,0},{56,40},{1,17}... | collective-permute-start | bytes 2359304 | tf_op jit(solution)/shard_map/ppermute | solution.py:35
  32.4 7.3 %collective-permute-done.4.refs_3_ = bf16[4,4,64,384]{3,2,1,0:T(8,128)(2,1)S(1)} collective-permute-done((bf16[4,4,64,384]{3,2,1,0:T(8,128)(2,1)S(1)}, bf16[4,4,64,384]{3,2,1,0:T(8,128)(2,1)S(1)}, u32[]{:S(2)}, u32[]{:S(2)}) %collective-permute-start.4) | collective-permute-done | bytes 786464 | tf_op jit(solution)/shard_map/ppermute | solution.py:35
  39.6 2.2 %collective-permute-start.5 = (bf16[4,4,64,384]{3,2,1,0:T(8,128)(2,1)S(1)}, bf16[4,4,64,384]{3,2,1,0:T(8,128)(2,1)S(1)}, u32[]{:S(2)}, u32[]{:S(2)}) collective-permute-start(bf16[4,4,64,384]{3,2,1,0:T(8,128)(2,1)S(1)} %collective-permute-done.4.refs_3_), channel_id=1, source_target_pairs={{0,64},{8,200},{64,128},{72,8},{128,192},{136,72},{192,0},{200,136... | collective-permute-start | bytes 2359304 | tf_op jit(solution)/shard_map/ppermute | solution.py:35
  42.0 2.8 %collective-permute-start.11 = (bf16[4,4,64,384]{3,2,1,0:T(8,128)(2,1)S(1)}, bf16[4,4,64,384]{3,2,1,0:T(8,128)(2,1)S(1)}, u32[]{:S(2)}, u32[]{:S(2)}) collective-permute-start(bf16[4,4,64,384]{3,2,1,0:T(8,128)(2,1)S(1)} %collective-permute-done.10.refs_7_), channel_id=1, source_target_pairs={{0,16},{8,56},{16,32},{24,8},{32,48},{40,24},{48,0},{56,40},{1,17}... | collective-permute-start | bytes 2359304 | tf_op jit(solution)/shard_map/ppermute | solution.py:35
  44.8 6.0 %collective-permute-done.5.refs_4_ = bf16[4,4,64,384]{3,2,1,0:T(8,128)(2,1)S(1)} collective-permute-done((bf16[4,4,64,384]{3,2,1,0:T(8,128)(2,1)S(1)}, bf16[4,4,64,384]{3,2,1,0:T(8,128)(2,1)S(1)}, u32[]{:S(2)}, u32[]{:S(2)}) %collective-permute-start.5) | collective-permute-done | bytes 786464 | tf_op jit(solution)/shard_map/ppermute | solution.py:35
  50.9 3.4 %collective-permute-start.6 = (bf16[4,4,64,384]{3,2,1,0:T(8,128)(2,1)S(1)}, bf16[4,4,64,384]{3,2,1,0:T(8,128)(2,1)S(1)}, u32[]{:S(2)}, u32[]{:S(2)}) collective-permute-start(bf16[4,4,64,384]{3,2,1,0:T(8,128)(2,1)S(1)} %collective-permute-done.5.refs_4_), channel_id=1, source_target_pairs={{0,64},{8,200},{64,128},{72,8},{128,192},{136,72},{192,0},{200,136... | collective-permute-start | bytes 2359304 | tf_op jit(solution)/shard_map/ppermute | solution.py:35
  54.2 3.0 %collective-permute-start.12 = (bf16[4,4,64,384]{3,2,1,0:T(8,128)(2,1)S(1)}, bf16[4,4,64,384]{3,2,1,0:T(8,128)(2,1)S(1)}, u32[]{:S(2)}, u32[]{:S(2)}) collective-permute-start(bf16[4,4,64,384]{3,2,1,0:T(8,128)(2,1)S(1)} %collective-permute-done.11.refs_8_), channel_id=1, source_target_pairs={{0,16},{8,56},{16,32},{24,8},{32,48},{40,24},{48,0},{56,40},{1,17}... | collective-permute-start | bytes 2359304 | tf_op jit(solution)/shard_map/ppermute | solution.py:35
  57.9 5.3 %collective-permute-done.6.refs_5_ = bf16[4,4,64,384]{3,2,1,0:T(8,128)(2,1)S(1)} collective-permute-done((bf16[4,4,64,384]{3,2,1,0:T(8,128)(2,1)S(1)}, bf16[4,4,64,384]{3,2,1,0:T(8,128)(2,1)S(1)}, u32[]{:S(2)}, u32[]{:S(2)}) %collective-permute-start.6) | collective-permute-done | bytes 786464 | tf_op jit(solution)/shard_map/ppermute | solution.py:35
  63.2 3.0 %collective-permute-done.12.refs_9_ = bf16[4,4,64,384]{3,2,1,0:T(8,128)(2,1)S(1)} collective-permute-done((bf16[4,4,64,384]{3,2,1,0:T(8,128)(2,1)S(1)}, bf16[4,4,64,384]{3,2,1,0:T(8,128)(2,1)S(1)}, u32[]{:S(2)}, u32[]{:S(2)}) %collective-permute-start.12) | collective-permute-done | bytes 786464 | tf_op jit(solution)/shard_map/ppermute | solution.py:35
  67.1 5.6 %all-gather.2.cloned.1.call-done.refs_1_ = bf16[2048,2176]{1,0:T(8,128)(2,1)} async-done(((bf16[128,2176]{1,0:T(8,128)(2,1)}), bf16[2048,2176]{1,0:T(8,128)(2,1)}) %all-gather.2.cloned.1.call-update) | async-done | bytes 8912912 | tf_op jit(solution)/shard_map/all_gather | solution.py:213
  72.7 22.8 %shard_map.85 = (bf16[8,2,128,1024]{3,2,1,0:T(8,128)(2,1)}, bf16[4,4,64,384]{3,2,1,0:T(8,128)(2,1)S(1)}, bf16[4,4,64,384]{3,2,1,0:T(8,128)(2,1)}, bf16[4,4,64,38...) custom-call(s32[5]{0:T(128)} %stack.62.refs_0_, ...), custom_call_target="tpu_custom_call" | custom-call | flops 12999999488 | bytes 26000000 | tf_op jit(solution)/shard_map/pallas_call | solution.py:165
  95.5 1.3 collective-permute-start.14
  96.8 1.5 collective-permute-start.16
  99.5 1.5 collective-permute-start.24
  101.0 15.1 %collective-permute-done.14 = bf16[4,4,64,384]{3,2,1,0:T(8,128)(2,1)S(1)} collective-permute-done((bf16[4,4,64,384]{3,2,1,0:T(8,128)(2,1)}, bf16[4,4,64,384]{3,2,1,0:T(8,128)(2,1)S(1)}, u32[]{:S(2)}, u32[]{:S(2)}) %collective-permute-start.14) | collective-permute-done | bytes 786464 | tf_op jit(solution)/shard_map/ppermute | solution.py:40
  116.3 2.7 %collective-permute-start.18 = (bf16[2,4,64,384]{3,2,1,0:T(8,128)(2,1)S(1)}, bf16[2,4,64,384]{3,2,1,0:T(8,128)(2,1)S(1)}, u32[]{:S(2)}, u32[]{:S(2)}) collective-permute-start(bf16[2,4,64,384]{3,2,1,0:T(8,128)(2,1)S(1)} %add_convert_fusion.4), channel_id=1, source_target_pairs={{0,192},{64,0},{128,64},{192,128},{1,193},{65,1},{129,65},{193,129... | collective-permute-start | bytes 1179656 | tf_op jit(solution)/shard_map/ppermute | solution.py:40
  119.2 1.2 collective-permute-start.23
  120.5 1.6 collective-permute-start.26
  122.1 5.1 %collective-permute-done.15 = bf16[2,4,64,384]{3,2,1,0:T(8,128)(2,1)S(1)} collective-permute-done((bf16[2,4,64,384]{3,2,1,0:T(8,128)(2,1)S(1)}, bf16[2,4,64,384]{3,2,1,0:T(8,128)(2,1)S(1)}, u32[]{:S(2)}, u32[]{:S(2)}) %collective-permute-start.15) | collective-permute-done | bytes 393248 | tf_op jit(solution)/shard_map/ppermute | solution.py:40
  127.6 1.4 collective-permute-start.17
  129.0 2.5 %collective-permute-start.19 = (bf16[4,64,384]{2,1,0:T(8,128)(2,1)S(1)}, bf16[4,64,384]{2,1,0:T(8,128)(2,1)S(1)}, u32[]{:S(2)}, u32[]{:S(2)}) collective-permute-start(bf16[4,64,384]{2,1,0:T(8,128)(2,1)S(1)} %get-tuple-element.38), channel_id=1, source_target_pairs={{0,32},{16,48},{32,0},{48,16},{1,33},{17,49},{33,1},{49,17},{2,34}... | collective-permute-start | bytes 589832 | tf_op jit(solution)/shard_map/ppermute | solution.py:40
  133.3 3.8 %collective-permute-start.27 = (bf16[4,64,384]{2,1,0:T(8,128)(2,1)S(1)}, bf16[4,64,384]{2,1,0:T(8,128)(2,1)S(1)}, u32[]{:S(2)}, u32[]{:S(2)}) collective-permute-start(bf16[4,64,384]{2,1,0:T(8,128)(2,1)S(1)} %get-tuple-element.36), channel_id=1, source_target_pairs={{0,128},{64,192},{128,0},{192,64},{1,129},{65,193},{129,1},{193,65... | collective-permute-start | bytes 589832 | tf_op jit(solution)/shard_map/ppermute | solution.py:40
  137.1 1.4 collective-permute-done.19
  138.6 3.3 %collective-permute-start.21 = (bf16[4,32,384]{2,1,0:T(8,128)(2,1)S(1)}, bf16[4,32,384]{2,1,0:T(8,128)(2,1)S(1)}, u32[]{:S(2)}, u32[]{:S(2)}) collective-permute-start(bf16[4,32,384]{2,1,0:T(8,128)(2,1)S(1)} %select_convert_fusion.1), channel_id=1, source_target_pairs={{0,8},{8,0},{1,9},{9,1},{2,10},{10,2},{3,11},{11,3},{4,12},{12,4},... | collective-permute-start | bytes 294920 | tf_op jit(solution)/shard_map/ppermute | solution.py:29
  143.1 4.2 %collective-permute-start.29 = (bf16[4,32,384]{2,1,0:T(8,128)(2,1)S(1)}, bf16[4,32,384]{2,1,0:T(8,128)(2,1)S(1)}, u32[]{:S(2)}, u32[]{:S(2)}) collective-permute-start(bf16[4,32,384]{2,1,0:T(8,128)(2,1)S(1)} %select_convert_fusion), channel_id=1, source_target_pairs={{0,8},{8,0},{1,9},{9,1},{2,10},{10,2},{3,11},{11,3},{4,12},{12,4},... | collective-permute-start | bytes 294920 | tf_op jit(solution)/shard_map/ppermute | solution.py:29
  147.3 2.0 %reduce-scatter.2.cloned.1.call-done = bf16[1,2,128,1024]{3,2,1,0:T(8,128)(2,1)} async-done(((bf16[8,2,128,1024]{3,2,1,0:T(8,128)(2,1)}), bf16[1,2,128,1024]{3,2,1,0:T(8,128)(2,1)}) %reduce-scatter.2.cloned.1.call-update) | async-done | bytes 524304 | tf_op jit(solution)/shard_map/reduce_scatter | solution.py:229
  (90 shorter events, 19.2 us)
Async XLA Ops:
  7.2 65.5 %all-gather.2.cloned.1.call-start = ((), (), s32[]{:S(2)}) async-start(), calls=%async_computation.1 | async-start | bytes 9469952 | tf_op jit(solution)/shard_map/all_gather | solution.py:213
  9.9 139.4 %reduce-scatter.2.cloned.1.call-start = ((), (), s32[]{:S(2)}) async-start(), calls=%async_computation.2 | async-start | bytes 4718592 | tf_op jit(solution)/shard_map/reduce_scatter | solution.py:229
  10.1 4.4 %collective-permute-start = (bf16[2,4,32,384]{3,2,1,0:T(8,128)(2,1)S(1)}, bf16[2,4,32,384]{3,2,1,0:T(8,128)(2,1)S(1)}, u32[]{:S(2)}, u32[]{:S(2)}) collective-permute-start(bf16[2,4,32,384]{3,2,1,0:T(8,128)(2,1)S(1)} %pad_maximum_fusion.2), channel_id=1, source_target_pairs={{0,8},{8,0},{1,9},{9,1},{2,10},{10,2},{3,11},{11,3},{4,12},{12,4},... | collective-permute-start | bytes 589832 | tf_op jit(solution)/shard_map/ppermute | solution.py:29
  14.6 7.7 %collective-permute-start.2 = (bf16[4,64,384]{2,1,0:T(8,128)(2,1)S(1)}, bf16[4,64,384]{2,1,0:T(8,128)(2,1)S(1)}, u32[]{:S(2)}, u32[]{:S(2)}) collective-permute-start(bf16[4,64,384]{2,1,0:T(8,128)(2,1)S(1)} %get-tuple-element.49), channel_id=1, source_target_pairs={{0,32},{8,40},{16,48},{24,56},{32,0},{40,8},{48,16},{56,24},{1,33}... | collective-permute-start | bytes 589832 | tf_op jit(solution)/shard_map/ppermute | solution.py:35
  15.7 9.2 %collective-permute-start.1 = (bf16[4,64,384]{2,1,0:T(8,128)(2,1)S(1)}, bf16[4,64,384]{2,1,0:T(8,128)(2,1)S(1)}, u32[]{:S(2)}, u32[]{:S(2)}) collective-permute-start(bf16[4,64,384]{2,1,0:T(8,128)(2,1)S(1)} %get-tuple-element.49), channel_id=1, source_target_pairs={{0,16},{8,56},{16,32},{24,8},{32,48},{40,24},{48,0},{56,40},{1,17}... | collective-permute-start | bytes 589832 | tf_op jit(solution)/shard_map/ppermute | solution.py:35
  16.6 10.7 %collective-permute-start.3 = (bf16[4,64,384]{2,1,0:T(8,128)(2,1)S(1)}, bf16[4,64,384]{2,1,0:T(8,128)(2,1)S(1)}, u32[]{:S(2)}, u32[]{:S(2)}) collective-permute-start(bf16[4,64,384]{2,1,0:T(8,128)(2,1)S(1)} %get-tuple-element.49), channel_id=1, source_target_pairs={{0,48},{8,24},{16,0},{24,40},{32,16},{40,56},{48,32},{56,8},{1,49}... | collective-permute-start | bytes 589832 | tf_op jit(solution)/shard_map/ppermute | solution.py:35
  17.2 12.1 %collective-permute-start.8 = (bf16[4,64,384]{2,1,0:T(8,128)(2,1)S(1)}, bf16[4,64,384]{2,1,0:T(8,128)(2,1)S(1)}, u32[]{:S(2)}, u32[]{:S(2)}) collective-permute-start(bf16[4,64,384]{2,1,0:T(8,128)(2,1)S(1)} %get-tuple-element.45), channel_id=1, source_target_pairs={{0,128},{8,136},{64,192},{72,200},{128,0},{136,8},{192,64},{200,72... | collective-permute-start | bytes 589832 | tf_op jit(solution)/shard_map/ppermute | solution.py:35
  20.2 9.1 %collective-permute-start.7 = (bf16[4,64,384]{2,1,0:T(8,128)(2,1)S(1)}, bf16[4,64,384]{2,1,0:T(8,128)(2,1)S(1)}, u32[]{:S(2)}, u32[]{:S(2)}) collective-permute-start(bf16[4,64,384]{2,1,0:T(8,128)(2,1)S(1)} %get-tuple-element.45), channel_id=1, source_target_pairs={{0,64},{8,200},{64,128},{72,8},{128,192},{136,72},{192,0},{200,136... | collective-permute-start | bytes 589832 | tf_op jit(solution)/shard_map/ppermute | solution.py:35
  22.4 8.2 %collective-permute-start.9 = (bf16[4,64,384]{2,1,0:T(8,128)(2,1)S(1)}, bf16[4,64,384]{2,1,0:T(8,128)(2,1)S(1)}, u32[]{:S(2)}, u32[]{:S(2)}) collective-permute-start(bf16[4,64,384]{2,1,0:T(8,128)(2,1)S(1)} %get-tuple-element.45), channel_id=1, source_target_pairs={{0,192},{8,72},{64,0},{72,136},{128,64},{136,200},{192,128},{200,8... | collective-permute-start | bytes 589832 | tf_op jit(solution)/shard_map/ppermute | solution.py:35
  28.4 11.2 %collective-permute-start.4 = (bf16[4,4,64,384]{3,2,1,0:T(8,128)(2,1)S(1)}, bf16[4,4,64,384]{3,2,1,0:T(8,128)(2,1)S(1)}, u32[]{:S(2)}, u32[]{:S(2)}) collective-permute-start(bf16[4,4,64,384]{3,2,1,0:T(8,128)(2,1)S(1)} %pad_maximum_fusion.refs_2_), channel_id=1, source_target_pairs={{0,64},{8,200},{64,128},{72,8},{128,192},{136,72},{192,0},{200,136... | collective-permute-start | bytes 2359304 | tf_op jit(solution)/shard_map/ppermute | solution.py:35
  30.7 11.3 %collective-permute-start.10 = (bf16[4,4,64,384]{3,2,1,0:T(8,128)(2,1)S(1)}, bf16[4,4,64,384]{3,2,1,0:T(8,128)(2,1)S(1)}, u32[]{:S(2)}, u32[]{:S(2)}) collective-permute-start(bf16[4,4,64,384]{3,2,1,0:T(8,128)(2,1)S(1)} %pad_maximum_fusion.1.refs_6_), channel_id=1, source_target_pairs={{0,16},{8,56},{16,32},{24,8},{32,48},{40,24},{48,0},{56,40},{1,17}... | collective-permute-start | bytes 2359304 | tf_op jit(solution)/shard_map/ppermute | solution.py:35
  39.6 11.2 %collective-permute-start.5 = (bf16[4,4,64,384]{3,2,1,0:T(8,128)(2,1)S(1)}, bf16[4,4,64,384]{3,2,1,0:T(8,128)(2,1)S(1)}, u32[]{:S(2)}, u32[]{:S(2)}) collective-permute-start(bf16[4,4,64,384]{3,2,1,0:T(8,128)(2,1)S(1)} %collective-permute-done.4.refs_3_), channel_id=1, source_target_pairs={{0,64},{8,200},{64,128},{72,8},{128,192},{136,72},{192,0},{200,136... | collective-permute-start | bytes 2359304 | tf_op jit(solution)/shard_map/ppermute | solution.py:35
  42.0 12.2 %collective-permute-start.11 = (bf16[4,4,64,384]{3,2,1,0:T(8,128)(2,1)S(1)}, bf16[4,4,64,384]{3,2,1,0:T(8,128)(2,1)S(1)}, u32[]{:S(2)}, u32[]{:S(2)}) collective-permute-start(bf16[4,4,64,384]{3,2,1,0:T(8,128)(2,1)S(1)} %collective-permute-done.10.refs_7_), channel_id=1, source_target_pairs={{0,16},{8,56},{16,32},{24,8},{32,48},{40,24},{48,0},{56,40},{1,17}... | collective-permute-start | bytes 2359304 | tf_op jit(solution)/shard_map/ppermute | solution.py:35
  50.9 12.3 %collective-permute-start.6 = (bf16[4,4,64,384]{3,2,1,0:T(8,128)(2,1)S(1)}, bf16[4,4,64,384]{3,2,1,0:T(8,128)(2,1)S(1)}, u32[]{:S(2)}, u32[]{:S(2)}) collective-permute-start(bf16[4,4,64,384]{3,2,1,0:T(8,128)(2,1)S(1)} %collective-permute-done.5.refs_4_), channel_id=1, source_target_pairs={{0,64},{8,200},{64,128},{72,8},{128,192},{136,72},{192,0},{200,136... | collective-permute-start | bytes 2359304 | tf_op jit(solution)/shard_map/ppermute | solution.py:35
  54.2 12.0 %collective-permute-start.12 = (bf16[4,4,64,384]{3,2,1,0:T(8,128)(2,1)S(1)}, bf16[4,4,64,384]{3,2,1,0:T(8,128)(2,1)S(1)}, u32[]{:S(2)}, u32[]{:S(2)}) collective-permute-start(bf16[4,4,64,384]{3,2,1,0:T(8,128)(2,1)S(1)} %collective-permute-done.11.refs_8_), channel_id=1, source_target_pairs={{0,16},{8,56},{16,32},{24,8},{32,48},{40,24},{48,0},{56,40},{1,17}... | collective-permute-start | bytes 2359304 | tf_op jit(solution)/shard_map/ppermute | solution.py:35
  95.5 20.5 %collective-permute-start.14 = (bf16[4,4,64,384]{3,2,1,0:T(8,128)(2,1)}, bf16[4,4,64,384]{3,2,1,0:T(8,128)(2,1)S(1)}, u32[]{:S(2)}, u32[]{:S(2)}) collective-permute-start(bf16[4,4,64,384]{3,2,1,0:T(8,128)(2,1)} %get-tuple-element.17), channel_id=1, source_target_pairs={{0,64},{64,128},{128,192},{192,0},{1,65},{65,129},{129,193},{193,1... | collective-permute-start | bytes 2359304 | tf_op jit(solution)/shard_map/ppermute | solution.py:40
  96.8 19.4 %collective-permute-start.16 = (bf16[4,4,64,384]{3,2,1,0:T(8,128)(2,1)}, bf16[4,4,64,384]{3,2,1,0:T(8,128)(2,1)S(1)}, u32[]{:S(2)}, u32[]{:S(2)}) collective-permute-start(bf16[4,4,64,384]{3,2,1,0:T(8,128)(2,1)} %get-tuple-element.18), channel_id=1, source_target_pairs={{0,192},{64,0},{128,64},{192,128},{1,193},{65,1},{129,65},{193,129... | collective-permute-start | bytes 2359304 | tf_op jit(solution)/shard_map/ppermute | solution.py:40
  98.3 20.8 %collective-permute-start.22 = (bf16[4,4,64,384]{3,2,1,0:T(8,128)(2,1)}, bf16[4,4,64,384]{3,2,1,0:T(8,128)(2,1)S(1)}, u32[]{:S(2)}, u32[]{:S(2)}) collective-permute-start(bf16[4,4,64,384]{3,2,1,0:T(8,128)(2,1)} %get-tuple-element.22), channel_id=1, source_target_pairs={{0,16},{16,32},{32,48},{48,0},{1,17},{17,33},{33,49},{49,1},{2,18}... | collective-permute-start | bytes 2359304 | tf_op jit(solution)/shard_map/ppermute | solution.py:40
  99.5 21.0 %collective-permute-start.24 = (bf16[4,4,64,384]{3,2,1,0:T(8,128)(2,1)}, bf16[4,4,64,384]{3,2,1,0:T(8,128)(2,1)S(1)}, u32[]{:S(2)}, u32[]{:S(2)}) collective-permute-start(bf16[4,4,64,384]{3,2,1,0:T(8,128)(2,1)} %get-tuple-element.23), channel_id=1, source_target_pairs={{0,48},{16,0},{32,16},{48,32},{1,49},{17,1},{33,17},{49,33},{2,50}... | collective-permute-start | bytes 2359304 | tf_op jit(solution)/shard_map/ppermute | solution.py:40
  116.1 11.1 %collective-permute-start.15 = (bf16[2,4,64,384]{3,2,1,0:T(8,128)(2,1)S(1)}, bf16[2,4,64,384]{3,2,1,0:T(8,128)(2,1)S(1)}, u32[]{:S(2)}, u32[]{:S(2)}) collective-permute-start(bf16[2,4,64,384]{3,2,1,0:T(8,128)(2,1)S(1)} %add_convert_fusion.5), channel_id=1, source_target_pairs={{0,64},{64,128},{128,192},{192,0},{1,65},{65,129},{129,193},{193,1... | collective-permute-start | bytes 1179656 | tf_op jit(solution)/shard_map/ppermute | solution.py:40
  116.3 10.8 %collective-permute-start.18 = (bf16[2,4,64,384]{3,2,1,0:T(8,128)(2,1)S(1)}, bf16[2,4,64,384]{3,2,1,0:T(8,128)(2,1)S(1)}, u32[]{:S(2)}, u32[]{:S(2)}) collective-permute-start(bf16[2,4,64,384]{3,2,1,0:T(8,128)(2,1)S(1)} %add_convert_fusion.4), channel_id=1, source_target_pairs={{0,192},{64,0},{128,64},{192,128},{1,193},{65,1},{129,65},{193,129... | collective-permute-start | bytes 1179656 | tf_op jit(solution)/shard_map/ppermute | solution.py:40
  119.2 13.6 %collective-permute-start.23 = (bf16[2,4,64,384]{3,2,1,0:T(8,128)(2,1)S(1)}, bf16[2,4,64,384]{3,2,1,0:T(8,128)(2,1)S(1)}, u32[]{:S(2)}, u32[]{:S(2)}) collective-permute-start(bf16[2,4,64,384]{3,2,1,0:T(8,128)(2,1)S(1)} %add_convert_fusion.2), channel_id=1, source_target_pairs={{0,16},{16,32},{32,48},{48,0},{1,17},{17,33},{33,49},{49,1},{2,18}... | collective-permute-start | bytes 1179656 | tf_op jit(solution)/shard_map/ppermute | solution.py:40
  120.5 12.2 %collective-permute-start.26 = (bf16[2,4,64,384]{3,2,1,0:T(8,128)(2,1)S(1)}, bf16[2,4,64,384]{3,2,1,0:T(8,128)(2,1)S(1)}, u32[]{:S(2)}, u32[]{:S(2)}) collective-permute-start(bf16[2,4,64,384]{3,2,1,0:T(8,128)(2,1)S(1)} %add_convert_fusion.1), channel_id=1, source_target_pairs={{0,48},{16,0},{32,16},{48,32},{1,49},{17,1},{33,17},{49,33},{2,50}... | collective-permute-start | bytes 1179656 | tf_op jit(solution)/shard_map/ppermute | solution.py:40
  127.6 9.6 %collective-permute-start.17 = (bf16[4,64,384]{2,1,0:T(8,128)(2,1)S(1)}, bf16[4,64,384]{2,1,0:T(8,128)(2,1)S(1)}, u32[]{:S(2)}, u32[]{:S(2)}) collective-permute-start(bf16[4,64,384]{2,1,0:T(8,128)(2,1)S(1)} %fusion.12), channel_id=1, source_target_pairs={{0,16},{16,32},{32,48},{48,0},{1,17},{17,33},{33,49},{49,1},{2,18}... | collective-permute-start | bytes 589832 | tf_op jit(solution)/shard_map/ppermute | solution.py:40
  129.0 9.5 %collective-permute-start.19 = (bf16[4,64,384]{2,1,0:T(8,128)(2,1)S(1)}, bf16[4,64,384]{2,1,0:T(8,128)(2,1)S(1)}, u32[]{:S(2)}, u32[]{:S(2)}) collective-permute-start(bf16[4,64,384]{2,1,0:T(8,128)(2,1)S(1)} %get-tuple-element.38), channel_id=1, source_target_pairs={{0,32},{16,48},{32,0},{48,16},{1,33},{17,49},{33,1},{49,17},{2,34}... | collective-permute-start | bytes 589832 | tf_op jit(solution)/shard_map/ppermute | solution.py:40
  131.6 6.9 %collective-permute-start.20 = (bf16[4,64,384]{2,1,0:T(8,128)(2,1)S(1)}, bf16[4,64,384]{2,1,0:T(8,128)(2,1)S(1)}, u32[]{:S(2)}, u32[]{:S(2)}) collective-permute-start(bf16[4,64,384]{2,1,0:T(8,128)(2,1)S(1)} %get-tuple-element.39), channel_id=1, source_target_pairs={{0,48},{16,0},{32,16},{48,32},{1,49},{17,1},{33,17},{49,33},{2,50}... | collective-permute-start | bytes 589832 | tf_op jit(solution)/shard_map/ppermute | solution.py:40
  133.1 8.8 %collective-permute-start.25 = (bf16[4,64,384]{2,1,0:T(8,128)(2,1)S(1)}, bf16[4,64,384]{2,1,0:T(8,128)(2,1)S(1)}, u32[]{:S(2)}, u32[]{:S(2)}) collective-permute-start(bf16[4,64,384]{2,1,0:T(8,128)(2,1)S(1)} %fusion.13), channel_id=1, source_target_pairs={{0,64},{64,128},{128,192},{192,0},{1,65},{65,129},{129,193},{193,1... | collective-permute-start | bytes 589832 | tf_op jit(solution)/shard_map/ppermute | solution.py:40
  133.3 9.7 %collective-permute-start.27 = (bf16[4,64,384]{2,1,0:T(8,128)(2,1)S(1)}, bf16[4,64,384]{2,1,0:T(8,128)(2,1)S(1)}, u32[]{:S(2)}, u32[]{:S(2)}) collective-permute-start(bf16[4,64,384]{2,1,0:T(8,128)(2,1)S(1)} %get-tuple-element.36), channel_id=1, source_target_pairs={{0,128},{64,192},{128,0},{192,64},{1,129},{65,193},{129,1},{193,65... | collective-permute-start | bytes 589832 | tf_op jit(solution)/shard_map/ppermute | solution.py:40
  137.1 5.9 %collective-permute-start.28 = (bf16[4,64,384]{2,1,0:T(8,128)(2,1)S(1)}, bf16[4,64,384]{2,1,0:T(8,128)(2,1)S(1)}, u32[]{:S(2)}, u32[]{:S(2)}) collective-permute-start(bf16[4,64,384]{2,1,0:T(8,128)(2,1)S(1)} %get-tuple-element.37), channel_id=1, source_target_pairs={{0,192},{64,0},{128,64},{192,128},{1,193},{65,1},{129,65},{193,129... | collective-permute-start | bytes 589832 | tf_op jit(solution)/shard_map/ppermute | solution.py:40
  138.6 11.3 %collective-permute-start.21 = (bf16[4,32,384]{2,1,0:T(8,128)(2,1)S(1)}, bf16[4,32,384]{2,1,0:T(8,128)(2,1)S(1)}, u32[]{:S(2)}, u32[]{:S(2)}) collective-permute-start(bf16[4,32,384]{2,1,0:T(8,128)(2,1)S(1)} %select_convert_fusion.1), channel_id=1, source_target_pairs={{0,8},{8,0},{1,9},{9,1},{2,10},{10,2},{3,11},{11,3},{4,12},{12,4},... | collective-permute-start | bytes 294920 | tf_op jit(solution)/shard_map/ppermute | solution.py:29
  143.1 7.8 %collective-permute-start.29 = (bf16[4,32,384]{2,1,0:T(8,128)(2,1)S(1)}, bf16[4,32,384]{2,1,0:T(8,128)(2,1)S(1)}, u32[]{:S(2)}, u32[]{:S(2)}) collective-permute-start(bf16[4,32,384]{2,1,0:T(8,128)(2,1)S(1)} %select_convert_fusion), channel_id=1, source_target_pairs={{0,8},{8,0},{1,9},{9,1},{2,10},{10,2},{3,11},{11,3},{4,12},{12,4},... | collective-permute-start | bytes 294920 | tf_op jit(solution)/shard_map/ppermute | solution.py:29
  149.3 2.8 %collective-permute-start.13 = (bf16[2,128,1024]{2,1,0:T(8,128)(2,1)}, bf16[2,128,1024]{2,1,0:T(8,128)(2,1)S(1)}, u32[]{:S(2)}, u32[]{:S(2)}) collective-permute-start(bf16[2,128,1024]{2,1,0:T(8,128)(2,1)} %bitcast.97), channel_id=1, source_target_pairs={{0,8},{8,0},{1,9},{9,1},{2,10},{10,2},{3,11},{11,3},{4,12},{12,4},... | collective-permute-start | bytes 1572872 | tf_op jit(solution)/shard_map/ppermute | solution.py:29
  (11 other events, 59.1 us)
Sparse Core Ops, SparseCore 0:
  10.0 62.5 all-gather.1
  95.7 53.5 reduce-scatter.1
